TPU v7x, 32 devices: a whole 2x2x4 slice. The times are simulated.
32 devices in a mesh: groups: 2 (over y), hx: 16 (over z, x, core).
Axes of the slice: x: 2, y: 2, z: 4, core: 2. Of those that a mesh axis runs over, the one named last changes fastest.
Arguments:
- tokens: bfloat16 [32, 8192], P(('groups', 'hx')), parts along dimension 0, may hold values from -6 to 6
- gate_codes: bfloat16 [8192, 26624], P(None, 'hx'), may hold values from -8 to 7, as said below
- gate_scales: float32 [64, 26624], P(None, 'hx'), may hold values from 0.00077339803 to 0.00773398
- up_codes: bfloat16 [8192, 26624], P(None, 'hx'), may hold values from -8 to 7, as said below
- up_scales: float32 [64, 26624], P(None, 'hx'), may hold values from 0.00077339803 to 0.00773398
- down_codes: bfloat16 [26624, 8192], P('hx'), may hold values from -8 to 7, as said below
- down_scales: float32 [8192], replicated, may hold values from 0.00061286293 to 0.006128629
- hadamard: int32 [52, 52], replicated, may hold values from -1 to 1, as said below
Outputs:
- mixed: bfloat16 [32, 8192], P(('groups', 'hx')), parts along dimension 0
There are 2 independent parts, one for each index of `groups`. A program takes and returns all parts, laid end to end along the dimension named above; an argument that names none is the same for every part. Nothing has to cross between parts.
Inputs may be any that keep to these rules, and one draw needn't show every extreme that they name: `gate_codes`: whole numbers. `up_codes`: whole numbers. `down_codes`: whole numbers. `hadamard`: a Hadamard matrix: every entry is -1 or 1 and any two rows are orthogonal.
All inputs are finite; a program needn't handle non-finite values.
Results may differ from a plain program's by a relative error of at most 0.015.
Values may be sent and summed in bfloat16 or wider, within the bound.
No kernel may reach another device: no remote copies, remote signals or barrier semaphores. Data moves between devices by JAX's collectives and lax.ppermute only.
A program may use at most 192 MiB of HBM per device.

v0:
```python
import math

import jax
import jax.numpy as jnp
from jax import lax
from jax.sharding import PartitionSpec as P

HA = 512
HB = 52
FF = 26624


def sylvester(size):
    index_vec = jnp.arange(size, dtype=jnp.int32)
    parity = jnp.zeros((size, size), jnp.int32)
    for level in range(max(size.bit_length() - 1, 0)):
        left_bits = jnp.right_shift(index_vec[:, None], level) & 1
        right_bits = jnp.right_shift(index_vec[None, :], level) & 1
        parity = parity + left_bits * right_bits
    return (1 - 2 * (parity % 2)).astype(jnp.float32)


def dequantize(codes, scales):
    row_total, col_total = codes.shape
    group_total = scales.shape[0]
    grouped = codes.astype(jnp.float32).reshape(group_total, row_total // group_total, col_total)
    return (grouped * scales[:, None, :]).reshape(row_total, col_total).astype(jnp.bfloat16)


def per_device(
    tokens, gate_codes, gate_scales, up_codes, up_scales, down_codes, down_scales, hadamard
):
    gate_weight = dequantize(gate_codes, gate_scales)
    up_weight = dequantize(up_codes, up_scales)
    tile_rows = lax.all_gather(tokens, "hx", axis=0, tiled=True)
    gate = jnp.dot(tile_rows, gate_weight, preferred_element_type=jnp.float32)
    up_part = jnp.dot(tile_rows, up_weight, preferred_element_type=jnp.float32)
    hidden = jax.nn.silu(gate) * up_part
    factor = hadamard.astype(jnp.float32)
    gathered = lax.all_to_all(
        hidden.astype(jnp.bfloat16), "hx", split_axis=0, concat_axis=1, tiled=True
    ).astype(hidden.dtype)
    row_count = gathered.shape[0]
    cube = gathered.reshape(row_count, HA, HB)
    cube = jnp.einsum("tab,ac->tcb", cube, sylvester(HA), precision=lax.Precision.HIGHEST)
    cube = jnp.einsum("tcb,bd->tcd", cube, factor, precision=lax.Precision.HIGHEST)
    turned = lax.all_to_all(
        cube.reshape(row_count, FF).astype(jnp.bfloat16),
        "hx",
        split_axis=1,
        concat_axis=0,
        tiled=True,
    ).astype(jnp.float32)
    rotated = (turned * (1.0 / math.sqrt(FF))).astype(jnp.bfloat16)
    summed = lax.psum_scatter(
        jnp.dot(rotated, down_codes, preferred_element_type=jnp.float32),
        "hx",
        scatter_dimension=0,
        tiled=True,
    )
    mixed = (summed * down_scales[None, :]).astype(jnp.bfloat16)
    return mixed


def solution(mesh):
    in_specs = (
        P(("groups", "hx"), None),
        P(None, "hx"),
        P(None, "hx"),
        P(None, "hx"),
        P(None, "hx"),
        P("hx", None),
        P(),
        P(),
    )
    out_specs = P(("groups", "hx"), None)
    return jax.shard_map(
        per_device, mesh=mesh, in_specs=in_specs, out_specs=out_specs, check_vma=False
    )
```

profile of v0, /device:TPU:0, one launch (start us, length us, event | category | flops | bytes accessed | tf_op | source)
XLA Modules:
  0.0 227.3 jit_solution(11263058405985309339)
XLA Ops:
  6.5 24.8 %all-gather = bf16[16,1,8192]{2,1,0:T(2,128)(2,1)S(1)} all-gather(bf16[1,1,8192]{2,1,0:T(2,128)(2,1)} %bitcast.40), channel_id=1, replica_groups=mesh['groups'=2,'hx'=16] {'hx'}, dimensions={0}, use_global_device_ids=true | all-gather | bytes 278528 | tf_op jit(solution)/shard_map/all_gather | solution.py:35
  31.3 19.3 %fusion.1 = bf16[8192,1664]{1,0:T(8,128)(2,1)} fusion(bf16[8192,1664]{1,0:T(8,128)(2,1)} %param.9, f32[64,1664]{1,0:T(8,128)} %param.10), kind=kLoop, calls=%fused_computation.3 | loop fusion | flops 40894464 | bytes 54951936 | tf_op jit(solution)/shard_map/convert_element_type | solution.py:27
  50.7 0.0 copy-start
  50.7 10.7 %convolution_bitcast_fusion.1 = f32[16,1664]{1,0:T(8,128)S(1)} fusion(bf16[8192,1664]{1,0:T(8,128)(2,1)} %fusion.1, bf16[16,1,8192]{2,1,0:T(2,128)(2,1)S(1)} %all-gather), kind=kOutput, calls=%fused_computation.6 | convolution fusion | flops 436207616 | bytes 27631616 | tf_op jit(solution)/shard_map/dot_general | solution.py:36
  61.4 0.0 copy-done
  61.4 19.2 %fusion = bf16[8192,1664]{1,0:T(8,128)(2,1)} fusion(bf16[8192,1664]{1,0:T(8,128)(2,1)} %param.11, f32[64,1664]{1,0:T(8,128)S(1)} %copy-done), kind=kLoop, calls=%fused_computation.1 | loop fusion | flops 40894464 | bytes 54951936 | tf_op jit(solution)/shard_map/convert_element_type | solution.py:27
  80.6 0.0 copy-start.2
  80.6 10.7 %fusion.4 = bf16[16,1,1664]{2,0,1:T(8,128)(2,1)S(1)} fusion(bf16[8192,1664]{1,0:T(8,128)(2,1)} %fusion, f32[16,1664]{1,0:T(8,128)S(1)} %convolution_bitcast_fusion.1, bf16[16,1,8192]{2,1,0:T(2,128)(2,1)S(1)} %all-gather), kind=kOutput, calls=%fused_computation.8 | convolution fusion | flops 436367360 | bytes 27684864 | tf_op jit(solution)/shard_map/dot_general | solution.py:37
  91.4 0.0 copy-start.3
  91.4 0.0 copy-start.1
  91.4 0.5 broadcast.214
  91.9 0.7 reduce.1
  92.6 0.7 reshape.182
  93.3 3.5 %all-to-all-start = ((bf16[16,2,832]{2,1,0:T(2,128)(2,1)}), bf16[16,2,832]{2,1,0:T(2,128)(2,1)S(1)}, u32[]{:S(2)}, u32[]{:S(2)}) async-start(bf16[16,2,832]{2,1,0:T(2,128)(2,1)} %reshape.182), calls=%async_computation | async-start | bytes 114688 | tf_op jit(solution)/shard_map/all_to_all | solution.py:40
  96.8 0.0 all-reduce.3.cloned.1.call-start
  96.9 6.7 %all-to-all-done = bf16[16,2,832]{2,1,0:T(2,128)(2,1)S(1)} async-done(((bf16[16,2,832]{2,1,0:T(2,128)(2,1)}), bf16[16,2,832]{2,1,0:T(2,128)(2,1)S(1)}, u32[]{:S(2)}, u32[]{:S(2)}) %all-to-all-start) | async-done | bytes 53280 | tf_op jit(solution)/shard_map/all_to_all | solution.py:40
  103.6 0.1 reshape.183
  103.7 0.3 reduce
  104.0 0.4 reshape.177
  104.4 1.7 fusion.9
  106.1 0.0 copy-done.2
  106.2 0.3 convolution_convert_fusion
  106.5 0.1 copy.14
  106.6 0.2 convert_element_type.63
  106.8 0.9 reduce.2
  107.8 0.1 reshape.184
  107.9 9.4 %all_to_all.23 = bf16[16,2,832]{2,1,0:T(2,128)(2,1)S(1)} all-to-all(bf16[16,2,832]{2,1,0:T(2,128)(2,1)S(1)} %reshape.184), channel_id=1, replica_groups=mesh['groups'=2,'hx'=16] {'hx'}, dimensions={0} | all-to-all | bytes 106496 | tf_op jit(solution)/shard_map/all_to_all | solution.py:47
  117.3 0.1 reshape.185
  117.4 13.2 %fusion.40 = f32[16,8192]{1,0:T(8,128)} fusion(bf16[1664,8192]{1,0:T(8,128)(2,1)} %param.13, bf16[1,16,1664]{2,0,1:T(2,128)(2,1)S(1)} %bitcast.39), kind=kOutput, calls=%fused_computation.48 | convolution fusion | flops 436287488 | bytes 27840512 | tf_op jit(solution)/shard_map/dot_general | solution.py:56
  130.6 0.0 all-reduce.3.cloned.1.call-update
  130.7 0.0 copy-done.3
  130.7 0.6 dynamic-slice
  131.3 86.9 %all-reduce.3.cloned.1.call-done = f32[16,8192]{1,0:T(8,128)} async-done(((f32[16,8192]{1,0:T(8,128)}), f32[16,8192]{1,0:T(8,128)}) %all-reduce.3.cloned.1.call-update) | async-done | bytes 524304
  218.2 0.0 copy-done.1
  218.2 2.2 fusion.44
  (5 shorter events, 0.0 us)
Async XLA Ops:
  50.7 10.8 %copy-start = (f32[64,1664]{1,0:T(8,128)S(1)}, f32[64,1664]{1,0:T(8,128)}, u32[]{:S(2)}) copy-start(f32[64,1664]{1,0:T(8,128)} %param.12) | copy-start | bytes 1277956
  80.6 25.5 %copy-start.2 = (s32[52,52]{1,0:T(8,128)S(1)}, s32[52,52]{1,0:T(8,128)}, u32[]{:S(2)}) copy-start(s32[52,52]{1,0:T(8,128)} %param.15) | copy-start | bytes 32452
  91.4 39.3 %copy-start.3 = (u32[32]{0:T(128)S(1)}, u32[32]{0:T(128)}, u32[]{:S(2)}) copy-start(u32[32]{0:T(128)} %constant.24) | copy-start | bytes 388
  91.4 126.8 %copy-start.1 = (f32[8192]{0:T(1024)S(1)}, f32[8192]{0:T(1024)}, u32[]{:S(2)}) copy-start(f32[8192]{0:T(1024)} %param.14) | copy-start | bytes 98308
  93.3 10.3 %all-to-all-start = ((bf16[16,2,832]{2,1,0:T(2,128)(2,1)}), bf16[16,2,832]{2,1,0:T(2,128)(2,1)S(1)}, u32[]{:S(2)}, u32[]{:S(2)}) async-start(bf16[16,2,832]{2,1,0:T(2,128)(2,1)} %reshape.182), calls=%async_computation | async-start | bytes 114688 | tf_op jit(solution)/shard_map/all_to_all | solution.py:40
  96.8 121.4 %all-reduce.3.cloned.1.call-start = ((), (), s32[]{:S(2)}) async-start(), calls=%async_computation.2 | async-start | bytes 1048576
Sparse Core Ops, SparseCore 0:
  130.8 87.3 all-reduce.2
where the time goes:
time: 228 us; the launch traced here: 227 us
  waiting for transfers between devices  93.6 us (41%)
  other arithmetic  42.7 us (19%)
  matrix products  36.7 us (16%)
  blocking collectives  34.2 us (15%)
  between operations  13.6 us (6%)
  starting transfers between devices  3.52 us (2%)
  local copies, waits for them, and re-layouts  3.02 us (1%)
    unnamed x2, waiting for transfers between devices  86.9 us
    convert_element_type x2, other arithmetic, dequantize(): (grouped * scales[:, None, :]).reshape(row_total, col_total)  38.5 us
    all_gather x1, blocking collectives, per_device(): tile_rows = lax.all_gather(tokens, 'hx', axis=0, tiled=True)  24.8 us
    dot_general x1, matrix products, per_device(): jnp.dot(rotated, down_codes, preferred_element_type=jnp.float32)  13.2 us
    dot_general x1, matrix products, per_device(): gate = jnp.dot(tile_rows, gate_weight, preferred_element_type=jnp.float32)  10.7 us
    dot_general x1, matrix products, per_device(): up_part = jnp.dot(tile_rows, up_weight, preferred_element_type=jnp.float32)  10.7 us
    all_to_all x1, blocking collectives, per_device(): lax.all_to_all(cube.reshape(row_count, FF).astype(jnp.bfloat16), 'hx', sp...  9.4 us
    all_to_all x1, waiting for transfers between devices, per_device(): lax.all_to_all(hidden.astype(jnp.bfloat16), 'hx', split_axis=0, concat_ax...  6.69 us
  transfers between devices with their start and end apart: 2, of which 2 were waited for; matrix products, arithmetic and copies ran while one was open for 0% of the time, Pallas kernels for 0%

commit v1 on v0

v1 whole, which is shorter than its diff:
```python
import functools
import math

import jax
import jax.numpy as jnp
from jax import lax
from jax.experimental import pallas as pl
from jax.experimental.pallas import tpu as pltpu
from jax.sharding import PartitionSpec as P

F8 = jnp.float8_e4m3fn
MIB = 2**20
CHUNK = 512
SLOTS = 4


def row_stream(source, buffers, sems, rows):
    total = source.shape[0] // rows
    depth = buffers.shape[0]

    def copy(step):
        slot = lax.rem(step, depth)
        first = pl.multiple_of(step * rows, rows)
        return pltpu.make_async_copy(source.at[pl.ds(first, rows), :], buffers.at[slot], sems.at[slot])

    return total, depth, copy


def pack_kernel(codes_ref, hadamard_ref, packed_ref, turn_ref, buffers, sems):
    total, depth, copy = row_stream(codes_ref, buffers, sems, buffers.shape[1])
    rows = buffers.shape[1]
    for step in range(min(depth, total)):
        copy(step).start()

    size = turn_ref.shape[0]
    small = hadamard_ref.shape[0]
    high = size // small
    unit = lax.broadcasted_iota(jnp.int32, (size, small), 0)
    part = lax.broadcasted_iota(jnp.int32, (size, small), 1)
    pick = (unit % small == part).astype(jnp.bfloat16)
    spread = jnp.dot(pick, hadamard_ref[...].astype(jnp.bfloat16), preferred_element_type=jnp.float32)
    unit_a = lax.broadcasted_iota(jnp.int32, (size, high), 0) // small
    part_a = lax.broadcasted_iota(jnp.int32, (size, high), 1)
    pick_a = (unit_a == part_a).astype(jnp.bfloat16)
    both = unit_a & part_a
    parity = jnp.zeros_like(both)
    for level in range(max(high.bit_length() - 1, 0)):
        parity = parity ^ (jnp.right_shift(both, level) & 1)
    spread_a = (1 - 2 * parity).astype(jnp.bfloat16)
    spread = spread.astype(jnp.bfloat16)
    cols = (((1,), (1,)), ((), ()))
    for first in range(0, size, 128):
        last = min(first + 128, size)
        low = lax.dot_general(spread[first:last], pick, cols, preferred_element_type=jnp.float32)
        top = lax.dot_general(spread_a[first:last], pick_a, cols, preferred_element_type=jnp.float32)
        turn_ref[first:last, :] = (low * top).astype(turn_ref.dtype)

    def body(step, carry):
        slot = lax.rem(step, depth)
        copy(step).wait()
        first = pl.multiple_of(step * rows, rows)
        packed_ref[pl.ds(first, rows), :] = buffers[slot].astype(packed_ref.dtype)

        @pl.when(step + depth < total)
        def _():
            copy(step + depth).start()

        return carry

    lax.fori_loop(0, total, body, 0)


def hidden_kernel(
    group, tokens_ref, gate_ref, gate_scales_ref, up_ref, up_scales_ref, turn_ref, out_ref, buffers, gate_sum, up_sum, sems
):
    total, depth, copy = row_stream(up_ref, buffers, sems, buffers.shape[1])
    rows = buffers.shape[1]
    count = tokens_ref.shape[0]
    for step in range(min(depth, total)):
        copy(step).start()
    gate_sum[...] = jnp.zeros_like(gate_sum)
    up_sum[...] = jnp.zeros_like(up_sum)
    low_half = lax.broadcasted_iota(jnp.int32, (count, 2 * group), 1) < group

    def body(step, carry):
        slot = lax.rem(step, depth)
        copy(step).wait()
        for pair in range(rows // (2 * group)):
            index = step * (rows // (2 * group)) + pair
            first = pl.multiple_of(index * 2 * group, 2 * group)
            two = tokens_ref[:, pl.ds(first, 2 * group)]
            none = jnp.zeros_like(two)
            stacked = jnp.concatenate([jnp.where(low_half, two, none), jnp.where(low_half, none, two)], axis=0)
            gate = jnp.dot(stacked, gate_ref[pl.ds(first, 2 * group), :], preferred_element_type=jnp.float32)
            here = buffers[slot, pair * 2 * group : (pair + 1) * 2 * group, :]
            up = jnp.dot(stacked, here, preferred_element_type=jnp.float32)
            gate_sum[...] += (
                gate[:count] * gate_scales_ref[pl.ds(2 * index, 1), :]
                + gate[count:] * gate_scales_ref[pl.ds(2 * index + 1, 1), :]
            )
            up_sum[...] += (
                up[:count] * up_scales_ref[pl.ds(2 * index, 1), :]
                + up[count:] * up_scales_ref[pl.ds(2 * index + 1, 1), :]
            )

        @pl.when(step + depth < total)
        def _():
            copy(step + depth).start()

        return carry

    lax.fori_loop(0, total, body, 0, unroll=4)
    gate = gate_sum[...]
    hidden = gate / (1.0 + jnp.exp(-gate)) * up_sum[...]
    coarse = hidden.astype(jnp.bfloat16)
    fine = (hidden - coarse.astype(jnp.float32)).astype(jnp.bfloat16)
    both = jnp.dot(jnp.concatenate([coarse, fine], axis=0), turn_ref[...], preferred_element_type=jnp.float32)
    out_ref[...] = both[:count] + both[count:]


def down_kernel(scale, width, turned_ref, codes_ref, out_ref):
    rotated = (turned_ref[...] * scale).astype(jnp.bfloat16)
    for first in range(0, codes_ref.shape[1], width):
        span = slice(first, first + width)
        out_ref[:, span] = jnp.dot(rotated, codes_ref[:, span], preferred_element_type=jnp.float32).astype(out_ref.dtype)


VMEM = pl.BlockSpec(memory_space=pltpu.VMEM)
ANY = pl.BlockSpec(memory_space=pl.ANY)


def in_vmem(value):
    return pltpu.with_memory_space_constraint(value, pltpu.VMEM)


def per_device(
    devices, tokens, gate_codes, gate_scales, up_codes, up_scales, down_codes, down_scales, hadamard
):
    width, units = gate_codes.shape
    group = width // gate_scales.shape[0]
    small = hadamard.shape[0]
    own = tokens.shape[0]
    count = own * devices
    lanes = 128
    total_units = units * devices
    me = lax.axis_index("hx")

    copies = jnp.broadcast_to(tokens.reshape(1, own, width // lanes, lanes), (devices, own, width // lanes, lanes))
    rows = lax.all_to_all(copies, "hx", split_axis=0, concat_axis=0, tiled=True).reshape(count, width)

    gate_packed, turn = pl.pallas_call(
        pack_kernel,
        out_shape=(pltpu.VMEM((width, units), F8), pltpu.VMEM((units, units), F8)),
        in_specs=[ANY, VMEM],
        out_specs=(VMEM, VMEM),
        scratch_shapes=[pltpu.VMEM((SLOTS, CHUNK, units), jnp.bfloat16), pltpu.SemaphoreType.DMA((SLOTS,))],
        compiler_params=pltpu.CompilerParams(vmem_limit_bytes=14 * MIB),
        cost_estimate=pl.CostEstimate(flops=0, bytes_accessed=2 * width * units, transcendentals=0),
    )(gate_codes, hadamard)

    turned = pl.pallas_call(
        functools.partial(hidden_kernel, group),
        out_shape=jax.ShapeDtypeStruct((count, units), jnp.float32),
        in_specs=[VMEM, VMEM, VMEM, ANY, VMEM, VMEM],
        out_specs=VMEM,
        scratch_shapes=[
            pltpu.VMEM((SLOTS, CHUNK, units), jnp.bfloat16),
            pltpu.VMEM((count, units), jnp.float32),
            pltpu.VMEM((count, units), jnp.float32),
            pltpu.SemaphoreType.DMA((SLOTS,)),
        ],
        compiler_params=pltpu.CompilerParams(vmem_limit_bytes=16 * MIB),
        cost_estimate=pl.CostEstimate(flops=4 * count * width * units, bytes_accessed=2 * width * units, transcendentals=0),
    )(rows, in_vmem(gate_packed), gate_scales, up_codes, up_scales, in_vmem(turn))

    bit = 1
    while bit < devices:
        other = lax.ppermute(turned.astype(jnp.bfloat16), "hx", [(at, at ^ bit) for at in range(devices)])
        sign = jnp.where((me & bit) == 0, 1.0, -1.0).astype(jnp.float32)
        turned = turned * sign + other.astype(jnp.float32)
        bit *= 2

    shares = pl.pallas_call(
        functools.partial(down_kernel, 1.0 / math.sqrt(total_units), 1024),
        out_shape=jax.ShapeDtypeStruct((count, width), jnp.bfloat16),
        in_specs=[VMEM, VMEM],
        out_specs=VMEM,
        compiler_params=pltpu.CompilerParams(vmem_limit_bytes=16 * MIB),
        cost_estimate=pl.CostEstimate(flops=2 * count * width * units, bytes_accessed=2 * width * units, transcendentals=0),
    )(turned, in_vmem(down_codes))

    shares = shares.reshape(devices, own, width // lanes, lanes)
    shares = lax.all_to_all(shares, "hx", split_axis=0, concat_axis=0, tiled=True)
    summed = jnp.sum(shares.astype(jnp.float32), axis=0).reshape(own, width)
    return (summed * down_scales[None, :]).astype(jnp.bfloat16)


def solution(mesh):
    in_specs = (
        P(("groups", "hx"), None),
        P(None, "hx"),
        P(None, "hx"),
        P(None, "hx"),
        P(None, "hx"),
        P("hx", None),
        P(),
        P(),
    )
    out_specs = P(("groups", "hx"), None)
    body = functools.partial(per_device, mesh.shape["hx"])
    return jax.shard_map(body, mesh=mesh, in_specs=in_specs, out_specs=out_specs, check_vma=False)
```

time: 228 us -> 88.3 us (0.39)
  waiting for transfers between devices: 93.6 us -> 7.68 us
  other arithmetic: 42.7 us -> 1.06 us
  matrix products: 36.7 us -> 0 us
  Pallas kernels: 0 us -> 25.2 us
  local copies, waits for them, and re-layouts: 3.02 us -> 22.8 us
  blocking collectives: 34.2 us -> 16.4 us
  between operations: 13.6 us -> 0.12 us
  starting transfers between devices: 3.52 us -> 14.5 us
    unnamed x2 -> x0, waiting for transfers between devices: 86.9 us -> none
    convert_element_type x3 -> x5, other arithmetic: 40.8 us -> 0.09 us  [the longest x4 0.08 us: per_device(): turned.astype(jnp.bfloat16)]
    dot_general x5 -> x0, matrix products: 36.7 us -> none  [the longest x1 13.2 us: per_device(): jnp.dot(rotated, down_codes, preferred_element_type=jnp.float32)]
    pallas_call x0 -> x3, Pallas kernels: none -> 25.2 us  [the longest x1 11.3 us: per_device(): pl.pallas_call(pack_kernel, out_shape=(pltpu.VMEM((width, units), F8), pl...]
    all_gather x1 -> x0, blocking collectives: 24.8 us -> none  [per_device(): tile_rows = lax.all_gather(tokens, 'hx', axis=0, tiled=True)]
    unnamed x13 -> x16, local copies, waits for them, and re-layouts: 1.74 us -> 21.4 us
    ppermute x0 -> x4, waiting for transfers between devices: none -> 7.68 us  [per_device(): lax.ppermute(turned.astype(jnp.bfloat16), 'hx', [(at, at ^ bit) for at in...]
    ppermute x0 -> x4, starting transfers between devices: none -> 7.13 us  [per_device(): lax.ppermute(turned.astype(jnp.bfloat16), 'hx', [(at, at ^ bit) for at in...]
  transfers between devices with their start and end apart: 2 -> 5, of which waited for: 2 -> 4; matrix products, arithmetic and copies ran while one was open for 0% -> 0% of each run, Pallas kernels for 0% -> 13%
where the time goes in v1:
time: 88.3 us; the launch traced here: 87.8 us
  Pallas kernels  25.2 us (29%)
  local copies, waits for them, and re-layouts  22.8 us (26%)
  blocking collectives  16.4 us (19%)
  starting transfers between devices  14.5 us (16%)
  waiting for transfers between devices  7.68 us (9%)
  other arithmetic  1.06 us (1%)
    unnamed x16, local copies, waits for them, and re-layouts  21.4 us
    all_to_all x1, blocking collectives, per_device(): lax.all_to_all(shares, 'hx', split_axis=0, concat_axis=0, tiled=True)  16.4 us
    pallas_call x1, Pallas kernels, per_device(): pl.pallas_call(pack_kernel, out_shape=(pltpu.VMEM((width, units), F8), pl...  11.3 us
    pallas_call x1, Pallas kernels, per_device(): pl.pallas_call(functools.partial(hidden_kernel, group), out_shape=jax.Sha...  10.3 us
    ppermute x4, waiting for transfers between devices, per_device(): lax.ppermute(turned.astype(jnp.bfloat16), 'hx', [(at, at ^ bit) for at in...  7.68 us
    all_to_all x1, starting transfers between devices, per_device(): lax.all_to_all(copies, 'hx', split_axis=0, concat_axis=0, tiled=True)  7.41 us
    ppermute x4, starting transfers between devices, per_device(): lax.ppermute(turned.astype(jnp.bfloat16), 'hx', [(at, at ^ bit) for at in...  7.13 us
    pallas_call x1, Pallas kernels, per_device(): pl.pallas_call(functools.partial(down_kernel, 1.0 / math.sqrt(total_units...  3.63 us
  transfers between devices with their start and end apart: 5, of which 4 were waited for; matrix products, arithmetic and copies ran while one was open for 0% of the time, Pallas kernels for 13%

profile of v1, /device:TPU:0, one launch (start us, length us, event | category | flops | bytes accessed | tf_op | source)
XLA Modules:
  0.0 87.8 jit_solution(16144130083083316480)
XLA Ops:
  0.0 0.0 copy-start.3
  0.0 0.9 %reduce.1 = bf16[8192]{0:T(1024)(128)(2,1)S(1)} reduce(bf16[1,8192]{1,0:T(2,128)(2,1)} %param.8, bf16[]{:T(256)} %constant.21), dimensions={0}, to_apply=%param.8.reduce_sub_computation | reduce | bytes 32770 | tf_op args[0]
  0.9 0.8 broadcast_in_dim.9
  1.7 7.4 %all-to-all-start = ((bf16[16,1,64,128]{3,2,1,0:T(8,128)(2,1)}), bf16[16,1,64,128]{3,2,1,0:T(8,128)(2,1)}, u32[]{:S(2)}, u32[]{:S(2)}) async-start(bf16[16,1,64,128]{3,2,1,0:T(8,128)(2,1)} %broadcast_in_dim.9), calls=%async_computation | async-start | bytes 524288 | tf_op jit(solution)/shard_map/all_to_all | solution.py:149
  9.1 0.0 copy-start.5
  9.1 0.7 copy-done.5
  9.8 11.3 %shard_map.82 = (f8e4m3fn[8192,1664]{1,0:T(32,128)(4,1)S(1)}, f8e4m3fn[1664,1664]{1,0:T(32,128)(4,1)S(1)}) custom-call(bf16[8192,1664]{1,0:T(8,128)(2,1)} %codes_ref.2, s32[52,52]{1,0:T(8,128)S(1)} %copy-done.5), custom_call_target="tpu_custom_call" | custom-call | bytes 27262976 | tf_op jit(solution)/shard_map/pallas_call | solution.py:151
  21.1 0.0 copy-start.1
  21.2 4.9 %copy-done.1 = f8e4m3fn[8192,1664]{1,0:T(32,128)(4,1)} copy-done((f8e4m3fn[8192,1664]{1,0:T(32,128)(4,1)}, f8e4m3fn[8192,1664]{1,0:T(32,128)(4,1)S(1)}, u32[]{:S(2)}) %copy-start.1) | copy-done | bytes 13631512
  26.0 0.0 all-to-all-done
  26.0 1.1 %copy.13 = bf16[2,8,64,128]{3,1,2,0:T(8,128)(2,1)S(1)} copy(bf16[2,8,64,128]{3,2,1,0:T(8,128)(2,1)} %bitcast.4) | data formatting | bytes 524288
  27.2 0.0 copy-done.3
  27.2 0.0 copy-start.2
  27.2 4.9 %copy-done.2 = f8e4m3fn[8192,1664]{1,0:T(32,128)(4,1)S(1)} copy-done((f8e4m3fn[8192,1664]{1,0:T(32,128)(4,1)S(1)}, f8e4m3fn[8192,1664]{1,0:T(32,128)(4,1)}, u32[]{:S(2)}) %copy-start.2) | copy-done | bytes 13631512
  32.1 0.0 copy-start.4
  32.1 1.0 %copy-done.4 = f32[64,1664]{1,0:T(8,128)S(1)} copy-done((f32[64,1664]{1,0:T(8,128)S(1)}, f32[64,1664]{1,0:T(8,128)}, u32[]{:S(2)}) %copy-start.4) | copy-done | bytes 426008
  33.1 0.0 copy-start.6
  33.1 10.3 %shard_map.83 = f32[16,1664]{1,0:T(8,128)S(1)} custom-call(bf16[16,8192]{1,0:T(8,128)(2,1)S(1)} %bitcast.16, f8e4m3fn[8192,1664]{1,0:T(32,128)(4,1)S(1)} %copy-done.2, f32[64,1664]{1,0:T(8,128)S(1)} %copy-done.3, bf16[8192,1664]{1,0:T(8,128)(2,1)} %up_ref.1, f32[64,1664]{1,0:T(8,128)S(1)} %copy-done.4, f8e4m3fn[1664,1664]{1,0:T(32,128)(4,1)S(1)} %get-tuple-element.8.turn_ref), custom_call_target="tpu_custom_call" | custom-call | flops 872415232 | bytes 27262976 | tf_op jit(solution)/shard_map/pallas_call | solution.py:161
  43.4 0.4 collective-permute-start
  43.8 0.9 %collective-permute-done = bf16[16,1664]{1,0:T(8,128)(2,1)S(1)} collective-permute-done((bf16[16,1664]{1,0:T(8,128)(2,1)S(1)}, bf16[16,1664]{1,0:T(8,128)(2,1)S(1)}, u32[]{:S(2)}, u32[]{:S(2)}) %collective-permute-start) | collective-permute-done | bytes 53280 | tf_op jit(solution)/shard_map/ppermute | solution.py:178
  44.7 1.9 %collective-permute-start.1 = (bf16[16,1664]{1,0:T(8,128)(2,1)S(1)}, bf16[16,1664]{1,0:T(8,128)(2,1)S(1)}, u32[]{:S(2)}, u32[]{:S(2)}) collective-permute-start(bf16[16,1664]{1,0:T(8,128)(2,1)S(1)} %fusion), channel_id=1, source_target_pairs={{0,2},{1,3},{2,0},{3,1},{4,6},{5,7},{6,4},{7,5},{8,10},{9,11},{10,... | collective-permute-start | bytes 159752 | tf_op jit(solution)/shard_map/ppermute | solution.py:178
  46.7 2.3 %collective-permute-done.1 = bf16[16,1664]{1,0:T(8,128)(2,1)S(1)} collective-permute-done((bf16[16,1664]{1,0:T(8,128)(2,1)S(1)}, bf16[16,1664]{1,0:T(8,128)(2,1)S(1)}, u32[]{:S(2)}, u32[]{:S(2)}) %collective-permute-start.1) | collective-permute-done | bytes 53280 | tf_op jit(solution)/shard_map/ppermute | solution.py:178
  49.0 1.9 %collective-permute-start.2 = (bf16[16,1664]{1,0:T(8,128)(2,1)S(1)}, bf16[16,1664]{1,0:T(8,128)(2,1)S(1)}, u32[]{:S(2)}, u32[]{:S(2)}) collective-permute-start(bf16[16,1664]{1,0:T(8,128)(2,1)S(1)} %get-tuple-element.9), channel_id=1, source_target_pairs={{0,4},{1,5},{2,6},{3,7},{4,0},{5,1},{6,2},{7,3},{8,12},{9,13},{10,... | collective-permute-start | bytes 159752 | tf_op jit(solution)/shard_map/ppermute | solution.py:178
  50.9 2.3 %collective-permute-done.2 = bf16[16,1664]{1,0:T(8,128)(2,1)S(1)} collective-permute-done((bf16[16,1664]{1,0:T(8,128)(2,1)S(1)}, bf16[16,1664]{1,0:T(8,128)(2,1)S(1)}, u32[]{:S(2)}, u32[]{:S(2)}) %collective-permute-start.2) | collective-permute-done | bytes 53280 | tf_op jit(solution)/shard_map/ppermute | solution.py:178
  53.2 2.8 %collective-permute-start.3 = (bf16[16,1664]{1,0:T(8,128)(2,1)S(1)}, bf16[16,1664]{1,0:T(8,128)(2,1)S(1)}, u32[]{:S(2)}, u32[]{:S(2)}) collective-permute-start(bf16[16,1664]{1,0:T(8,128)(2,1)S(1)} %fusion.1), channel_id=1, source_target_pairs={{0,8},{1,9},{2,10},{3,11},{4,12},{5,13},{6,14},{7,15},{8,0},{9,1},... | collective-permute-start | bytes 159752 | tf_op jit(solution)/shard_map/ppermute | solution.py:178
  56.0 2.3 %collective-permute-done.3 = bf16[16,1664]{1,0:T(8,128)(2,1)S(1)} collective-permute-done((bf16[16,1664]{1,0:T(8,128)(2,1)S(1)}, bf16[16,1664]{1,0:T(8,128)(2,1)S(1)}, u32[]{:S(2)}, u32[]{:S(2)}) %collective-permute-start.3) | collective-permute-done | bytes 53280 | tf_op jit(solution)/shard_map/ppermute | solution.py:178
  58.3 0.0 copy-start
  58.3 8.7 %copy-done = bf16[1664,8192]{1,0:T(8,128)(2,1)S(1)} copy-done((bf16[1664,8192]{1,0:T(8,128)(2,1)S(1)}, bf16[1664,8192]{1,0:T(8,128)(2,1)}, u32[]{:S(2)}) %copy-start) | copy-done | bytes 27263000
  67.1 3.6 %shard_map.84 = bf16[16,8192]{1,0:T(8,128)(2,1)S(1)} custom-call(f32[16,1664]{1,0:T(8,128)S(1)} %convert_add_fusion.turned_ref, bf16[1664,8192]{1,0:T(8,128)(2,1)S(1)} %copy-done), custom_call_target="tpu_custom_call" | custom-call | flops 436207616 | bytes 27262976 | tf_op jit(solution)/shard_map/pallas_call | solution.py:183
  70.7 0.1 copy.11
  70.8 16.4 %all_to_all.10 = bf16[16,1,64,128]{3,2,1,0:T(8,128)(2,1)S(1)} all-to-all(bf16[16,1,64,128]{3,2,1,0:T(8,128)(2,1)S(1)} %bitcast.18), channel_id=1, replica_groups=mesh['groups'=2,'hx'=16] {'hx'}, dimensions={0} | all-to-all | bytes 524288 | tf_op jit(solution)/shard_map/all_to_all | solution.py:193
  87.2 0.0 copy-done.6
  87.2 0.6 convert_element_type.43
  (7 shorter events, 0.2 us)
Async XLA Ops:
  0.0 27.2 %copy-start.3 = (f32[64,1664]{1,0:T(8,128)S(1)}, f32[64,1664]{1,0:T(8,128)}, u32[]{:S(2)}) copy-start(f32[64,1664]{1,0:T(8,128)} %gate_scales_ref.1) | copy-start | bytes 1277956
  1.7 24.4 %all-to-all-start = ((bf16[16,1,64,128]{3,2,1,0:T(8,128)(2,1)}), bf16[16,1,64,128]{3,2,1,0:T(8,128)(2,1)}, u32[]{:S(2)}, u32[]{:S(2)}) async-start(bf16[16,1,64,128]{3,2,1,0:T(8,128)(2,1)} %broadcast_in_dim.9), calls=%async_computation | async-start | bytes 524288 | tf_op jit(solution)/shard_map/all_to_all | solution.py:149
  9.1 0.8 copy-start.5
  21.1 4.9 %copy-start.1 = (f8e4m3fn[8192,1664]{1,0:T(32,128)(4,1)}, f8e4m3fn[8192,1664]{1,0:T(32,128)(4,1)S(1)}, u32[]{:S(2)}) copy-start(f8e4m3fn[8192,1664]{1,0:T(32,128)(4,1)S(1)} %get-tuple-element.7.gate_ref) | copy-start | bytes 40894468
  27.2 4.9 %copy-start.2 = (f8e4m3fn[8192,1664]{1,0:T(32,128)(4,1)S(1)}, f8e4m3fn[8192,1664]{1,0:T(32,128)(4,1)}, u32[]{:S(2)}) copy-start(f8e4m3fn[8192,1664]{1,0:T(32,128)(4,1)} %copy-done.1) | copy-start | bytes 40894468
  32.1 1.0 %copy-start.4 = (f32[64,1664]{1,0:T(8,128)S(1)}, f32[64,1664]{1,0:T(8,128)}, u32[]{:S(2)}) copy-start(f32[64,1664]{1,0:T(8,128)} %up_scales_ref.1) | copy-start | bytes 1277956
  33.1 54.1 %copy-start.6 = (f32[8192]{0:T(1024)S(1)}, f32[8192]{0:T(1024)}, u32[]{:S(2)}) copy-start(f32[8192]{0:T(1024)} %param.14) | copy-start | bytes 98308
  43.4 1.3 %collective-permute-start = (bf16[16,1664]{1,0:T(8,128)(2,1)S(1)}, bf16[16,1664]{1,0:T(8,128)(2,1)S(1)}, u32[]{:S(2)}, u32[]{:S(2)}) collective-permute-start(bf16[16,1664]{1,0:T(8,128)(2,1)S(1)} %convert_element_type.33), channel_id=1, source_target_pairs={{0,1},{1,0},{2,3},{3,2},{4,5},{5,4},{6,7},{7,6},{8,9},{9,8},{10,11... | collective-permute-start | bytes 159752 | tf_op jit(solution)/shard_map/ppermute | solution.py:178
  44.7 4.2 %collective-permute-start.1 = (bf16[16,1664]{1,0:T(8,128)(2,1)S(1)}, bf16[16,1664]{1,0:T(8,128)(2,1)S(1)}, u32[]{:S(2)}, u32[]{:S(2)}) collective-permute-start(bf16[16,1664]{1,0:T(8,128)(2,1)S(1)} %fusion), channel_id=1, source_target_pairs={{0,2},{1,3},{2,0},{3,1},{4,6},{5,7},{6,4},{7,5},{8,10},{9,11},{10,... | collective-permute-start | bytes 159752 | tf_op jit(solution)/shard_map/ppermute | solution.py:178
  49.0 4.2 %collective-permute-start.2 = (bf16[16,1664]{1,0:T(8,128)(2,1)S(1)}, bf16[16,1664]{1,0:T(8,128)(2,1)S(1)}, u32[]{:S(2)}, u32[]{:S(2)}) collective-permute-start(bf16[16,1664]{1,0:T(8,128)(2,1)S(1)} %get-tuple-element.9), channel_id=1, source_target_pairs={{0,4},{1,5},{2,6},{3,7},{4,0},{5,1},{6,2},{7,3},{8,12},{9,13},{10,... | collective-permute-start | bytes 159752 | tf_op jit(solution)/shard_map/ppermute | solution.py:178
  53.2 5.1 %collective-permute-start.3 = (bf16[16,1664]{1,0:T(8,128)(2,1)S(1)}, bf16[16,1664]{1,0:T(8,128)(2,1)S(1)}, u32[]{:S(2)}, u32[]{:S(2)}) collective-permute-start(bf16[16,1664]{1,0:T(8,128)(2,1)S(1)} %fusion.1), channel_id=1, source_target_pairs={{0,8},{1,9},{2,10},{3,11},{4,12},{5,13},{6,14},{7,15},{8,0},{9,1},... | collective-permute-start | bytes 159752 | tf_op jit(solution)/shard_map/ppermute | solution.py:178
  58.3 8.8 %copy-start = (bf16[1664,8192]{1,0:T(8,128)(2,1)S(1)}, bf16[1664,8192]{1,0:T(8,128)(2,1)}, u32[]{:S(2)}) copy-start(bf16[1664,8192]{1,0:T(8,128)(2,1)} %codes_ref.3) | copy-start | bytes 81788928

commit v2 on v0

v2 whole, which is shorter than its diff:
```python
import functools
import math

import jax
import jax.numpy as jnp
from jax import lax
from jax.experimental import pallas as pl
from jax.experimental.pallas import tpu as pltpu
from jax.sharding import PartitionSpec as P

MIB = 2**20
LANES = 128
CHUNK = 512
SLOTS = 6
SPAN = 512
AHEAD = 8
SPANS = (5, 3, 3, 5)

VMEM = pl.BlockSpec(memory_space=pltpu.VMEM)
HBM = pl.BlockSpec(memory_space=pltpu.HBM)
ANY = pl.BlockSpec(memory_space=pl.ANY)


def in_vmem(value):
    return pltpu.with_memory_space_constraint(value, pltpu.VMEM)


def in_hbm(value):
    return pltpu.with_memory_space_constraint(value, pltpu.HBM)


def fetch(source, target, sem):
    copy = pltpu.make_async_copy(source, target, sem)
    copy.start()
    return copy


def fetch_columns(first, step, codes_ref, out_ref, sems):
    copies = []
    for index in range(out_ref.shape[1] // step):
        here = codes_ref.at[:, pl.ds(first + index * step, step)]
        copies.append(fetch(here, out_ref.at[:, pl.ds(index * step, step)], sems.at[index]))
    return copies


def columns_kernel(first, step, bit, codes_ref, after_ref, out_ref, sign_ref, sems):
    copies = fetch_columns(first, step, codes_ref, out_ref, sems)
    sign = 1.0 - 2.0 * ((lax.axis_index("hx") // bit) % 2).astype(jnp.float32)
    sign_ref[...] = jnp.full(sign_ref.shape, sign, jnp.float32)
    for copy in copies:
        copy.wait()


def columns_small_kernel(first, step, codes_ref, after_ref, hadamard_ref, out_ref, small_ref, sems):
    copies = [fetch(hadamard_ref, small_ref, sems.at[out_ref.shape[1] // step])]
    copies += fetch_columns(first, step, codes_ref, out_ref, sems)
    for copy in copies:
        copy.wait()


def hidden_kernel(
    group, parts, bits, pieces_ref, gate_codes_ref, gate_scales_ref, up_codes_ref, up_scales_ref,
    gate_ref, up_ref, send_ref, signs_ref, buffers, gate_rows, up_rows, tokens_ref, wide_ref, gate_sum, up_sum, sems, scale_sems,
):
    depth, rows, units = buffers.shape
    everyone, own, tiles, lanes = pieces_ref.shape
    count = everyone // parts * own
    width = tiles * lanes
    steps = width // rows
    mine = lax.axis_index("groups")

    def copy(which, step):
        slot = lax.rem(2 * step + which, depth)
        source = (gate_codes_ref, up_codes_ref)[which]
        first = pl.multiple_of(mine * width + step * rows, rows)
        return pltpu.make_async_copy(source.at[pl.ds(first, rows), :], buffers.at[slot], sems.at[slot])

    first = pl.multiple_of(mine * (width // group), width // group)
    scale_copies = [
        fetch(gate_scales_ref.at[pl.ds(first, width // group), :], gate_rows, scale_sems.at[0]),
        fetch(up_scales_ref.at[pl.ds(first, width // group), :], up_rows, scale_sems.at[1]),
    ]
    ahead = depth // 2
    for step in range(min(ahead, steps)):
        for which in range(2):
            copy(which, step).start()
    me = lax.axis_index("hx")
    for index, bit in enumerate(bits):
        sign = 1.0 - 2.0 * ((me // bit) % 2).astype(jnp.float32)
        signs_ref[index] = jnp.full((count, units), sign, jnp.float32)
    for part in range(parts):
        begin = lax.rem(mine + part, parts) * (everyone // parts)
        for index in range(everyone // parts):
            for at in range(own):
                where = (part * count + index * own + at) * tiles
                wide_ref[where : where + tiles, :] = pieces_ref[begin + index, at].astype(jnp.float32)
    for tile in range(tiles):
        here = wide_ref[pl.ds(tile, parts * count, stride=tiles), :]
        tokens_ref[:, tile * lanes : (tile + 1) * lanes] = here.astype(jnp.bfloat16)
    gate_sum[...] = jnp.zeros_like(gate_sum)
    up_sum[...] = jnp.zeros_like(up_sum)
    low_half = lax.broadcasted_iota(jnp.int32, (parts * count, 2 * group), 1) < group
    for scale_copy in scale_copies:
        scale_copy.wait()

    def add(total_ref, scales_ref, which, step):
        slot = lax.rem(2 * step + which, depth)
        copy(which, step).wait()
        for pair in range(rows // (2 * group)):
            index = step * (rows // (2 * group)) + pair
            two = tokens_ref[:, pl.ds(pl.multiple_of(index * 2 * group, 2 * group), 2 * group)]
            none = jnp.zeros_like(two)
            stacked = jnp.concatenate([jnp.where(low_half, two, none), jnp.where(low_half, none, two)], axis=0)
            codes = buffers[slot, pair * 2 * group : (pair + 1) * 2 * group, :]
            sums = jnp.dot(stacked, codes, preferred_element_type=jnp.float32)
            total_ref[...] += (
                sums[: parts * count] * scales_ref[pl.ds(2 * index, 1), :]
                + sums[parts * count :] * scales_ref[pl.ds(2 * index + 1, 1), :]
            )

        @pl.when(step + ahead < steps)
        def _():
            copy(which, step + ahead).start()

    def body(step, carry):
        add(gate_sum, gate_rows, 0, step)
        add(up_sum, up_rows, 1, step)
        return carry

    lax.fori_loop(0, steps, body, 0, unroll=2)
    gate_ref[...] = gate_sum[:count, :]
    up_ref[...] = up_sum[:count, :]
    for part in range(1, parts):
        span = slice(part * count, (part + 1) * count)
        send_ref[part - 1, 0] = gate_sum[span, :].astype(send_ref.dtype)
        send_ref[part - 1, 1] = up_sum[span, :].astype(send_ref.dtype)


def rotate_kernel(parts, gate_ref, up_ref, hadamard_ref, *refs):
    others = refs[: parts - 1]
    out_ref, send_ref = refs[parts - 1 :]
    count, units = gate_ref.shape
    small = hadamard_ref.shape[0]
    high = units // small
    gate = gate_ref[...]
    up = up_ref[...]
    for other in others:
        gate = gate + other[0].astype(jnp.float32)
        up = up + other[1].astype(jnp.float32)
    hidden = gate / (1.0 + jnp.exp(-gate)) * up
    tall = jnp.concatenate([hidden[:, at * small : (at + 1) * small] for at in range(high)], axis=0)
    coarse = tall.astype(jnp.bfloat16)
    fine = (tall - coarse.astype(jnp.float32)).astype(jnp.bfloat16)
    factor = hadamard_ref[...].astype(jnp.bfloat16)
    tall = jnp.dot(coarse, factor, preferred_element_type=jnp.float32) + jnp.dot(
        fine, factor, preferred_element_type=jnp.float32
    )
    blocks = [tall[at * count : (at + 1) * count] for at in range(high)]
    bit = 1
    while bit < high:
        for at in range(high):
            if at & bit == 0:
                blocks[at], blocks[at | bit] = blocks[at] + blocks[at | bit], blocks[at] - blocks[at | bit]
        bit *= 2
    turned = jnp.concatenate(blocks, axis=1)
    out_ref[...] = turned
    send_ref[...] = turned.astype(send_ref.dtype)


def down_kernel(scale, masks, parts, *refs):
    turned_ref, codes_ref = refs[:2]
    held = refs[2 : 2 + parts]
    keep_ref, send_ref, wide_ref, buffers, sems = refs[2 + parts :]
    depth, _, span = buffers.shape
    begin = sum(part.shape[1] for part in held)
    total = (codes_ref.shape[1] - begin) // span

    def copy(step):
        here = codes_ref.at[:, pl.ds(begin + step * span, span)]
        return pltpu.make_async_copy(here, buffers.at[step % depth], sems.at[step % depth])

    for step in range(min(depth, total)):
        copy(step).start()
    me = lax.axis_index("hx")
    half, own, tiles, lanes = keep_ref.shape
    count = turned_ref.shape[0]
    rotated = (turned_ref[...] * scale).astype(jnp.bfloat16)
    row = lax.broadcasted_iota(jnp.int32, (count, count), 0)
    col = lax.broadcasted_iota(jnp.int32, (count, count), 1)
    slot = row // own
    mask = jnp.zeros_like(slot)
    for index in range(len(masks).bit_length() - 1):
        mask = mask | jnp.where((jnp.right_shift(slot, index) & 1) == 1, masks[1 << index], 0)
    order = ((slot * 0 + me) ^ mask) * own + (row - slot * own) == col
    rotated = jnp.dot(order.astype(jnp.bfloat16), rotated, preferred_element_type=jnp.float32).astype(jnp.bfloat16)

    def put(first, codes):
        sums = jnp.dot(rotated, codes, preferred_element_type=jnp.float32)
        for tile in range(span // lanes):
            wide_ref[pl.ds(first // lanes + tile, count, stride=tiles), :] = sums[:, tile * lanes : (tile + 1) * lanes]

    def put_streamed(step):
        copy(step).wait()
        put(begin + step * span, buffers[step % depth])
        if step + depth < total:
            copy(step + depth).start()

    base = 0
    for part in held:
        for first in range(0, part.shape[1], span):
            put(base + first, part[:, first : first + span])
        base += part.shape[1]
    for step in range(total):
        put_streamed(step)
    for index in range(half):
        for at in range(own):
            first = (index * own + at) * tiles
            keep_ref[index, at] = wide_ref[first : first + tiles, :]
            first += half * own * tiles
            send_ref[index, at] = wide_ref[first : first + tiles, :].astype(send_ref.dtype)


def per_device(
    parts, devices, tokens, gate_codes, gate_scales, up_codes, up_scales, down_codes, down_scales, hadamard
):
    width, units = gate_codes.shape
    group = width // gate_scales.shape[0]
    own = tokens.shape[0]
    count = own * devices
    total_units = units * devices
    bits = [1 << level for level in range(devices.bit_length() - 1)]
    tiles = width // LANES
    share = tiles // parts

    def swap(value, bit):
        return lax.ppermute(value, "hx", [(at, at ^ bit) for at in range(devices)])

    def cost(nbytes, flops=0):
        return pl.CostEstimate(flops=flops, bytes_accessed=nbytes, transcendentals=0)

    pieces = jnp.swapaxes(tokens.reshape(own, parts, share, LANES), 0, 1)
    pieces = jnp.broadcast_to(pieces[:, None], (parts, devices, own, share, LANES))
    pieces = pieces.reshape(parts * devices, own, share, LANES)
    pieces = lax.all_to_all(pieces, ("groups", "hx"), split_axis=0, concat_axis=0, tiled=True)

    early = [bit for index, bit in enumerate(bits) if not 1 <= index < 4]
    gate, up, send, signs = pl.pallas_call(
        functools.partial(hidden_kernel, group, parts, early),
        out_shape=(
            pltpu.VMEM((count, units), jnp.float32),
            pltpu.VMEM((count, units), jnp.float32),
            pltpu.VMEM((parts - 1, 2, count, units), jnp.bfloat16),
            pltpu.VMEM((len(early), count, units), jnp.float32),
        ),
        in_specs=[VMEM, HBM, HBM, HBM, HBM],
        out_specs=(VMEM, VMEM, VMEM, VMEM),
        scratch_shapes=[
            pltpu.VMEM((SLOTS, CHUNK, units), jnp.bfloat16),
            pltpu.VMEM((width // parts // group, units), jnp.float32),
            pltpu.VMEM((width // parts // group, units), jnp.float32),
            pltpu.VMEM((parts * count, width // parts), jnp.bfloat16),
            pltpu.VMEM((parts * count * share, LANES), jnp.float32),
            pltpu.VMEM((parts * count, units), jnp.float32),
            pltpu.VMEM((parts * count, units), jnp.float32),
            pltpu.SemaphoreType.DMA((SLOTS,)),
            pltpu.SemaphoreType.DMA((2,)),
        ],
        compiler_params=pltpu.CompilerParams(vmem_limit_bytes=24 * MIB),
        cost_estimate=cost(4 * width * units // parts, 4 * count * width * units),
    )(pieces, in_hbm(gate_codes), in_hbm(gate_scales), in_hbm(up_codes), in_hbm(up_scales))

    others = [
        lax.ppermute(send[step - 1], "groups", [(at, (at + step) % parts) for at in range(parts)]) for step in range(1, parts)
    ]
    held = []
    first = 0
    columns = SPANS[0] * SPAN
    part, small = pl.pallas_call(
        functools.partial(columns_small_kernel, first, SPAN),
        out_shape=(pltpu.VMEM((units, columns), jnp.bfloat16), pltpu.VMEM(hadamard.shape, hadamard.dtype)),
        in_specs=[HBM, ANY, HBM],
        out_specs=(VMEM, VMEM),
        scratch_shapes=[pltpu.SemaphoreType.DMA((SPANS[0] + 1,))],
        compiler_params=pltpu.CompilerParams(vmem_limit_bytes=2 * MIB),
        cost_estimate=cost(2 * units * columns),
    )(in_hbm(down_codes), send, in_hbm(hadamard))
    held.append(part)
    first += columns

    turned, send = pl.pallas_call(
        functools.partial(rotate_kernel, parts),
        out_shape=(pltpu.VMEM((count, units), jnp.float32), jax.ShapeDtypeStruct((count, units), jnp.bfloat16)),
        in_specs=[VMEM] * (2 + parts),
        out_specs=(VMEM, VMEM),
        compiler_params=pltpu.CompilerParams(vmem_limit_bytes=8 * MIB),
        cost_estimate=cost(16 * count * units),
    )(in_vmem(gate), in_vmem(up), in_vmem(small), *others)

    for index, bit in enumerate(bits):
        other = swap(send, bit)
        if 1 <= index < 4:
            columns = SPANS[index] * SPAN
            part, sign = pl.pallas_call(
                functools.partial(columns_kernel, first, SPAN, bit),
                out_shape=(pltpu.VMEM((units, columns), jnp.bfloat16), pltpu.VMEM((count, units), jnp.float32)),
                in_specs=[HBM, ANY],
                out_specs=(VMEM, VMEM),
                scratch_shapes=[pltpu.SemaphoreType.DMA((SPANS[index],))],
                compiler_params=pltpu.CompilerParams(vmem_limit_bytes=2 * MIB),
                cost_estimate=cost(2 * units * columns),
            )(in_hbm(down_codes), send)
            held.append(part)
            first += columns
        else:
            sign = signs[early.index(bit)]
        turned = turned * sign + other.astype(jnp.float32)
        send = turned.astype(jnp.bfloat16)

    order = [1] + [bit for bit in bits[1:]]
    spread = [0]
    for bit in reversed(order):
        spread = spread + [mask | bit for mask in spread]
    ahead = max(min((width - first) // SPAN, AHEAD), 1)
    keep, send = pl.pallas_call(
        functools.partial(down_kernel, 1.0 / math.sqrt(total_units), spread, len(held)),
        out_shape=(
            jax.ShapeDtypeStruct((devices // 2, own, tiles, LANES), jnp.float32),
            jax.ShapeDtypeStruct((devices // 2, own, tiles, LANES), jnp.bfloat16),
        ),
        in_specs=[VMEM, HBM] + [VMEM] * len(held),
        out_specs=(VMEM, VMEM),
        scratch_shapes=[
            pltpu.VMEM((count * tiles, LANES), jnp.float32),
            pltpu.VMEM((ahead, units, SPAN), jnp.bfloat16),
            pltpu.SemaphoreType.DMA((ahead,)),
        ],
        compiler_params=pltpu.CompilerParams(vmem_limit_bytes=20 * MIB),
        cost_estimate=cost(width * units, 2 * count * width * units),
    )(turned, in_hbm(down_codes), *[in_vmem(part) for part in held])
    summed = keep + swap(send, order[0]).astype(jnp.float32)
    for bit in order[1:]:
        half = summed.shape[0] // 2
        summed = summed[:half] + swap(summed[half:].astype(jnp.bfloat16), bit).astype(jnp.float32)
    return (summed.reshape(own, width) * down_scales[None, :]).astype(jnp.bfloat16)


def solution(mesh):
    in_specs = (
        P(("groups", "hx"), None),
        P(None, "hx"),
        P(None, "hx"),
        P(None, "hx"),
        P(None, "hx"),
        P("hx", None),
        P(),
        P(),
    )
    out_specs = P(("groups", "hx"), None)
    body = functools.partial(per_device, mesh.shape["groups"], mesh.shape["hx"])
    return jax.shard_map(body, mesh=mesh, in_specs=in_specs, out_specs=out_specs, check_vma=False)
```

time: 228 us -> 69.1 us (0.30)
  waiting for transfers between devices: 93.6 us -> 17.2 us
  other arithmetic: 42.7 us -> 1.02 us
  matrix products: 36.7 us -> 0 us
  Pallas kernels: 0 us -> 26.9 us
  blocking collectives: 34.2 us -> 17.4 us
  between operations: 13.6 us -> 0.13 us
  local copies, waits for them, and re-layouts: 3.02 us -> 0.7 us
    unnamed x2 -> x0, waiting for transfers between devices: 86.9 us -> none
    convert_element_type x3 -> x4, other arithmetic: 40.8 us -> 0.1 us  [the longest x3 0.09 us: per_device(): send = turned.astype(jnp.bfloat16)]
    dot_general x5 -> x0, matrix products: 36.7 us -> none  [the longest x1 13.2 us: per_device(): jnp.dot(rotated, down_codes, preferred_element_type=jnp.float32)]
    pallas_call x0 -> x7, Pallas kernels: none -> 26.9 us  [the longest x1 10.3 us: per_device(): pl.pallas_call(functools.partial(hidden_kernel, group, parts, early), out...]
    all_gather x1 -> x0, blocking collectives: 24.8 us -> none  [per_device(): tile_rows = lax.all_gather(tokens, 'hx', axis=0, tiled=True)]
    ppermute x0 -> x9, waiting for transfers between devices: none -> 17.2 us  [the longest x8 16.3 us: swap(): return lax.ppermute(value, 'hx', [(at, at ^ bit) for at in range(devices)])]
    all_to_all x1, blocking collectives: 9.4 us -> 17.4 us  [per_device(): lax.all_to_all(pieces, ('groups', 'hx'), split_axis=0, concat_axis=0, til...]
    all_to_all x1 -> x0, waiting for transfers between devices: 6.69 us -> none  [per_device(): lax.all_to_all(hidden.astype(jnp.bfloat16), 'hx', split_axis=0, concat_ax...]
  transfers between devices with their start and end apart: 2 -> 9, of which waited for: 2 -> 9; matrix products, arithmetic and copies ran while one was open for 0% -> 0% of each run, Pallas kernels for 0% -> 18%
where the time goes in v2:
time: 69.1 us; the launch traced here: 68.9 us
  Pallas kernels  26.9 us (39%)
  blocking collectives  17.4 us (25%)
  waiting for transfers between devices  17.2 us (25%)
  starting transfers between devices  5.6 us (8%)
  other arithmetic  1.02 us (1%)
  local copies, waits for them, and re-layouts  0.7 us (1%)
    all_to_all x1, blocking collectives, per_device(): lax.all_to_all(pieces, ('groups', 'hx'), split_axis=0, concat_axis=0, til...  17.4 us
    ppermute x8, waiting for transfers between devices, swap(): return lax.ppermute(value, 'hx', [(at, at ^ bit) for at in range(devices)])  16.3 us
    pallas_call x1, Pallas kernels, per_device(): pl.pallas_call(functools.partial(hidden_kernel, group, parts, early), out...  10.3 us
    pallas_call x3, Pallas kernels, per_device(): pl.pallas_call(functools.partial(columns_kernel, first, SPAN, bit), out_s...  8.63 us
    ppermute x8, starting transfers between devices, swap(): return lax.ppermute(value, 'hx', [(at, at ^ bit) for at in range(devices)])  4.8 us
    pallas_call x1, Pallas kernels, per_device(): pl.pallas_call(functools.partial(down_kernel, 1.0 / math.sqrt(total_units...  3.84 us
    pallas_call x1, Pallas kernels, per_device(): pl.pallas_call(functools.partial(columns_small_kernel, first, SPAN), out_...  3.59 us
  transfers between devices with their start and end apart: 9, of which 9 were waited for; matrix products, arithmetic and copies ran while one was open for 0% of the time, Pallas kernels for 18%

profile of v2, /device:TPU:0, one launch (start us, length us, event | category | flops | bytes accessed | tf_op | source)
XLA Modules:
  0.0 68.9 jit_solution(17397727450230310052)
XLA Ops:
  0.0 0.8 %reduce = bf16[8192]{0:T(1024)(128)(2,1)S(1)} reduce(bf16[1,8192]{1,0:T(2,128)(2,1)} %param.8, bf16[]{:T(256)} %constant.1), dimensions={0}, to_apply=%param.8.reduce_sub_computation | reduce | bytes 32770 | tf_op args[0]
  0.9 17.4 %all_to_all.5.pieces_ref = bf16[32,1,32,128]{3,2,1,0:T(8,128)(2,1)S(1)} all-to-all(bf16[32,1,32,128]{3,2,1,0:T(8,128)(2,1)S(1)} %bitcast.15), channel_id=1, replica_groups=mesh['groups'=2,'hx'=16] {'groups','hx'}, dimensions={0} | all-to-all | bytes 524288 | tf_op jit(solution)/shard_map/all_to_all | solution.py:244
  18.3 10.3 %shard_map.82 = (f32[16,1664]{1,0:T(8,128)S(1)}, f32[16,1664]{1,0:T(8,128)S(1)}, bf16[1,2,16,1664]{3,2,1,0:T(8,128)(2,1)S(1)}, f32[1,16,1664]{2,1,0:T(8,128)S(1)}) custom-call(bf16[32,1,32,128]{3,2,1,0:T(8,128)(2,1)S(1)} %all_to_all.5.pieces_ref, bf16[8192,1664]{1,0:T(8,128)(2,1)} %gate_codes_ref.1, f32[64,1664]{1,0:T(8,128)} %gate_scales_ref.1, ...), custom_call_target="tpu_custom_call" | custom-call | flops 872415232 | bytes 27262976 | tf_op jit(solution)/shard_map/pallas_call | solution.py:247
  28.6 0.8 %collective-permute-start = (bf16[2,16,1664]{2,1,0:T(8,128)(2,1)S(1)}, bf16[2,16,1664]{2,1,0:T(8,128)(2,1)S(1)}, u32[]{:S(2)}, u32[]{:S(2)}) collective-permute-start(bf16[2,16,1664]{2,1,0:T(8,128)(2,1)S(1)} %bitcast.14), channel_id=1, source_target_pairs={{0,16},{16,0},{1,17},{17,1},{2,18},{18,2},{3,19},{19,3},{4,20},{20... | collective-permute-start | bytes 319496 | tf_op jit(solution)/shard_map/ppermute | solution.py:273
  29.5 3.6 %shard_map.83 = (bf16[1664,2560]{1,0:T(8,128)(2,1)S(1)}, s32[52,52]{1,0:T(8,128)S(1)}) custom-call(bf16[1664,8192]{1,0:T(8,128)(2,1)} %refs_1_.1, bf16[1,2,16,1664]{3,2,1,0:T(8,128)(2,1)S(1)} %get-tuple-element.23.after_ref, s32[52,52]{1,0:T(8,128)} %hadamard_ref.1), custom_call_target="tpu_custom_call" | custom-call | bytes 8519680 | tf_op jit(solution)/shard_map/pallas_call | solution.py:278
  33.1 0.8 %collective-permute-done.refs_0_ = bf16[2,16,1664]{2,1,0:T(8,128)(2,1)S(1)} collective-permute-done((bf16[2,16,1664]{2,1,0:T(8,128)(2,1)S(1)}, bf16[2,16,1664]{2,1,0:T(8,128)(2,1)S(1)}, u32[]{:S(2)}, u32[]{:S(2)}) %collective-permute-start) | collective-permute-done | bytes 106528 | tf_op jit(solution)/shard_map/ppermute | solution.py:273
  33.9 0.5 shard_map.84
  34.4 0.1 collective-permute-start.1
  34.4 1.2 %collective-permute-done.1 = bf16[16,1664]{1,0:T(8,128)(2,1)S(1)} collective-permute-done((bf16[16,1664]{1,0:T(8,128)(2,1)S(1)}, bf16[16,1664]{1,0:T(8,128)(2,1)S(1)}, u32[]{:S(2)}, u32[]{:S(2)}) %collective-permute-start.1) | collective-permute-done | bytes 53280 | tf_op jit(solution)/shard_map/ppermute | solution.py:236
  35.7 1.1 %collective-permute-start.2 = (bf16[16,1664]{1,0:T(8,128)(2,1)S(1)}, bf16[16,1664]{1,0:T(8,128)(2,1)S(1)}, u32[]{:S(2)}, u32[]{:S(2)}) collective-permute-start(bf16[16,1664]{1,0:T(8,128)(2,1)S(1)} %get-tuple-element.39.after_ref), channel_id=1, source_target_pairs={{0,2},{1,3},{2,0},{3,1},{4,6},{5,7},{6,4},{7,5},{8,10},{9,11},{10,... | collective-permute-start | bytes 159752 | tf_op jit(solution)/shard_map/ppermute | solution.py:236
  36.8 2.5 %shard_map.85 = (bf16[1664,1536]{1,0:T(8,128)(2,1)S(1)}, f32[16,1664]{1,0:T(8,128)S(1)}) custom-call(bf16[1664,8192]{1,0:T(8,128)(2,1)} %refs_1_.1, bf16[16,1664]{1,0:T(8,128)(2,1)S(1)} %get-tuple-element.39.after_ref), custom_call_target="tpu_custom_call" | custom-call | bytes 5111808 | tf_op jit(solution)/shard_map/pallas_call | solution.py:303
  39.3 0.6 collective-permute-done.2
  39.9 0.7 %collective-permute-start.3 = (bf16[16,1664]{1,0:T(8,128)(2,1)S(1)}, bf16[16,1664]{1,0:T(8,128)(2,1)S(1)}, u32[]{:S(2)}, u32[]{:S(2)}) collective-permute-start(bf16[16,1664]{1,0:T(8,128)(2,1)S(1)} %fusion.4.after_ref), channel_id=1, source_target_pairs={{0,4},{1,5},{2,6},{3,7},{4,0},{5,1},{6,2},{7,3},{8,12},{9,13},{10,... | collective-permute-start | bytes 159752 | tf_op jit(solution)/shard_map/ppermute | solution.py:236
  40.6 2.5 %shard_map.86 = (bf16[1664,1536]{1,0:T(8,128)(2,1)S(1)}, f32[16,1664]{1,0:T(8,128)S(1)}) custom-call(bf16[1664,8192]{1,0:T(8,128)(2,1)} %refs_1_.1, bf16[16,1664]{1,0:T(8,128)(2,1)S(1)} %fusion.4.after_ref), custom_call_target="tpu_custom_call" | custom-call | bytes 5111808 | tf_op jit(solution)/shard_map/pallas_call | solution.py:303
  43.2 0.9 %collective-permute-done.3 = bf16[16,1664]{1,0:T(8,128)(2,1)S(1)} collective-permute-done((bf16[16,1664]{1,0:T(8,128)(2,1)S(1)}, bf16[16,1664]{1,0:T(8,128)(2,1)S(1)}, u32[]{:S(2)}, u32[]{:S(2)}) %collective-permute-start.3) | collective-permute-done | bytes 53280 | tf_op jit(solution)/shard_map/ppermute | solution.py:236
  44.2 0.7 collective-permute-start.4
  44.8 3.6 %shard_map.87 = (bf16[1664,2560]{1,0:T(8,128)(2,1)S(1)}, f32[16,1664]{1,0:T(8,128)S(1)}) custom-call(bf16[1664,8192]{1,0:T(8,128)(2,1)} %refs_1_.1, bf16[16,1664]{1,0:T(8,128)(2,1)S(1)} %get-tuple-element.37.after_ref), custom_call_target="tpu_custom_call" | custom-call | bytes 8519680 | tf_op jit(solution)/shard_map/pallas_call | solution.py:303
  48.4 1.4 %collective-permute-done.4 = bf16[16,1664]{1,0:T(8,128)(2,1)S(1)} collective-permute-done((bf16[16,1664]{1,0:T(8,128)(2,1)S(1)}, bf16[16,1664]{1,0:T(8,128)(2,1)S(1)}, u32[]{:S(2)}, u32[]{:S(2)}) %collective-permute-start.4) | collective-permute-done | bytes 53280 | tf_op jit(solution)/shard_map/ppermute | solution.py:236
  49.8 0.0 copy-start
  49.9 3.8 %shard_map.88 = (f32[8,1,64,128]{3,2,1,0:T(8,128)S(1)}, bf16[8,1,64,128]{3,2,1,0:T(8,128)(2,1)S(1)}) custom-call(f32[16,1664]{1,0:T(8,128)S(1)} %convert_add_fusion.1.refs_0_, bf16[1664,8192]{1,0:T(8,128)(2,1)} %refs_1_.1, bf16[1664,2560]{1,0:T(8,128)(2,1)S(1)} %get-tuple-element.31.refs_2_, bf16[1664,1536]{1,0:T(8,128)(2,1)S(1)} %get-tuple-element.32.refs_3_, ...), custom_call_target="tpu_custom_call" | custom-call | flops 436207616 | bytes 13631488 | tf_op jit(solution)/shard_map/pallas_call | solution.py:324
  53.7 0.1 collective-permute-start.5
  53.8 1.3 %collective-permute-done.5 = bf16[8,1,64,128]{3,2,1,0:T(8,128)(2,1)S(1)} collective-permute-done((bf16[8,1,64,128]{3,2,1,0:T(8,128)(2,1)S(1)}, bf16[8,1,64,128]{3,2,1,0:T(8,128)(2,1)S(1)}, u32[]{:S(2)}, u32[]{:S(2)}) %collective-permute-start.5) | collective-permute-done | bytes 131104 | tf_op jit(solution)/shard_map/ppermute | solution.py:236
  55.2 1.0 %collective-permute-start.6 = (bf16[4,1,64,128]{3,2,1,0:T(8,128)(2,1)S(1)}, bf16[4,1,64,128]{3,2,1,0:T(8,128)(2,1)S(1)}, u32[]{:S(2)}, u32[]{:S(2)}) collective-permute-start(bf16[4,1,64,128]{3,2,1,0:T(8,128)(2,1)S(1)} %slice.45), channel_id=1, source_target_pairs={{0,2},{1,3},{2,0},{3,1},{4,6},{5,7},{6,4},{7,5},{8,10},{9,11},{10,... | collective-permute-start | bytes 196616 | tf_op jit(solution)/shard_map/ppermute | solution.py:236
  56.1 3.4 %collective-permute-done.6 = bf16[4,1,64,128]{3,2,1,0:T(8,128)(2,1)S(1)} collective-permute-done((bf16[4,1,64,128]{3,2,1,0:T(8,128)(2,1)S(1)}, bf16[4,1,64,128]{3,2,1,0:T(8,128)(2,1)S(1)}, u32[]{:S(2)}, u32[]{:S(2)}) %collective-permute-start.6) | collective-permute-done | bytes 65568 | tf_op jit(solution)/shard_map/ppermute | solution.py:236
  59.5 0.3 collective-permute-start.7
  59.8 3.7 %collective-permute-done.7 = bf16[2,1,64,128]{3,2,1,0:T(8,128)(2,1)S(1)} collective-permute-done((bf16[2,1,64,128]{3,2,1,0:T(8,128)(2,1)S(1)}, bf16[2,1,64,128]{3,2,1,0:T(8,128)(2,1)S(1)}, u32[]{:S(2)}, u32[]{:S(2)}) %collective-permute-start.7) | collective-permute-done | bytes 32800 | tf_op jit(solution)/shard_map/ppermute | solution.py:236
  63.5 1.0 %collective-permute-start.8 = (bf16[1,1,64,128]{3,2,1,0:T(8,128)(2,1)S(1)}, bf16[1,1,64,128]{3,2,1,0:T(8,128)(2,1)S(1)}, u32[]{:S(2)}, u32[]{:S(2)}) collective-permute-start(bf16[1,1,64,128]{3,2,1,0:T(8,128)(2,1)S(1)} %slice.47), channel_id=1, source_target_pairs={{0,8},{1,9},{2,10},{3,11},{4,12},{5,13},{6,14},{7,15},{8,0},{9,1},... | collective-permute-start | bytes 49160 | tf_op jit(solution)/shard_map/ppermute | solution.py:236
  64.5 3.7 %collective-permute-done.8 = bf16[1,1,64,128]{3,2,1,0:T(8,128)(2,1)S(1)} collective-permute-done((bf16[1,1,64,128]{3,2,1,0:T(8,128)(2,1)S(1)}, bf16[1,1,64,128]{3,2,1,0:T(8,128)(2,1)S(1)}, u32[]{:S(2)}, u32[]{:S(2)}) %collective-permute-start.8) | collective-permute-done | bytes 16416 | tf_op jit(solution)/shard_map/ppermute | solution.py:236
  68.3 0.0 copy-done
  68.3 0.6 convert_element_type.54
  (12 shorter events, 0.2 us)
Async XLA Ops:
  28.6 5.2 %collective-permute-start = (bf16[2,16,1664]{2,1,0:T(8,128)(2,1)S(1)}, bf16[2,16,1664]{2,1,0:T(8,128)(2,1)S(1)}, u32[]{:S(2)}, u32[]{:S(2)}) collective-permute-start(bf16[2,16,1664]{2,1,0:T(8,128)(2,1)S(1)} %bitcast.14), channel_id=1, source_target_pairs={{0,16},{16,0},{1,17},{17,1},{2,18},{18,2},{3,19},{19,3},{4,20},{20... | collective-permute-start | bytes 319496 | tf_op jit(solution)/shard_map/ppermute | solution.py:273
  34.4 1.3 %collective-permute-start.1 = (bf16[16,1664]{1,0:T(8,128)(2,1)S(1)}, bf16[16,1664]{1,0:T(8,128)(2,1)S(1)}, u32[]{:S(2)}, u32[]{:S(2)}) collective-permute-start(bf16[16,1664]{1,0:T(8,128)(2,1)S(1)} %get-tuple-element.27), channel_id=1, source_target_pairs={{0,1},{1,0},{2,3},{3,2},{4,5},{5,4},{6,7},{7,6},{8,9},{9,8},{10,11... | collective-permute-start | bytes 159752 | tf_op jit(solution)/shard_map/ppermute | solution.py:236
  35.7 4.2 %collective-permute-start.2 = (bf16[16,1664]{1,0:T(8,128)(2,1)S(1)}, bf16[16,1664]{1,0:T(8,128)(2,1)S(1)}, u32[]{:S(2)}, u32[]{:S(2)}) collective-permute-start(bf16[16,1664]{1,0:T(8,128)(2,1)S(1)} %get-tuple-element.39.after_ref), channel_id=1, source_target_pairs={{0,2},{1,3},{2,0},{3,1},{4,6},{5,7},{6,4},{7,5},{8,10},{9,11},{10,... | collective-permute-start | bytes 159752 | tf_op jit(solution)/shard_map/ppermute | solution.py:236
  39.9 4.2 %collective-permute-start.3 = (bf16[16,1664]{1,0:T(8,128)(2,1)S(1)}, bf16[16,1664]{1,0:T(8,128)(2,1)S(1)}, u32[]{:S(2)}, u32[]{:S(2)}) collective-permute-start(bf16[16,1664]{1,0:T(8,128)(2,1)S(1)} %fusion.4.after_ref), channel_id=1, source_target_pairs={{0,4},{1,5},{2,6},{3,7},{4,0},{5,1},{6,2},{7,3},{8,12},{9,13},{10,... | collective-permute-start | bytes 159752 | tf_op jit(solution)/shard_map/ppermute | solution.py:236
  44.2 5.7 %collective-permute-start.4 = (bf16[16,1664]{1,0:T(8,128)(2,1)S(1)}, bf16[16,1664]{1,0:T(8,128)(2,1)S(1)}, u32[]{:S(2)}, u32[]{:S(2)}) collective-permute-start(bf16[16,1664]{1,0:T(8,128)(2,1)S(1)} %get-tuple-element.37.after_ref), channel_id=1, source_target_pairs={{0,8},{1,9},{2,10},{3,11},{4,12},{5,13},{6,14},{7,15},{8,0},{9,1},... | collective-permute-start | bytes 159752 | tf_op jit(solution)/shard_map/ppermute | solution.py:236
  49.8 18.4 %copy-start = (f32[8192]{0:T(1024)S(1)}, f32[8192]{0:T(1024)}, u32[]{:S(2)}) copy-start(f32[8192]{0:T(1024)} %param.14) | copy-start | bytes 98308
  53.7 1.4 %collective-permute-start.5 = (bf16[8,1,64,128]{3,2,1,0:T(8,128)(2,1)S(1)}, bf16[8,1,64,128]{3,2,1,0:T(8,128)(2,1)S(1)}, u32[]{:S(2)}, u32[]{:S(2)}) collective-permute-start(bf16[8,1,64,128]{3,2,1,0:T(8,128)(2,1)S(1)} %get-tuple-element.36), channel_id=1, source_target_pairs={{0,1},{1,0},{2,3},{3,2},{4,5},{5,4},{6,7},{7,6},{8,9},{9,8},{10,11... | collective-permute-start | bytes 393224 | tf_op jit(solution)/shard_map/ppermute | solution.py:236
  55.2 4.3 %collective-permute-start.6 = (bf16[4,1,64,128]{3,2,1,0:T(8,128)(2,1)S(1)}, bf16[4,1,64,128]{3,2,1,0:T(8,128)(2,1)S(1)}, u32[]{:S(2)}, u32[]{:S(2)}) collective-permute-start(bf16[4,1,64,128]{3,2,1,0:T(8,128)(2,1)S(1)} %slice.45), channel_id=1, source_target_pairs={{0,2},{1,3},{2,0},{3,1},{4,6},{5,7},{6,4},{7,5},{8,10},{9,11},{10,... | collective-permute-start | bytes 196616 | tf_op jit(solution)/shard_map/ppermute | solution.py:236
  59.5 4.0 %collective-permute-start.7 = (bf16[2,1,64,128]{3,2,1,0:T(8,128)(2,1)S(1)}, bf16[2,1,64,128]{3,2,1,0:T(8,128)(2,1)S(1)}, u32[]{:S(2)}, u32[]{:S(2)}) collective-permute-start(bf16[2,1,64,128]{3,2,1,0:T(8,128)(2,1)S(1)} %slice.46), channel_id=1, source_target_pairs={{0,4},{1,5},{2,6},{3,7},{4,0},{5,1},{6,2},{7,3},{8,12},{9,13},{10,... | collective-permute-start | bytes 98312 | tf_op jit(solution)/shard_map/ppermute | solution.py:236
  63.5 4.7 %collective-permute-start.8 = (bf16[1,1,64,128]{3,2,1,0:T(8,128)(2,1)S(1)}, bf16[1,1,64,128]{3,2,1,0:T(8,128)(2,1)S(1)}, u32[]{:S(2)}, u32[]{:S(2)}) collective-permute-start(bf16[1,1,64,128]{3,2,1,0:T(8,128)(2,1)S(1)} %slice.47), channel_id=1, source_target_pairs={{0,8},{1,9},{2,10},{3,11},{4,12},{5,13},{6,14},{7,15},{8,0},{9,1},... | collective-permute-start | bytes 49160 | tf_op jit(solution)/shard_map/ppermute | solution.py:236

commit v3 on v2

v3 whole, which is shorter than its diff:
```python
import functools
import math

import jax
import jax.numpy as jnp
from jax import lax
from jax.experimental import pallas as pl
from jax.experimental.pallas import tpu as pltpu
from jax.sharding import PartitionSpec as P

MIB = 2**20
F8 = jnp.float8_e4m3fn
LANES = 128
CHUNK = 512
SLOTS = 5
UNROLL = 2
ROWS = (2, 5, 5)
SPAN = 512
AHEAD = 8
SPANS = (0, 5, 5, 6)

VMEM = pl.BlockSpec(memory_space=pltpu.VMEM)
HBM = pl.BlockSpec(memory_space=pltpu.HBM)
ANY = pl.BlockSpec(memory_space=pl.ANY)


def in_vmem(value):
    return pltpu.with_memory_space_constraint(value, pltpu.VMEM)


def in_hbm(value):
    return pltpu.with_memory_space_constraint(value, pltpu.HBM)


def fetch(source, target, sem):
    copy = pltpu.make_async_copy(source, target, sem)
    copy.start()
    return copy


def fetch_columns(first, step, codes_ref, out_ref, sems):
    copies = []
    for index in range(out_ref.shape[1] // step):
        here = codes_ref.at[:, pl.ds(first + index * step, step)]
        copies.append(fetch(here, out_ref.at[:, pl.ds(index * step, step)], sems.at[index]))
    return copies


def columns_kernel(first, step, bit, codes_ref, after_ref, out_ref, sign_ref, sems):
    copies = fetch_columns(first, step, codes_ref, out_ref, sems)
    sign = 1.0 - 2.0 * ((lax.axis_index("hx") // bit) % 2).astype(jnp.float32)
    sign_ref[...] = jnp.full(sign_ref.shape, sign, jnp.float32)
    for copy in copies:
        copy.wait()


def rows_kernel(first, step, codes_ref, after_ref, out_ref, same_ref, sems):
    copies = [fetch(after_ref, same_ref, sems.at[out_ref.shape[0] // step])]
    for index in range(out_ref.shape[0] // step):
        here = codes_ref.at[pl.ds(first + index * step, step), :]
        copies.append(fetch(here, out_ref.at[pl.ds(index * step, step), :], sems.at[index]))
    for copy in copies:
        copy.wait()


def first_rows_kernel(first, step, codes_ref, tokens_ref, out_ref, tiled_ref, token_ref, wide_ref, sems):
    _, own, tiles, lanes = tiled_ref.shape
    token = fetch(tokens_ref, token_ref, sems.at[out_ref.shape[0] // step])
    copies = []
    for index in range(out_ref.shape[0] // step):
        here = codes_ref.at[pl.ds(first + index * step, step), :]
        copies.append(fetch(here, out_ref.at[pl.ds(index * step, step), :], sems.at[index]))
    token.wait()
    for at in range(own):
        row = token_ref[at : at + 1, :].astype(jnp.float32)
        for tile in range(tiles):
            wide_ref[tile : tile + 1, :] = row[:, tile * lanes : (tile + 1) * lanes]
        tiled_ref[0, at] = wide_ref[...].astype(tiled_ref.dtype)
    for copy in copies:
        copy.wait()


def rotate(gate, up, hadamard):
    count, units = gate.shape
    small = hadamard.shape[0]
    high = units // small
    hidden = gate / (1.0 + jnp.exp(-gate)) * up
    tall = jnp.concatenate([hidden[:, at * small : (at + 1) * small] for at in range(high)], axis=0)
    coarse = tall.astype(jnp.bfloat16)
    fine = (tall - coarse.astype(jnp.float32)).astype(jnp.bfloat16)
    factor = hadamard.astype(jnp.bfloat16)
    tall = jnp.dot(coarse, factor, preferred_element_type=jnp.float32) + jnp.dot(
        fine, factor, preferred_element_type=jnp.float32
    )
    blocks = [tall[at * count : (at + 1) * count] for at in range(high)]
    bit = 1
    while bit < high:
        for at in range(high):
            if at & bit == 0:
                blocks[at], blocks[at | bit] = blocks[at] + blocks[at | bit], blocks[at] - blocks[at | bit]
        bit *= 2
    return jnp.concatenate(blocks, axis=1)


def hidden_kernel(group, masks, bits, parts, *refs):
    pieces_ref, gate_codes_ref, gate_scales_ref, up_codes_ref, up_scales_ref, hadamard_ref = refs[:6]
    held = refs[6 : 6 + parts]
    out_ref, send_ref, signs_ref, buffers, late, gate_rows, up_rows, small_ref, tokens_ref, wide_ref = refs[6 + parts : 16 + parts]
    gate_sum, up_sum, sems, late_sems, small_sems = refs[16 + parts :]
    depth, rows, units = buffers.shape
    devices, own, tiles, lanes = pieces_ref.shape
    count = devices * own
    steps = up_codes_ref.shape[0] // rows
    ready = sum(part.shape[0] for part in held) // rows
    late_steps = steps - ready

    def copy(step):
        slot = lax.rem(step, depth)
        first = pl.multiple_of(step * rows, rows)
        return pltpu.make_async_copy(up_codes_ref.at[pl.ds(first, rows), :], buffers.at[slot], sems.at[slot])

    def late_copy(index):
        source = gate_codes_ref.at[pl.ds(pl.multiple_of((ready + index) * rows, rows), rows), :]
        target = late.at[pl.ds(pl.multiple_of(index * rows, rows), rows), :]
        return pltpu.make_async_copy(source, target, late_sems.at[index])

    copy(0).start()
    small_copies = [
        fetch(up_scales_ref, up_rows, small_sems.at[1]),
        fetch(gate_scales_ref, gate_rows, small_sems.at[0]),
        fetch(hadamard_ref, small_ref, small_sems.at[2]),
    ]
    for step in range(1, min(depth, steps)):
        copy(step).start()
    me = lax.axis_index("hx")
    for index, bit in enumerate(bits):
        sign = 1.0 - 2.0 * ((me // bit) % 2).astype(jnp.float32)
        signs_ref[index] = jnp.full((count, units), sign, jnp.float32)
    for slot, mask in enumerate(masks):
        for at in range(own):
            where = pl.multiple_of(((me ^ mask) * own + at) * tiles, tiles)
            wide_ref[pl.ds(where, tiles), :] = pieces_ref[slot, at].astype(jnp.float32)
    for tile in range(tiles):
        here = wide_ref[pl.ds(tile, count, stride=tiles), :]
        tokens_ref[:, tile * lanes : (tile + 1) * lanes] = here.astype(jnp.bfloat16)
    gate_sum[...] = jnp.zeros_like(gate_sum)
    up_sum[...] = jnp.zeros_like(up_sum)
    low_half = lax.broadcasted_iota(jnp.int32, (count, 2 * group), 1) < group
    for small_copy in small_copies:
        small_copy.wait()

    def add(total_ref, scales_ref, step, codes):
        for pair in range(rows // (2 * group)):
            index = step * (rows // (2 * group)) + pair
            two = tokens_ref[:, pl.ds(pl.multiple_of(index * 2 * group, 2 * group), 2 * group)]
            none = jnp.zeros_like(two)
            stacked = jnp.concatenate([jnp.where(low_half, two, none), jnp.where(low_half, none, two)], axis=0)
            sums = jnp.dot(stacked, codes(pair * 2 * group).astype(F8), preferred_element_type=jnp.float32)
            total_ref[...] += (
                sums[:count] * scales_ref[pl.ds(2 * index, 1), :] + sums[count:] * scales_ref[pl.ds(2 * index + 1, 1), :]
            )

    def loop(begin, end, source, base, waits):
        def body(step, carry):
            slot = lax.rem(step, depth)

            def in_source(first):
                return source[pl.ds(pl.multiple_of((step - base) * rows + first, 2 * group), 2 * group), :]

            def in_buffer(first):
                return buffers[slot, first : first + 2 * group, :]

            if not waits:

                @pl.when((lax.rem(step, 2) == 0) & (step // 2 < late_steps))
                def _():
                    late_copy(step // 2).start()

            else:
                late_copy(step - ready).wait()
            add(gate_sum, gate_rows, step, in_source)
            copy(step).wait()
            add(up_sum, up_rows, step, in_buffer)

            @pl.when(step + depth < steps)
            def _():
                copy(step + depth).start()

            return carry

        lax.fori_loop(begin, end, body, 0, unroll=UNROLL)

    before = 0
    for part in held:
        here = part.shape[0] // rows
        loop(before, before + here, part, before, False)
        before += here
    for index in range((ready + 1) // 2, late_steps):
        late_copy(index).start()
    loop(ready, steps, late, ready, True)
    turned = rotate(gate_sum[...], up_sum[...], small_ref[...])
    out_ref[...] = turned
    send_ref[...] = turned.astype(send_ref.dtype)


def down_kernel(scale, masks, parts, *refs):
    turned_ref, codes_ref = refs[:2]
    held = refs[2 : 2 + parts]
    keep_ref, send_ref, wide_ref, buffers, sems = refs[2 + parts :]
    depth, _, span = buffers.shape
    begin = sum(part.shape[1] for part in held)
    total = (codes_ref.shape[1] - begin) // span

    def copy(step):
        here = codes_ref.at[:, pl.ds(begin + step * span, span)]
        return pltpu.make_async_copy(here, buffers.at[step % depth], sems.at[step % depth])

    for step in range(min(depth, total)):
        copy(step).start()
    me = lax.axis_index("hx")
    half, own, tiles, lanes = keep_ref.shape
    count = turned_ref.shape[0]
    rotated = (turned_ref[...] * scale).astype(jnp.bfloat16)
    row = lax.broadcasted_iota(jnp.int32, (count, count), 0)
    col = lax.broadcasted_iota(jnp.int32, (count, count), 1)
    slot = row // own
    mask = jnp.zeros_like(slot)
    for index in range(len(masks).bit_length() - 1):
        mask = mask | jnp.where((jnp.right_shift(slot, index) & 1) == 1, masks[1 << index], 0)
    order = ((slot * 0 + me) ^ mask) * own + (row - slot * own) == col
    rotated = jnp.dot(order.astype(jnp.bfloat16), rotated, preferred_element_type=jnp.float32).astype(jnp.bfloat16)

    def put(first, codes):
        sums = jnp.dot(rotated, codes.astype(F8), preferred_element_type=jnp.float32)
        for tile in range(span // lanes):
            wide_ref[pl.ds(first // lanes + tile, count, stride=tiles), :] = sums[:, tile * lanes : (tile + 1) * lanes]

    def put_streamed(step):
        copy(step).wait()
        put(begin + step * span, buffers[step % depth])
        if step + depth < total:
            copy(step + depth).start()

    base = 0
    for part in held:
        for first in range(0, part.shape[1], span):
            put(base + first, part[:, first : first + span])
        base += part.shape[1]
    for step in range(total):
        put_streamed(step)
    for index in range(half):
        for at in range(own):
            first = (index * own + at) * tiles
            keep_ref[index, at] = wide_ref[first : first + tiles, :]
            first += half * own * tiles
            send_ref[index, at] = wide_ref[first : first + tiles, :].astype(send_ref.dtype)


def per_device(
    devices, tokens, gate_codes, gate_scales, up_codes, up_scales, down_codes, down_scales, hadamard
):
    width, units = gate_codes.shape
    group = width // gate_scales.shape[0]
    own = tokens.shape[0]
    count = own * devices
    total_units = units * devices
    bits = [1 << level for level in range(devices.bit_length() - 1)]
    tiles = width // LANES

    def swap(value, bit):
        return lax.ppermute(value, "hx", [(at, at ^ bit) for at in range(devices)])

    def cost(nbytes, flops=0):
        return pl.CostEstimate(flops=flops, bytes_accessed=nbytes, transcendentals=0)

    pieces = tokens
    gathered = [0]
    held = []
    first = 0
    for index, bit in enumerate(reversed(bits)):
        other = swap(pieces, bit)
        if index < len(ROWS):
            rows = ROWS[index] * CHUNK
            scratch = [pltpu.SemaphoreType.DMA((ROWS[index] + 1,))]
            if index == 0:
                scratch = [pltpu.VMEM((own, width), tokens.dtype), pltpu.VMEM((tiles, LANES), jnp.float32)] + scratch
            part, pieces = pl.pallas_call(
                functools.partial(first_rows_kernel if index == 0 else rows_kernel, first, CHUNK),
                out_shape=(
                    pltpu.VMEM((rows, units), jnp.bfloat16),
                    pltpu.VMEM((1 << index, own, tiles, LANES), tokens.dtype),
                ),
                in_specs=[HBM, HBM if index == 0 else ANY],
                out_specs=(VMEM, VMEM),
                scratch_shapes=scratch,
                compiler_params=pltpu.CompilerParams(vmem_limit_bytes=2 * MIB),
                cost_estimate=cost(2 * rows * units),
            )(in_hbm(gate_codes), in_hbm(pieces) if index == 0 else pieces)
            held.append(part)
            first += rows
        if index == 0:
            other = other.reshape(1, own, tiles, LANES)
        pieces = jnp.concatenate([pieces, other], axis=0)
        gathered = gathered + [mask | bit for mask in gathered]

    early = [bit for index, bit in enumerate(bits) if not 1 <= index < 4]
    turned, send, signs = pl.pallas_call(
        functools.partial(hidden_kernel, group, gathered, early, len(held)),
        out_shape=(
            pltpu.VMEM((count, units), jnp.float32),
            jax.ShapeDtypeStruct((count, units), jnp.bfloat16),
            pltpu.VMEM((len(early), count, units), jnp.float32),
        ),
        in_specs=[VMEM, HBM, HBM, HBM, HBM, HBM] + [VMEM] * len(held),
        out_specs=(VMEM, VMEM, VMEM),
        scratch_shapes=[
            pltpu.VMEM((SLOTS, CHUNK, units), jnp.bfloat16),
            pltpu.VMEM((width - first, units), jnp.bfloat16),
            pltpu.VMEM(gate_scales.shape, gate_scales.dtype),
            pltpu.VMEM(up_scales.shape, up_scales.dtype),
            pltpu.VMEM(hadamard.shape, hadamard.dtype),
            pltpu.VMEM((count, width), jnp.bfloat16),
            pltpu.VMEM((count * tiles, LANES), jnp.float32),
            pltpu.VMEM((count, units), jnp.float32),
            pltpu.VMEM((count, units), jnp.float32),
            pltpu.SemaphoreType.DMA((SLOTS,)),
            pltpu.SemaphoreType.DMA(((width - first) // CHUNK,)),
            pltpu.SemaphoreType.DMA((3,)),
        ],
        compiler_params=pltpu.CompilerParams(vmem_limit_bytes=28 * MIB),
        cost_estimate=cost(4 * width * units, 4 * count * width * units),
    )(
        pieces, in_hbm(gate_codes), in_hbm(gate_scales), in_hbm(up_codes), in_hbm(up_scales), in_hbm(hadamard),
        *[in_vmem(part) for part in held],
    )
    held = []
    first = 0

    for index, bit in enumerate(bits):
        other = swap(send, bit)
        if 1 <= index < 4:
            columns = SPANS[index] * SPAN
            part, sign = pl.pallas_call(
                functools.partial(columns_kernel, first, SPAN, bit),
                out_shape=(pltpu.VMEM((units, columns), jnp.bfloat16), pltpu.VMEM((count, units), jnp.float32)),
                in_specs=[HBM, ANY],
                out_specs=(VMEM, VMEM),
                scratch_shapes=[pltpu.SemaphoreType.DMA((SPANS[index],))],
                compiler_params=pltpu.CompilerParams(vmem_limit_bytes=2 * MIB),
                cost_estimate=cost(2 * units * columns),
            )(in_hbm(down_codes), send)
            held.append(part)
            first += columns
        else:
            sign = signs[early.index(bit)]
        turned = turned * sign + other.astype(jnp.float32)
        send = turned.astype(jnp.bfloat16)

    order = [1] + [bit for bit in bits[1:]]
    spread = [0]
    for bit in reversed(order):
        spread = spread + [mask | bit for mask in spread]
    ahead = max(min((width - first) // SPAN, AHEAD), 1)
    keep, send = pl.pallas_call(
        functools.partial(down_kernel, 1.0 / math.sqrt(total_units), spread, len(held)),
        out_shape=(
            jax.ShapeDtypeStruct((devices // 2, own, tiles, LANES), jnp.float32),
            jax.ShapeDtypeStruct((devices // 2, own, tiles, LANES), jnp.bfloat16),
        ),
        in_specs=[VMEM, HBM] + [VMEM] * len(held),
        out_specs=(VMEM, VMEM),
        scratch_shapes=[
            pltpu.VMEM((count * tiles, LANES), jnp.float32),
            pltpu.VMEM((ahead, units, SPAN), jnp.bfloat16),
            pltpu.SemaphoreType.DMA((ahead,)),
        ],
        compiler_params=pltpu.CompilerParams(vmem_limit_bytes=20 * MIB),
        cost_estimate=cost(width * units, 2 * count * width * units),
    )(turned, in_hbm(down_codes), *[in_vmem(part) for part in held])
    summed = keep + swap(send, order[0]).astype(jnp.float32)
    for bit in order[1:]:
        half = summed.shape[0] // 2
        summed = summed[:half] + swap(summed[half:].astype(jnp.bfloat16), bit).astype(jnp.float32)
    return (summed.reshape(own, width) * down_scales[None, :]).astype(jnp.bfloat16)


def solution(mesh):
    in_specs = (
        P(("groups", "hx"), None),
        P(None, "hx"),
        P(None, "hx"),
        P(None, "hx"),
        P(None, "hx"),
        P("hx", None),
        P(),
        P(),
    )
    out_specs = P(("groups", "hx"), None)
    body = functools.partial(per_device, mesh.shape["hx"])
    return jax.shard_map(body, mesh=mesh, in_specs=in_specs, out_specs=out_specs, check_vma=False)
```

time: 69.1 us -> 65.7 us (0.951)
  blocking collectives: 17.4 us -> 0 us
  starting transfers between devices: 5.6 us -> 15.8 us
  Pallas kernels: 26.9 us -> 35.4 us
  waiting for transfers between devices: 17.2 us -> 13.2 us
  other arithmetic: 1.02 us -> 0.32 us
    all_to_all x1 -> x0, blocking collectives: 17.4 us -> none  [per_device(): lax.all_to_all(pieces, ('groups', 'hx'), split_axis=0, concat_axis=0, til...]
    ppermute x8 -> x12, starting transfers between devices: 4.8 us -> 15.8 us  [swap(): return lax.ppermute(value, 'hx', [(at, at ^ bit) for at in range(devices)])]
    pallas_call x3 -> x4, Pallas kernels: 14.4 us -> 21.7 us  [the longest x1 12.6 us: per_device(): pl.pallas_call(functools.partial(hidden_kernel, group, gathered, early, l...]
    ppermute x8 -> x12, waiting for transfers between devices: 16.3 us -> 13.2 us  [swap(): return lax.ppermute(value, 'hx', [(at, at ^ bit) for at in range(devices)])]
    pallas_call x3, Pallas kernels: 8.63 us -> 11.2 us  [per_device(): pl.pallas_call(functools.partial(columns_kernel, first, SPAN, bit), out_s...]
    pallas_call x1, Pallas kernels: 3.84 us -> 2.41 us  [per_device(): pl.pallas_call(functools.partial(down_kernel, 1.0 / math.sqrt(total_units...]
    unnamed x1 -> x0, other arithmetic: 0.85 us -> none
    ppermute x1 -> x0, waiting for transfers between devices: 0.84 us -> none  [per_device(): lax.ppermute(send[step - 1], 'groups', [(at, (at + step) % parts) for at...]
  transfers between devices with their start and end apart: 9 -> 12, of which waited for: 9 -> 7; matrix products, arithmetic and copies ran while one was open for 0% -> 0% of each run, Pallas kernels for 18% -> 31%
where the time goes in v3:
time: 65.7 us; the launch traced here: 65.6 us
  Pallas kernels  35.4 us (54%)
  starting transfers between devices  15.8 us (24%)
  waiting for transfers between devices  13.2 us (20%)
  local copies, waits for them, and re-layouts  0.68 us (1%)
    ppermute x12, starting transfers between devices, swap(): return lax.ppermute(value, 'hx', [(at, at ^ bit) for at in range(devices)])  15.8 us
    ppermute x12, waiting for transfers between devices, swap(): return lax.ppermute(value, 'hx', [(at, at ^ bit) for at in range(devices)])  13.2 us
    pallas_call x1, Pallas kernels, per_device(): pl.pallas_call(functools.partial(hidden_kernel, group, gathered, early, l...  12.6 us
    pallas_call x3, Pallas kernels, per_device(): pl.pallas_call(functools.partial(columns_kernel, first, SPAN, bit), out_s...  11.2 us
    pallas_call x3, Pallas kernels, per_device(): pl.pallas_call(functools.partial(first_rows_kernel if index == 0 else row...  9.13 us
    pallas_call x1, Pallas kernels, per_device(): pl.pallas_call(functools.partial(down_kernel, 1.0 / math.sqrt(total_units...  2.41 us
  transfers between devices with their start and end apart: 12, of which 7 were waited for; matrix products, arithmetic and copies ran while one was open for 0% of the time, Pallas kernels for 31%

profile of v3, /device:TPU:0, one launch (start us, length us, event | category | flops | bytes accessed | tf_op | source)
XLA Modules:
  0.0 65.6 jit_solution(14432308977247175336)
XLA Ops:
  0.0 4.0 %collective-permute-start = (bf16[1,8192]{1,0:T(2,128)(2,1)}, bf16[1,8192]{1,0:T(2,128)(2,1)S(1)}, u32[]{:S(2)}, u32[]{:S(2)}) collective-permute-start(bf16[1,8192]{1,0:T(2,128)(2,1)} %tokens_ref.1), channel_id=1, source_target_pairs={{0,8},{1,9},{2,10},{3,11},{4,12},{5,13},{6,14},{7,15},{8,0},{9,1},... | collective-permute-start | bytes 49160 | tf_op jit(solution)/shard_map/ppermute | solution.py:271
  4.0 2.0 %shard_map.82 = (bf16[1024,1664]{1,0:T(8,128)(2,1)S(1)}, bf16[1,1,64,128]{3,2,1,0:T(8,128)(2,1)S(1)}) custom-call(bf16[8192,1664]{1,0:T(8,128)(2,1)} %refs_1_.2, bf16[1,8192]{1,0:T(2,128)(2,1)} %tokens_ref.1), custom_call_target="tpu_custom_call" | custom-call | bytes 3407872 | tf_op jit(solution)/shard_map/pallas_call | solution.py:287
  6.1 0.4 collective-permute-done
  6.5 0.1 reduce
  6.6 1.6 %collective-permute-start.1 = (bf16[2,1,64,128]{3,2,1,0:T(8,128)(2,1)S(1)}, bf16[2,1,64,128]{3,2,1,0:T(8,128)(2,1)S(1)}, u32[]{:S(2)}, u32[]{:S(2)}) collective-permute-start(bf16[2,1,64,128]{3,2,1,0:T(8,128)(2,1)S(1)} %pad_maximum_fusion.2.after_ref), channel_id=1, source_target_pairs={{0,4},{1,5},{2,6},{3,7},{4,0},{5,1},{6,2},{7,3},{8,12},{9,13},{10,... | collective-permute-start | bytes 98312 | tf_op jit(solution)/shard_map/ppermute | solution.py:271
  8.2 3.5 %shard_map.83 = (bf16[2560,1664]{1,0:T(8,128)(2,1)S(1)}, bf16[2,1,64,128]{3,2,1,0:T(8,128)(2,1)S(1)}) custom-call(bf16[8192,1664]{1,0:T(8,128)(2,1)} %refs_1_.2, bf16[2,1,64,128]{3,2,1,0:T(8,128)(2,1)S(1)} %pad_maximum_fusion.2.after_ref), custom_call_target="tpu_custom_call" | custom-call | bytes 8519680 | tf_op jit(solution)/shard_map/pallas_call | solution.py:287
  11.8 0.0 collective-permute-done.1
  11.8 1.6 %collective-permute-start.2 = (bf16[4,1,64,128]{3,2,1,0:T(8,128)(2,1)S(1)}, bf16[4,1,64,128]{3,2,1,0:T(8,128)(2,1)S(1)}, u32[]{:S(2)}, u32[]{:S(2)}) collective-permute-start(bf16[4,1,64,128]{3,2,1,0:T(8,128)(2,1)S(1)} %constant_dynamic-update-slice_fusion.after_ref), channel_id=1, source_target_pairs={{0,2},{1,3},{2,0},{3,1},{4,6},{5,7},{6,4},{7,5},{8,10},{9,11},{10,... | collective-permute-start | bytes 196616 | tf_op jit(solution)/shard_map/ppermute | solution.py:271
  13.4 3.6 %shard_map.84 = (bf16[2560,1664]{1,0:T(8,128)(2,1)S(1)}, bf16[4,1,64,128]{3,2,1,0:T(8,128)(2,1)S(1)}) custom-call(bf16[8192,1664]{1,0:T(8,128)(2,1)} %refs_1_.2, bf16[4,1,64,128]{3,2,1,0:T(8,128)(2,1)S(1)} %constant_dynamic-update-slice_fusion.after_ref), custom_call_target="tpu_custom_call" | custom-call | bytes 8519680 | tf_op jit(solution)/shard_map/pallas_call | solution.py:287
  16.9 0.0 collective-permute-done.2
  17.0 0.1 collective-permute-start.3
  17.1 1.3 %collective-permute-done.3 = bf16[8,1,64,128]{3,2,1,0:T(8,128)(2,1)S(1)} collective-permute-done((bf16[8,1,64,128]{3,2,1,0:T(8,128)(2,1)S(1)}, bf16[8,1,64,128]{3,2,1,0:T(8,128)(2,1)S(1)}, u32[]{:S(2)}, u32[]{:S(2)}) %collective-permute-start.3) | collective-permute-done | bytes 131104 | tf_op jit(solution)/shard_map/ppermute | solution.py:271
  18.4 12.6 %shard_map.85 = (f32[16,1664]{1,0:T(8,128)S(1)}, bf16[16,1664]{1,0:T(8,128)(2,1)S(1)}, f32[1,16,1664]{2,1,0:T(8,128)S(1)}) custom-call(bf16[16,1,64,128]{3,2,1,0:T(8,128)(2,1)S(1)} %pad_maximum_fusion.refs_0_, bf16[8192,1664]{1,0:T(8,128)(2,1)} %refs_1_.2, f32[64,1664]{1,0:T(8,128)} %refs_2_.1, bf16[8192,1664]{1,0:T(8,128)(2,1)} %refs_3_.1, ...), custom_call_target="tpu_custom_call" | custom-call | flops 872415232 | bytes 54525952 | tf_op jit(solution)/shard_map/pallas_call | solution.py:307
  31.0 0.2 collective-permute-start.4
  31.2 1.1 %collective-permute-done.4 = bf16[16,1664]{1,0:T(8,128)(2,1)S(1)} collective-permute-done((bf16[16,1664]{1,0:T(8,128)(2,1)S(1)}, bf16[16,1664]{1,0:T(8,128)(2,1)S(1)}, u32[]{:S(2)}, u32[]{:S(2)}) %collective-permute-start.4) | collective-permute-done | bytes 53280 | tf_op jit(solution)/shard_map/ppermute | solution.py:271
  32.4 0.7 %collective-permute-start.5 = (bf16[16,1664]{1,0:T(8,128)(2,1)S(1)}, bf16[16,1664]{1,0:T(8,128)(2,1)S(1)}, u32[]{:S(2)}, u32[]{:S(2)}) collective-permute-start(bf16[16,1664]{1,0:T(8,128)(2,1)S(1)} %get-tuple-element.41.after_ref), channel_id=1, source_target_pairs={{0,2},{1,3},{2,0},{3,1},{4,6},{5,7},{6,4},{7,5},{8,10},{9,11},{10,... | collective-permute-start | bytes 159752 | tf_op jit(solution)/shard_map/ppermute | solution.py:271
  33.1 3.6 %shard_map.86 = (bf16[1664,2560]{1,0:T(8,128)(2,1)S(1)}, f32[16,1664]{1,0:T(8,128)S(1)}) custom-call(bf16[1664,8192]{1,0:T(8,128)(2,1)} %refs_1_.3, bf16[16,1664]{1,0:T(8,128)(2,1)S(1)} %get-tuple-element.41.after_ref), custom_call_target="tpu_custom_call" | custom-call | bytes 8519680 | tf_op jit(solution)/shard_map/pallas_call | solution.py:343
  36.7 0.0 collective-permute-done.5
  36.7 0.7 %collective-permute-start.6 = (bf16[16,1664]{1,0:T(8,128)(2,1)S(1)}, bf16[16,1664]{1,0:T(8,128)(2,1)S(1)}, u32[]{:S(2)}, u32[]{:S(2)}) collective-permute-start(bf16[16,1664]{1,0:T(8,128)(2,1)S(1)} %fusion.4.after_ref), channel_id=1, source_target_pairs={{0,4},{1,5},{2,6},{3,7},{4,0},{5,1},{6,2},{7,3},{8,12},{9,13},{10,... | collective-permute-start | bytes 159752 | tf_op jit(solution)/shard_map/ppermute | solution.py:271
  37.4 3.6 %shard_map.87 = (bf16[1664,2560]{1,0:T(8,128)(2,1)S(1)}, f32[16,1664]{1,0:T(8,128)S(1)}) custom-call(bf16[1664,8192]{1,0:T(8,128)(2,1)} %refs_1_.3, bf16[16,1664]{1,0:T(8,128)(2,1)S(1)} %fusion.4.after_ref), custom_call_target="tpu_custom_call" | custom-call | bytes 8519680 | tf_op jit(solution)/shard_map/pallas_call | solution.py:343
  41.0 0.0 collective-permute-done.6
  41.1 2.8 %collective-permute-start.7 = (bf16[16,1664]{1,0:T(8,128)(2,1)S(1)}, bf16[16,1664]{1,0:T(8,128)(2,1)S(1)}, u32[]{:S(2)}, u32[]{:S(2)}) collective-permute-start(bf16[16,1664]{1,0:T(8,128)(2,1)S(1)} %get-tuple-element.39.after_ref), channel_id=1, source_target_pairs={{0,8},{1,9},{2,10},{3,11},{4,12},{5,13},{6,14},{7,15},{8,0},{9,1},... | collective-permute-start | bytes 159752 | tf_op jit(solution)/shard_map/ppermute | solution.py:271
  43.8 4.1 %shard_map.88 = (bf16[1664,3072]{1,0:T(8,128)(2,1)S(1)}, f32[16,1664]{1,0:T(8,128)S(1)}) custom-call(bf16[1664,8192]{1,0:T(8,128)(2,1)} %refs_1_.3, bf16[16,1664]{1,0:T(8,128)(2,1)S(1)} %get-tuple-element.39.after_ref), custom_call_target="tpu_custom_call" | custom-call | bytes 10223616 | tf_op jit(solution)/shard_map/pallas_call | solution.py:343
  47.9 0.0 collective-permute-done.7
  48.0 0.0 copy-start
  48.0 2.4 %shard_map.89 = (f32[8,1,64,128]{3,2,1,0:T(8,128)S(1)}, bf16[8,1,64,128]{3,2,1,0:T(8,128)(2,1)S(1)}) custom-call(f32[16,1664]{1,0:T(8,128)S(1)} %convert_add_fusion.1.refs_0_, bf16[1664,8192]{1,0:T(8,128)(2,1)} %refs_1_.3, bf16[1664,2560]{1,0:T(8,128)(2,1)S(1)} %get-tuple-element.34.refs_2_, bf16[1664,2560]{1,0:T(8,128)(2,1)S(1)} %get-tuple-element.35.refs_3_, ...), custom_call_target="tpu_custom_call" | custom-call | flops 436207616 | bytes 13631488 | tf_op jit(solution)/shard_map/pallas_call | solution.py:364
  50.4 0.1 collective-permute-start.8
  50.5 1.3 %collective-permute-done.8 = bf16[8,1,64,128]{3,2,1,0:T(8,128)(2,1)S(1)} collective-permute-done((bf16[8,1,64,128]{3,2,1,0:T(8,128)(2,1)S(1)}, bf16[8,1,64,128]{3,2,1,0:T(8,128)(2,1)S(1)}, u32[]{:S(2)}, u32[]{:S(2)}) %collective-permute-start.8) | collective-permute-done | bytes 131104 | tf_op jit(solution)/shard_map/ppermute | solution.py:271
  51.9 1.4 %collective-permute-start.9 = (bf16[4,1,64,128]{3,2,1,0:T(8,128)(2,1)S(1)}, bf16[4,1,64,128]{3,2,1,0:T(8,128)(2,1)S(1)}, u32[]{:S(2)}, u32[]{:S(2)}) collective-permute-start(bf16[4,1,64,128]{3,2,1,0:T(8,128)(2,1)S(1)} %slice.45), channel_id=1, source_target_pairs={{0,2},{1,3},{2,0},{3,1},{4,6},{5,7},{6,4},{7,5},{8,10},{9,11},{10,... | collective-permute-start | bytes 196616 | tf_op jit(solution)/shard_map/ppermute | solution.py:271
  53.3 2.9 %collective-permute-done.9 = bf16[4,1,64,128]{3,2,1,0:T(8,128)(2,1)S(1)} collective-permute-done((bf16[4,1,64,128]{3,2,1,0:T(8,128)(2,1)S(1)}, bf16[4,1,64,128]{3,2,1,0:T(8,128)(2,1)S(1)}, u32[]{:S(2)}, u32[]{:S(2)}) %collective-permute-start.9) | collective-permute-done | bytes 65568 | tf_op jit(solution)/shard_map/ppermute | solution.py:271
  56.2 1.5 %collective-permute-start.10 = (bf16[2,1,64,128]{3,2,1,0:T(8,128)(2,1)S(1)}, bf16[2,1,64,128]{3,2,1,0:T(8,128)(2,1)S(1)}, u32[]{:S(2)}, u32[]{:S(2)}) collective-permute-start(bf16[2,1,64,128]{3,2,1,0:T(8,128)(2,1)S(1)} %slice.46), channel_id=1, source_target_pairs={{0,4},{1,5},{2,6},{3,7},{4,0},{5,1},{6,2},{7,3},{8,12},{9,13},{10,... | collective-permute-start | bytes 98312 | tf_op jit(solution)/shard_map/ppermute | solution.py:271
  57.8 2.4 %collective-permute-done.10 = bf16[2,1,64,128]{3,2,1,0:T(8,128)(2,1)S(1)} collective-permute-done((bf16[2,1,64,128]{3,2,1,0:T(8,128)(2,1)S(1)}, bf16[2,1,64,128]{3,2,1,0:T(8,128)(2,1)S(1)}, u32[]{:S(2)}, u32[]{:S(2)}) %collective-permute-start.10) | collective-permute-done | bytes 32800 | tf_op jit(solution)/shard_map/ppermute | solution.py:271
  60.2 1.1 %collective-permute-start.11 = (bf16[1,1,64,128]{3,2,1,0:T(8,128)(2,1)S(1)}, bf16[1,1,64,128]{3,2,1,0:T(8,128)(2,1)S(1)}, u32[]{:S(2)}, u32[]{:S(2)}) collective-permute-start(bf16[1,1,64,128]{3,2,1,0:T(8,128)(2,1)S(1)} %slice.47), channel_id=1, source_target_pairs={{0,8},{1,9},{2,10},{3,11},{4,12},{5,13},{6,14},{7,15},{8,0},{9,1},... | collective-permute-start | bytes 49160 | tf_op jit(solution)/shard_map/ppermute | solution.py:271
  61.3 3.7 %collective-permute-done.11 = bf16[1,1,64,128]{3,2,1,0:T(8,128)(2,1)S(1)} collective-permute-done((bf16[1,1,64,128]{3,2,1,0:T(8,128)(2,1)S(1)}, bf16[1,1,64,128]{3,2,1,0:T(8,128)(2,1)S(1)}, u32[]{:S(2)}, u32[]{:S(2)}) %collective-permute-start.11) | collective-permute-done | bytes 16416 | tf_op jit(solution)/shard_map/ppermute | solution.py:271
  64.9 0.0 copy-done
  64.9 0.6 convert_element_type.54
  (16 shorter events, 0.3 us)
Async XLA Ops:
  0.0 6.5 %collective-permute-start = (bf16[1,8192]{1,0:T(2,128)(2,1)}, bf16[1,8192]{1,0:T(2,128)(2,1)S(1)}, u32[]{:S(2)}, u32[]{:S(2)}) collective-permute-start(bf16[1,8192]{1,0:T(2,128)(2,1)} %tokens_ref.1), channel_id=1, source_target_pairs={{0,8},{1,9},{2,10},{3,11},{4,12},{5,13},{6,14},{7,15},{8,0},{9,1},... | collective-permute-start | bytes 49160 | tf_op jit(solution)/shard_map/ppermute | solution.py:271
  6.6 5.2 %collective-permute-start.1 = (bf16[2,1,64,128]{3,2,1,0:T(8,128)(2,1)S(1)}, bf16[2,1,64,128]{3,2,1,0:T(8,128)(2,1)S(1)}, u32[]{:S(2)}, u32[]{:S(2)}) collective-permute-start(bf16[2,1,64,128]{3,2,1,0:T(8,128)(2,1)S(1)} %pad_maximum_fusion.2.after_ref), channel_id=1, source_target_pairs={{0,4},{1,5},{2,6},{3,7},{4,0},{5,1},{6,2},{7,3},{8,12},{9,13},{10,... | collective-permute-start | bytes 98312 | tf_op jit(solution)/shard_map/ppermute | solution.py:271
  11.8 5.1 %collective-permute-start.2 = (bf16[4,1,64,128]{3,2,1,0:T(8,128)(2,1)S(1)}, bf16[4,1,64,128]{3,2,1,0:T(8,128)(2,1)S(1)}, u32[]{:S(2)}, u32[]{:S(2)}) collective-permute-start(bf16[4,1,64,128]{3,2,1,0:T(8,128)(2,1)S(1)} %constant_dynamic-update-slice_fusion.after_ref), channel_id=1, source_target_pairs={{0,2},{1,3},{2,0},{3,1},{4,6},{5,7},{6,4},{7,5},{8,10},{9,11},{10,... | collective-permute-start | bytes 196616 | tf_op jit(solution)/shard_map/ppermute | solution.py:271
  17.0 1.4 %collective-permute-start.3 = (bf16[8,1,64,128]{3,2,1,0:T(8,128)(2,1)S(1)}, bf16[8,1,64,128]{3,2,1,0:T(8,128)(2,1)S(1)}, u32[]{:S(2)}, u32[]{:S(2)}) collective-permute-start(bf16[8,1,64,128]{3,2,1,0:T(8,128)(2,1)S(1)} %pad_maximum_fusion.1), channel_id=1, source_target_pairs={{0,1},{1,0},{2,3},{3,2},{4,5},{5,4},{6,7},{7,6},{8,9},{9,8},{10,11... | collective-permute-start | bytes 393224 | tf_op jit(solution)/shard_map/ppermute | solution.py:271
  31.0 1.3 %collective-permute-start.4 = (bf16[16,1664]{1,0:T(8,128)(2,1)S(1)}, bf16[16,1664]{1,0:T(8,128)(2,1)S(1)}, u32[]{:S(2)}, u32[]{:S(2)}) collective-permute-start(bf16[16,1664]{1,0:T(8,128)(2,1)S(1)} %get-tuple-element.30), channel_id=1, source_target_pairs={{0,1},{1,0},{2,3},{3,2},{4,5},{5,4},{6,7},{7,6},{8,9},{9,8},{10,11... | collective-permute-start | bytes 159752 | tf_op jit(solution)/shard_map/ppermute | solution.py:271
  32.4 4.3 %collective-permute-start.5 = (bf16[16,1664]{1,0:T(8,128)(2,1)S(1)}, bf16[16,1664]{1,0:T(8,128)(2,1)S(1)}, u32[]{:S(2)}, u32[]{:S(2)}) collective-permute-start(bf16[16,1664]{1,0:T(8,128)(2,1)S(1)} %get-tuple-element.41.after_ref), channel_id=1, source_target_pairs={{0,2},{1,3},{2,0},{3,1},{4,6},{5,7},{6,4},{7,5},{8,10},{9,11},{10,... | collective-permute-start | bytes 159752 | tf_op jit(solution)/shard_map/ppermute | solution.py:271
  36.7 4.3 %collective-permute-start.6 = (bf16[16,1664]{1,0:T(8,128)(2,1)S(1)}, bf16[16,1664]{1,0:T(8,128)(2,1)S(1)}, u32[]{:S(2)}, u32[]{:S(2)}) collective-permute-start(bf16[16,1664]{1,0:T(8,128)(2,1)S(1)} %fusion.4.after_ref), channel_id=1, source_target_pairs={{0,4},{1,5},{2,6},{3,7},{4,0},{5,1},{6,2},{7,3},{8,12},{9,13},{10,... | collective-permute-start | bytes 159752 | tf_op jit(solution)/shard_map/ppermute | solution.py:271
  41.1 6.8 %collective-permute-start.7 = (bf16[16,1664]{1,0:T(8,128)(2,1)S(1)}, bf16[16,1664]{1,0:T(8,128)(2,1)S(1)}, u32[]{:S(2)}, u32[]{:S(2)}) collective-permute-start(bf16[16,1664]{1,0:T(8,128)(2,1)S(1)} %get-tuple-element.39.after_ref), channel_id=1, source_target_pairs={{0,8},{1,9},{2,10},{3,11},{4,12},{5,13},{6,14},{7,15},{8,0},{9,1},... | collective-permute-start | bytes 159752 | tf_op jit(solution)/shard_map/ppermute | solution.py:271
  48.0 17.0 %copy-start = (f32[8192]{0:T(1024)S(1)}, f32[8192]{0:T(1024)}, u32[]{:S(2)}) copy-start(f32[8192]{0:T(1024)} %param.14) | copy-start | bytes 98308
  50.4 1.4 %collective-permute-start.8 = (bf16[8,1,64,128]{3,2,1,0:T(8,128)(2,1)S(1)}, bf16[8,1,64,128]{3,2,1,0:T(8,128)(2,1)S(1)}, u32[]{:S(2)}, u32[]{:S(2)}) collective-permute-start(bf16[8,1,64,128]{3,2,1,0:T(8,128)(2,1)S(1)} %get-tuple-element.38), channel_id=1, source_target_pairs={{0,1},{1,0},{2,3},{3,2},{4,5},{5,4},{6,7},{7,6},{8,9},{9,8},{10,11... | collective-permute-start | bytes 393224 | tf_op jit(solution)/shard_map/ppermute | solution.py:271
  51.9 4.3 %collective-permute-start.9 = (bf16[4,1,64,128]{3,2,1,0:T(8,128)(2,1)S(1)}, bf16[4,1,64,128]{3,2,1,0:T(8,128)(2,1)S(1)}, u32[]{:S(2)}, u32[]{:S(2)}) collective-permute-start(bf16[4,1,64,128]{3,2,1,0:T(8,128)(2,1)S(1)} %slice.45), channel_id=1, source_target_pairs={{0,2},{1,3},{2,0},{3,1},{4,6},{5,7},{6,4},{7,5},{8,10},{9,11},{10,... | collective-permute-start | bytes 196616 | tf_op jit(solution)/shard_map/ppermute | solution.py:271
  56.2 4.0 %collective-permute-start.10 = (bf16[2,1,64,128]{3,2,1,0:T(8,128)(2,1)S(1)}, bf16[2,1,64,128]{3,2,1,0:T(8,128)(2,1)S(1)}, u32[]{:S(2)}, u32[]{:S(2)}) collective-permute-start(bf16[2,1,64,128]{3,2,1,0:T(8,128)(2,1)S(1)} %slice.46), channel_id=1, source_target_pairs={{0,4},{1,5},{2,6},{3,7},{4,0},{5,1},{6,2},{7,3},{8,12},{9,13},{10,... | collective-permute-start | bytes 98312 | tf_op jit(solution)/shard_map/ppermute | solution.py:271
  60.2 4.7 %collective-permute-start.11 = (bf16[1,1,64,128]{3,2,1,0:T(8,128)(2,1)S(1)}, bf16[1,1,64,128]{3,2,1,0:T(8,128)(2,1)S(1)}, u32[]{:S(2)}, u32[]{:S(2)}) collective-permute-start(bf16[1,1,64,128]{3,2,1,0:T(8,128)(2,1)S(1)} %slice.47), channel_id=1, source_target_pairs={{0,8},{1,9},{2,10},{3,11},{4,12},{5,13},{6,14},{7,15},{8,0},{9,1},... | collective-permute-start | bytes 49160 | tf_op jit(solution)/shard_map/ppermute | solution.py:271

commit v4 on v3

--- a/solution.py
+++ b/solution.py
@@ -14,10 +14,10 @@
 CHUNK = 512
 SLOTS = 5
 UNROLL = 2
-ROWS = (2, 5, 5)
+ROWS = (2, 2, 2, 2)
 SPAN = 512
 AHEAD = 8
-SPANS = (0, 5, 5, 6)
+SPANS = (5, 3, 3, 5)
 
 VMEM = pl.BlockSpec(memory_space=pltpu.VMEM)
 HBM = pl.BlockSpec(memory_space=pltpu.HBM)
@@ -54,8 +54,10 @@
         copy.wait()
 
 
-def rows_kernel(first, step, codes_ref, after_ref, out_ref, same_ref, sems):
+def rows_kernel(before, step, codes_ref, after_ref, out_ref, same_ref, sems):
     copies = [fetch(after_ref, same_ref, sems.at[out_ref.shape[0] // step])]
+    share = codes_ref.shape[0] // lax.axis_size("groups")
+    first = pl.multiple_of(lax.axis_index("groups") * share + before, step)
     for index in range(out_ref.shape[0] // step):
         here = codes_ref.at[pl.ds(first + index * step, step), :]
         copies.append(fetch(here, out_ref.at[pl.ds(index * step, step), :], sems.at[index]))
@@ -63,21 +65,23 @@
         copy.wait()
 
 
-def first_rows_kernel(first, step, codes_ref, tokens_ref, out_ref, tiled_ref, token_ref, wide_ref, sems):
-    _, own, tiles, lanes = tiled_ref.shape
-    token = fetch(tokens_ref, token_ref, sems.at[out_ref.shape[0] // step])
-    copies = []
-    for index in range(out_ref.shape[0] // step):
-        here = codes_ref.at[pl.ds(first + index * step, step), :]
-        copies.append(fetch(here, out_ref.at[pl.ds(index * step, step), :], sems.at[index]))
-    token.wait()
-    for at in range(own):
-        row = token_ref[at : at + 1, :].astype(jnp.float32)
-        for tile in range(tiles):
-            wide_ref[tile : tile + 1, :] = row[:, tile * lanes : (tile + 1) * lanes]
-        tiled_ref[0, at] = wide_ref[...].astype(tiled_ref.dtype)
+def columns_small_kernel(first, step, codes_ref, after_ref, hadamard_ref, out_ref, small_ref, sems):
+    copies = [fetch(hadamard_ref, small_ref, sems.at[out_ref.shape[1] // step])]
+    copies += fetch_columns(first, step, codes_ref, out_ref, sems)
     for copy in copies:
         copy.wait()
+
+
+def tiles_kernel(mine_ref, *refs):
+    others, out_ref, wide_ref = refs[:-2], refs[-2], refs[-1]
+    _, own, tiles, lanes = out_ref.shape
+    first = pl.multiple_of(lax.axis_index("groups") * (tiles * lanes), tiles * lanes)
+    for index, token_ref in enumerate((mine_ref,) + others):
+        for at in range(own):
+            row = token_ref[at : at + 1, pl.ds(first, tiles * lanes)].astype(jnp.float32)
+            for tile in range(tiles):
+                wide_ref[tile : tile + 1, :] = row[:, tile * lanes : (tile + 1) * lanes]
+            out_ref[index, at] = wide_ref[...].astype(out_ref.dtype)
 
 
 def rotate(gate, up, hadamard):
@@ -102,50 +106,56 @@
     return jnp.concatenate(blocks, axis=1)
 
 
-def hidden_kernel(group, masks, bits, parts, *refs):
-    pieces_ref, gate_codes_ref, gate_scales_ref, up_codes_ref, up_scales_ref, hadamard_ref = refs[:6]
-    held = refs[6 : 6 + parts]
-    out_ref, send_ref, signs_ref, buffers, late, gate_rows, up_rows, small_ref, tokens_ref, wide_ref = refs[6 + parts : 16 + parts]
-    gate_sum, up_sum, sems, late_sems, small_sems = refs[16 + parts :]
+def rotate_kernel(gate_ref, up_ref, hadamard_ref, *refs):
+    others, out_ref, send_ref = refs[:-2], refs[-2], refs[-1]
+    gate = gate_ref[...]
+    up = up_ref[...]
+    for other in others:
+        gate = gate + other[0].astype(jnp.float32)
+        up = up + other[1].astype(jnp.float32)
+    turned = rotate(gate, up, hadamard_ref[...])
+    out_ref[...] = turned
+    send_ref[...] = turned.astype(send_ref.dtype)
+
+
+def hidden_kernel(group, parts, masks, bits, *refs):
+    pieces_ref, gate_scales_ref, up_codes_ref, up_scales_ref = refs[:4]
+    held = refs[4:-12]
+    gate_ref, up_ref, send_ref, signs_ref, buffers, gate_rows, up_rows, tokens_ref, wide_ref, gate_sum, up_sum, sems = refs[-12:]
     depth, rows, units = buffers.shape
-    devices, own, tiles, lanes = pieces_ref.shape
-    count = devices * own
-    steps = up_codes_ref.shape[0] // rows
-    ready = sum(part.shape[0] for part in held) // rows
-    late_steps = steps - ready
+    slots, own, tiles, lanes = pieces_ref.shape
+    count = slots // parts * own
+    share = tiles * lanes
+    steps = share // rows
+    mine = lax.axis_index("groups")
 
     def copy(step):
         slot = lax.rem(step, depth)
-        first = pl.multiple_of(step * rows, rows)
+        first = pl.multiple_of(mine * share + step * rows, rows)
         return pltpu.make_async_copy(up_codes_ref.at[pl.ds(first, rows), :], buffers.at[slot], sems.at[slot])
 
-    def late_copy(index):
-        source = gate_codes_ref.at[pl.ds(pl.multiple_of((ready + index) * rows, rows), rows), :]
-        target = late.at[pl.ds(pl.multiple_of(index * rows, rows), rows), :]
-        return pltpu.make_async_copy(source, target, late_sems.at[index])
-
-    copy(0).start()
+    first = pl.multiple_of(mine * (share // group), share // group)
     small_copies = [
-        fetch(up_scales_ref, up_rows, small_sems.at[1]),
-        fetch(gate_scales_ref, gate_rows, small_sems.at[0]),
-        fetch(hadamard_ref, small_ref, small_sems.at[2]),
+        fetch(gate_scales_ref.at[pl.ds(first, share // group), :], gate_rows, sems.at[depth]),
+        fetch(up_scales_ref.at[pl.ds(first, share // group), :], up_rows, sems.at[depth + 1]),
     ]
-    for step in range(1, min(depth, steps)):
+    for step in range(min(depth, steps)):
         copy(step).start()
     me = lax.axis_index("hx")
     for index, bit in enumerate(bits):
         sign = 1.0 - 2.0 * ((me // bit) % 2).astype(jnp.float32)
         signs_ref[index] = jnp.full((count, units), sign, jnp.float32)
     for slot, mask in enumerate(masks):
-        for at in range(own):
-            where = pl.multiple_of(((me ^ mask) * own + at) * tiles, tiles)
-            wide_ref[pl.ds(where, tiles), :] = pieces_ref[slot, at].astype(jnp.float32)
+        for part in range(parts):
+            for at in range(own):
+                where = pl.multiple_of((part * count + (me ^ mask) * own + at) * tiles, tiles)
+                wide_ref[pl.ds(where, tiles), :] = pieces_ref[slot * parts + part, at].astype(jnp.float32)
     for tile in range(tiles):
-        here = wide_ref[pl.ds(tile, count, stride=tiles), :]
+        here = wide_ref[pl.ds(tile, parts * count, stride=tiles), :]
         tokens_ref[:, tile * lanes : (tile + 1) * lanes] = here.astype(jnp.bfloat16)
     gate_sum[...] = jnp.zeros_like(gate_sum)
     up_sum[...] = jnp.zeros_like(up_sum)
-    low_half = lax.broadcasted_iota(jnp.int32, (count, 2 * group), 1) < group
+    low_half = lax.broadcasted_iota(jnp.int32, (parts * count, 2 * group), 1) < group
     for small_copy in small_copies:
         small_copy.wait()
 
@@ -157,28 +167,23 @@
             stacked = jnp.concatenate([jnp.where(low_half, two, none), jnp.where(low_half, none, two)], axis=0)
             sums = jnp.dot(stacked, codes(pair * 2 * group).astype(F8), preferred_element_type=jnp.float32)
             total_ref[...] += (
-                sums[:count] * scales_ref[pl.ds(2 * index, 1), :] + sums[count:] * scales_ref[pl.ds(2 * index + 1, 1), :]
+                sums[: parts * count] * scales_ref[pl.ds(2 * index, 1), :]
+                + sums[parts * count :] * scales_ref[pl.ds(2 * index + 1, 1), :]
             )
 
-    def loop(begin, end, source, base, waits):
-        def body(step, carry):
+    before = 0
+    for part in held:
+
+        def body(step, carry, part=part, before=before):
             slot = lax.rem(step, depth)
 
-            def in_source(first):
-                return source[pl.ds(pl.multiple_of((step - base) * rows + first, 2 * group), 2 * group), :]
+            def in_part(first):
+                return part[pl.ds(pl.multiple_of((step - before) * rows + first, 2 * group), 2 * group), :]
 
             def in_buffer(first):
                 return buffers[slot, first : first + 2 * group, :]
 
-            if not waits:
-
-                @pl.when((lax.rem(step, 2) == 0) & (step // 2 < late_steps))
-                def _():
-                    late_copy(step // 2).start()
-
-            else:
-                late_copy(step - ready).wait()
-            add(gate_sum, gate_rows, step, in_source)
+            add(gate_sum, gate_rows, step, in_part)
             copy(step).wait()
             add(up_sum, up_rows, step, in_buffer)
 
@@ -188,19 +193,14 @@
 
             return carry
 
-        lax.fori_loop(begin, end, body, 0, unroll=UNROLL)
-
-    before = 0
-    for part in held:
-        here = part.shape[0] // rows
-        loop(before, before + here, part, before, False)
-        before += here
-    for index in range((ready + 1) // 2, late_steps):
-        late_copy(index).start()
-    loop(ready, steps, late, ready, True)
-    turned = rotate(gate_sum[...], up_sum[...], small_ref[...])
-    out_ref[...] = turned
-    send_ref[...] = turned.astype(send_ref.dtype)
+        lax.fori_loop(before, before + part.shape[0] // rows, body, 0, unroll=UNROLL)
+        before += part.shape[0] // rows
+    gate_ref[...] = gate_sum[:count, :]
+    up_ref[...] = up_sum[:count, :]
+    for part in range(1, parts):
+        span = slice(part * count, (part + 1) * count)
+        send_ref[part - 1, 0] = gate_sum[span, :].astype(send_ref.dtype)
+        send_ref[part - 1, 1] = up_sum[span, :].astype(send_ref.dtype)
 
 
 def down_kernel(scale, masks, parts, *refs):
@@ -257,7 +257,7 @@
 
 
 def per_device(
-    devices, tokens, gate_codes, gate_scales, up_codes, up_scales, down_codes, down_scales, hadamard
+    parts, devices, tokens, gate_codes, gate_scales, up_codes, up_scales, down_codes, down_scales, hadamard
 ):
     width, units = gate_codes.shape
     group = width // gate_scales.shape[0]
@@ -273,68 +273,94 @@
     def cost(nbytes, flops=0):
         return pl.CostEstimate(flops=flops, bytes_accessed=nbytes, transcendentals=0)
 
-    pieces = tokens
+    share = width // parts
+    tiles_here = tiles // parts
+
+    def by_part(value, step):
+        return lax.ppermute(value, "groups", [(at, (at + step) % parts) for at in range(parts)])
+
+    def some_rows(index, first, after, in_space):
+        rows = ROWS[index] * CHUNK
+        return pl.pallas_call(
+            functools.partial(rows_kernel, first, CHUNK),
+            out_shape=(pltpu.VMEM((rows, units), jnp.bfloat16), pltpu.VMEM(after.shape, after.dtype)),
+            in_specs=[HBM, in_space],
+            out_specs=(VMEM, VMEM),
+            scratch_shapes=[pltpu.SemaphoreType.DMA((ROWS[index] + 1,))],
+            compiler_params=pltpu.CompilerParams(vmem_limit_bytes=2 * MIB),
+            cost_estimate=cost(2 * rows * units),
+        )(in_hbm(gate_codes), after)
+
+    others = [by_part(tokens, step) for step in range(1, parts)]
+    part, mine = some_rows(0, 0, in_hbm(tokens), HBM)
+    held = [part]
+    first = part.shape[0]
+    pieces = pl.pallas_call(
+        tiles_kernel,
+        out_shape=jax.ShapeDtypeStruct((parts, own, tiles_here, LANES), tokens.dtype),
+        in_specs=[VMEM] * parts,
+        out_specs=VMEM,
+        scratch_shapes=[pltpu.VMEM((tiles_here, LANES), jnp.float32)],
+        compiler_params=pltpu.CompilerParams(vmem_limit_bytes=2 * MIB),
+        cost_estimate=cost(4 * own * width),
+    )(in_vmem(mine), *others)
     gathered = [0]
-    held = []
-    first = 0
     for index, bit in enumerate(reversed(bits)):
         other = swap(pieces, bit)
-        if index < len(ROWS):
-            rows = ROWS[index] * CHUNK
-            scratch = [pltpu.SemaphoreType.DMA((ROWS[index] + 1,))]
-            if index == 0:
-                scratch = [pltpu.VMEM((own, width), tokens.dtype), pltpu.VMEM((tiles, LANES), jnp.float32)] + scratch
-            part, pieces = pl.pallas_call(
-                functools.partial(first_rows_kernel if index == 0 else rows_kernel, first, CHUNK),
-                out_shape=(
-                    pltpu.VMEM((rows, units), jnp.bfloat16),
-                    pltpu.VMEM((1 << index, own, tiles, LANES), tokens.dtype),
-                ),
-                in_specs=[HBM, HBM if index == 0 else ANY],
-                out_specs=(VMEM, VMEM),
-                scratch_shapes=scratch,
-                compiler_params=pltpu.CompilerParams(vmem_limit_bytes=2 * MIB),
-                cost_estimate=cost(2 * rows * units),
-            )(in_hbm(gate_codes), in_hbm(pieces) if index == 0 else pieces)
+        if index + 1 < len(ROWS):
+            part, pieces = some_rows(index + 1, first, pieces, ANY)
             held.append(part)
-            first += rows
-        if index == 0:
-            other = other.reshape(1, own, tiles, LANES)
+            first += part.shape[0]
         pieces = jnp.concatenate([pieces, other], axis=0)
         gathered = gathered + [mask | bit for mask in gathered]
 
     early = [bit for index, bit in enumerate(bits) if not 1 <= index < 4]
-    turned, send, signs = pl.pallas_call(
-        functools.partial(hidden_kernel, group, gathered, early, len(held)),
+    gate, up, send, signs = pl.pallas_call(
+        functools.partial(hidden_kernel, group, parts, gathered, early),
         out_shape=(
             pltpu.VMEM((count, units), jnp.float32),
-            jax.ShapeDtypeStruct((count, units), jnp.bfloat16),
+            pltpu.VMEM((count, units), jnp.float32),
+            pltpu.VMEM((parts - 1, 2, count, units), jnp.bfloat16),
             pltpu.VMEM((len(early), count, units), jnp.float32),
         ),
-        in_specs=[VMEM, HBM, HBM, HBM, HBM, HBM] + [VMEM] * len(held),
-        out_specs=(VMEM, VMEM, VMEM),
+        in_specs=[VMEM, HBM, HBM, HBM] + [VMEM] * len(held),
+        out_specs=(VMEM, VMEM, VMEM, VMEM),
         scratch_shapes=[
             pltpu.VMEM((SLOTS, CHUNK, units), jnp.bfloat16),
-            pltpu.VMEM((width - first, units), jnp.bfloat16),
-            pltpu.VMEM(gate_scales.shape, gate_scales.dtype),
-            pltpu.VMEM(up_scales.shape, up_scales.dtype),
-            pltpu.VMEM(hadamard.shape, hadamard.dtype),
-            pltpu.VMEM((count, width), jnp.bfloat16),
-            pltpu.VMEM((count * tiles, LANES), jnp.float32),
-            pltpu.VMEM((count, units), jnp.float32),
-            pltpu.VMEM((count, units), jnp.float32),
-            pltpu.SemaphoreType.DMA((SLOTS,)),
-            pltpu.SemaphoreType.DMA(((width - first) // CHUNK,)),
-            pltpu.SemaphoreType.DMA((3,)),
+            pltpu.VMEM((share // group, units), jnp.float32),
+            pltpu.VMEM((share // group, units), jnp.float32),
+            pltpu.VMEM((parts * count, share), jnp.bfloat16),
+            pltpu.VMEM((parts * count * tiles_here, LANES), jnp.float32),
+            pltpu.VMEM((parts * count, units), jnp.float32),
+            pltpu.VMEM((parts * count, units), jnp.float32),
+            pltpu.SemaphoreType.DMA((SLOTS + 2,)),
         ],
-        compiler_params=pltpu.CompilerParams(vmem_limit_bytes=28 * MIB),
-        cost_estimate=cost(4 * width * units, 4 * count * width * units),
-    )(
-        pieces, in_hbm(gate_codes), in_hbm(gate_scales), in_hbm(up_codes), in_hbm(up_scales), in_hbm(hadamard),
-        *[in_vmem(part) for part in held],
-    )
-    held = []
-    first = 0
+        compiler_params=pltpu.CompilerParams(vmem_limit_bytes=24 * MIB),
+        cost_estimate=cost(2 * share * units, 4 * count * width * units),
+    )(pieces, in_hbm(gate_scales), in_hbm(up_codes), in_hbm(up_scales), *[in_vmem(part) for part in held])
+
+    others = [by_part(send[step - 1], -step) for step in range(1, parts)]
+    columns = SPANS[0] * SPAN
+    part, small = pl.pallas_call(
+        functools.partial(columns_small_kernel, 0, SPAN),
+        out_shape=(pltpu.VMEM((units, columns), jnp.bfloat16), pltpu.VMEM(hadamard.shape, hadamard.dtype)),
+        in_specs=[HBM, ANY, HBM],
+        out_specs=(VMEM, VMEM),
+        scratch_shapes=[pltpu.SemaphoreType.DMA((SPANS[0] + 1,))],
+        compiler_params=pltpu.CompilerParams(vmem_limit_bytes=2 * MIB),
+        cost_estimate=cost(2 * units * columns),
+    )(in_hbm(down_codes), send, in_hbm(hadamard))
+    held = [part]
+    first = columns
+
+    turned, send = pl.pallas_call(
+        rotate_kernel,
+        out_shape=(pltpu.VMEM((count, units), jnp.float32), jax.ShapeDtypeStruct((count, units), jnp.bfloat16)),
+        in_specs=[VMEM] * (2 + parts),
+        out_specs=(VMEM, VMEM),
+        compiler_params=pltpu.CompilerParams(vmem_limit_bytes=8 * MIB),
+        cost_estimate=cost(16 * count * units),
+    )(in_vmem(gate), in_vmem(up), in_vmem(small), *others)
 
     for index, bit in enumerate(bits):
         other = swap(send, bit)
@@ -396,5 +422,5 @@
         P(),
     )
     out_specs = P(("groups", "hx"), None)
-    body = functools.partial(per_device, mesh.shape["hx"])
+    body = functools.partial(per_device, mesh.shape["groups"], mesh.shape["hx"])
     return jax.shard_map(body, mesh=mesh, in_specs=in_specs, out_specs=out_specs, check_vma=False)

time: 65.7 us -> 65.4 us (level)
  Pallas kernels: 35.4 us -> 29.1 us
  starting transfers between devices: 15.8 us -> 21.7 us
    ppermute x0 -> x2, starting transfers between devices: none -> 4.55 us  [by_part(): lax.ppermute(value, 'groups', [(at, (at + step) % parts) for at in range(...]
    pallas_call x4 -> x8, Pallas kernels: 21.7 us -> 17.9 us  [the longest x4 8.07 us: some_rows(): pl.pallas_call(functools.partial(rows_kernel, first, CHUNK), out_shape=(p...]
    pallas_call x3, Pallas kernels: 11.2 us -> 8.63 us  [per_device(): pl.pallas_call(functools.partial(columns_kernel, first, SPAN, bit), out_s...]
    ppermute x12, starting transfers between devices: 15.8 us -> 17.1 us  [swap(): return lax.ppermute(value, 'hx', [(at, at ^ bit) for at in range(devices)])]
  transfers between devices with their start and end apart: 12 -> 14, of which waited for: 7 -> 10; matrix products, arithmetic and copies ran while one was open for 0% -> 0% of each run, Pallas kernels for 31% -> 31%
where the time goes in v4:
time: 65.4 us; the launch traced here: 65.3 us
  Pallas kernels  29.1 us (44%)
  starting transfers between devices  21.7 us (33%)
  waiting for transfers between devices  13.4 us (20%)
  local copies, waits for them, and re-layouts  0.69 us (1%)
    ppermute x12, starting transfers between devices, swap(): return lax.ppermute(value, 'hx', [(at, at ^ bit) for at in range(devices)])  17.1 us
    ppermute x12, waiting for transfers between devices, swap(): return lax.ppermute(value, 'hx', [(at, at ^ bit) for at in range(devices)])  13.3 us
    pallas_call x3, Pallas kernels, per_device(): pl.pallas_call(functools.partial(columns_kernel, first, SPAN, bit), out_s...  8.63 us
    pallas_call x4, Pallas kernels, some_rows(): pl.pallas_call(functools.partial(rows_kernel, first, CHUNK), out_shape=(p...  8.07 us
    pallas_call x1, Pallas kernels, per_device(): pl.pallas_call(functools.partial(hidden_kernel, group, parts, gathered, e...  5.76 us
    ppermute x2, starting transfers between devices, by_part(): lax.ppermute(value, 'groups', [(at, (at + step) % parts) for at in range(...  4.55 us
    pallas_call x1, Pallas kernels, per_device(): pl.pallas_call(functools.partial(columns_small_kernel, 0, SPAN), out_shap...  3.59 us
    pallas_call x1, Pallas kernels, per_device(): pl.pallas_call(functools.partial(down_kernel, 1.0 / math.sqrt(total_units...  2.56 us
  transfers between devices with their start and end apart: 14, of which 10 were waited for; matrix products, arithmetic and copies ran while one was open for 0% of the time, Pallas kernels for 31%

profile of v4, /device:TPU:0, one launch (start us, length us, event | category | flops | bytes accessed | tf_op | source)
XLA Modules:
  0.0 65.3 jit_solution(10751096710532945675)
XLA Ops:
  0.0 3.0 %collective-permute-start = (bf16[1,8192]{1,0:T(2,128)(2,1)}, bf16[1,8192]{1,0:T(2,128)(2,1)S(1)}, u32[]{:S(2)}, u32[]{:S(2)}) collective-permute-start(bf16[1,8192]{1,0:T(2,128)(2,1)} %after_ref.1), channel_id=1, source_target_pairs={{0,16},{16,0},{1,17},{17,1},{2,18},{18,2},{3,19},{19,3},{4,20},{20... | collective-permute-start | bytes 49160 | tf_op jit(solution)/shard_map/ppermute | solution.py:280
  3.0 2.0 %shard_map.82 = (bf16[1024,1664]{1,0:T(8,128)(2,1)S(1)}, bf16[1,8192]{1,0:T(2,128)(2,1)S(1)}) custom-call(bf16[8192,1664]{1,0:T(8,128)(2,1)} %codes_ref.11, bf16[1,8192]{1,0:T(2,128)(2,1)} %after_ref.1), custom_call_target="tpu_custom_call" | custom-call | bytes 3407872 | tf_op jit(solution)/shard_map/pallas_call | solution.py:284
  5.0 0.1 collective-permute-done.refs_0_
  5.1 3.2 %collective-permute-start.1 = (bf16[2,1,32,128]{3,2,1,0:T(8,128)(2,1)S(1)}, bf16[2,1,32,128]{3,2,1,0:T(8,128)(2,1)S(1)}, u32[]{:S(2)}, u32[]{:S(2)}) collective-permute-start(bf16[2,1,32,128]{3,2,1,0:T(8,128)(2,1)S(1)} %shard_map.83.after_ref), channel_id=1, source_target_pairs={{0,8},{1,9},{2,10},{3,11},{4,12},{5,13},{6,14},{7,15},{8,0},{9,1},... | collective-permute-start | bytes 49160 | tf_op jit(solution)/shard_map/ppermute | solution.py:271
  8.3 2.0 %shard_map.84 = (bf16[1024,1664]{1,0:T(8,128)(2,1)S(1)}, bf16[2,1,32,128]{3,2,1,0:T(8,128)(2,1)S(1)}) custom-call(bf16[8192,1664]{1,0:T(8,128)(2,1)} %codes_ref.11, bf16[2,1,32,128]{3,2,1,0:T(8,128)(2,1)S(1)} %shard_map.83.after_ref), custom_call_target="tpu_custom_call" | custom-call | bytes 3407872 | tf_op jit(solution)/shard_map/pallas_call | solution.py:284
  10.3 0.0 collective-permute-done.1
  10.3 1.6 %collective-permute-start.2 = (bf16[4,1,32,128]{3,2,1,0:T(8,128)(2,1)S(1)}, bf16[4,1,32,128]{3,2,1,0:T(8,128)(2,1)S(1)}, u32[]{:S(2)}, u32[]{:S(2)}) collective-permute-start(bf16[4,1,32,128]{3,2,1,0:T(8,128)(2,1)S(1)} %constant_dynamic-update-slice_fusion.after_ref), channel_id=1, source_target_pairs={{0,4},{1,5},{2,6},{3,7},{4,0},{5,1},{6,2},{7,3},{8,12},{9,13},{10,... | collective-permute-start | bytes 98312 | tf_op jit(solution)/shard_map/ppermute | solution.py:271
  11.9 2.0 %shard_map.85 = (bf16[1024,1664]{1,0:T(8,128)(2,1)S(1)}, bf16[4,1,32,128]{3,2,1,0:T(8,128)(2,1)S(1)}) custom-call(bf16[8192,1664]{1,0:T(8,128)(2,1)} %codes_ref.11, bf16[4,1,32,128]{3,2,1,0:T(8,128)(2,1)S(1)} %constant_dynamic-update-slice_fusion.after_ref), custom_call_target="tpu_custom_call" | custom-call | bytes 3407872 | tf_op jit(solution)/shard_map/pallas_call | solution.py:284
  14.0 0.3 collective-permute-done.2
  14.3 1.5 %collective-permute-start.3 = (bf16[8,1,32,128]{3,2,1,0:T(8,128)(2,1)S(1)}, bf16[8,1,32,128]{3,2,1,0:T(8,128)(2,1)S(1)}, u32[]{:S(2)}, u32[]{:S(2)}) collective-permute-start(bf16[8,1,32,128]{3,2,1,0:T(8,128)(2,1)S(1)} %constant_dynamic-update-slice_fusion.2.after_ref), channel_id=1, source_target_pairs={{0,2},{1,3},{2,0},{3,1},{4,6},{5,7},{6,4},{7,5},{8,10},{9,11},{10,... | collective-permute-start | bytes 196616 | tf_op jit(solution)/shard_map/ppermute | solution.py:271
  15.8 2.1 %shard_map.86 = (bf16[1024,1664]{1,0:T(8,128)(2,1)S(1)}, bf16[8,1,32,128]{3,2,1,0:T(8,128)(2,1)S(1)}) custom-call(bf16[8192,1664]{1,0:T(8,128)(2,1)} %codes_ref.11, bf16[8,1,32,128]{3,2,1,0:T(8,128)(2,1)S(1)} %constant_dynamic-update-slice_fusion.2.after_ref), custom_call_target="tpu_custom_call" | custom-call | bytes 3407872 | tf_op jit(solution)/shard_map/pallas_call | solution.py:284
  17.8 0.7 %collective-permute-done.3 = bf16[8,1,32,128]{3,2,1,0:T(8,128)(2,1)S(1)} collective-permute-done((bf16[8,1,32,128]{3,2,1,0:T(8,128)(2,1)S(1)}, bf16[8,1,32,128]{3,2,1,0:T(8,128)(2,1)S(1)}, u32[]{:S(2)}, u32[]{:S(2)}) %collective-permute-start.3) | collective-permute-done | bytes 65568 | tf_op jit(solution)/shard_map/ppermute | solution.py:271
  18.6 0.1 collective-permute-start.4
  18.6 1.3 %collective-permute-done.4 = bf16[16,1,32,128]{3,2,1,0:T(8,128)(2,1)S(1)} collective-permute-done((bf16[16,1,32,128]{3,2,1,0:T(8,128)(2,1)S(1)}, bf16[16,1,32,128]{3,2,1,0:T(8,128)(2,1)S(1)}, u32[]{:S(2)}, u32[]{:S(2)}) %collective-permute-start.4) | collective-permute-done | bytes 131104 | tf_op jit(solution)/shard_map/ppermute | solution.py:271
  20.0 5.8 %shard_map.87 = (f32[16,1664]{1,0:T(8,128)S(1)}, f32[16,1664]{1,0:T(8,128)S(1)}, bf16[1,2,16,1664]{3,2,1,0:T(8,128)(2,1)S(1)}, f32[1,16,1664]{2,1,0:T(8,128)S(1)}) custom-call(bf16[32,1,32,128]{3,2,1,0:T(8,128)(2,1)S(1)} %pad_maximum_fusion.refs_0_, f32[64,1664]{1,0:T(8,128)} %refs_1_.2, bf16[8192,1664]{1,0:T(8,128)(2,1)} %refs_2_.1, f32[64,1664]{1,0:T(8,128)} %refs_3_.1, ...), custom_call_target="tpu_custom_call" | custom-call | flops 872415232 | bytes 13631488 | tf_op jit(solution)/shard_map/pallas_call | solution.py:318
  25.8 1.6 %collective-permute-start.5 = (bf16[2,16,1664]{2,1,0:T(8,128)(2,1)S(1)}, bf16[2,16,1664]{2,1,0:T(8,128)(2,1)S(1)}, u32[]{:S(2)}, u32[]{:S(2)}) collective-permute-start(bf16[2,16,1664]{2,1,0:T(8,128)(2,1)S(1)} %bitcast.12), channel_id=1, source_target_pairs={{0,16},{16,0},{1,17},{17,1},{2,18},{18,2},{3,19},{19,3},{4,20},{20... | collective-permute-start | bytes 319496 | tf_op jit(solution)/shard_map/ppermute | solution.py:280
  27.4 3.6 %shard_map.88 = (bf16[1664,2560]{1,0:T(8,128)(2,1)S(1)}, s32[52,52]{1,0:T(8,128)S(1)}) custom-call(bf16[1664,8192]{1,0:T(8,128)(2,1)} %refs_1_.3, bf16[1,2,16,1664]{3,2,1,0:T(8,128)(2,1)S(1)} %get-tuple-element.39.after_ref, s32[52,52]{1,0:T(8,128)} %hadamard_ref.1), custom_call_target="tpu_custom_call" | custom-call | bytes 8519680 | tf_op jit(solution)/shard_map/pallas_call | solution.py:344
  31.0 0.0 collective-permute-done.5.refs_0_
  31.0 0.5 shard_map.89
  31.4 0.1 collective-permute-start.6
  31.5 1.2 %collective-permute-done.6 = bf16[16,1664]{1,0:T(8,128)(2,1)S(1)} collective-permute-done((bf16[16,1664]{1,0:T(8,128)(2,1)S(1)}, bf16[16,1664]{1,0:T(8,128)(2,1)S(1)}, u32[]{:S(2)}, u32[]{:S(2)}) %collective-permute-start.6) | collective-permute-done | bytes 53280 | tf_op jit(solution)/shard_map/ppermute | solution.py:271
  32.8 1.5 %collective-permute-start.7 = (bf16[16,1664]{1,0:T(8,128)(2,1)S(1)}, bf16[16,1664]{1,0:T(8,128)(2,1)S(1)}, u32[]{:S(2)}, u32[]{:S(2)}) collective-permute-start(bf16[16,1664]{1,0:T(8,128)(2,1)S(1)} %get-tuple-element.55.after_ref), channel_id=1, source_target_pairs={{0,2},{1,3},{2,0},{3,1},{4,6},{5,7},{6,4},{7,5},{8,10},{9,11},{10,... | collective-permute-start | bytes 159752 | tf_op jit(solution)/shard_map/ppermute | solution.py:271
  34.3 2.5 %shard_map.90 = (bf16[1664,1536]{1,0:T(8,128)(2,1)S(1)}, f32[16,1664]{1,0:T(8,128)S(1)}) custom-call(bf16[1664,8192]{1,0:T(8,128)(2,1)} %refs_1_.3, bf16[16,1664]{1,0:T(8,128)(2,1)S(1)} %get-tuple-element.55.after_ref), custom_call_target="tpu_custom_call" | custom-call | bytes 5111808 | tf_op jit(solution)/shard_map/pallas_call | solution.py:369
  36.9 0.1 collective-permute-done.7
  37.0 1.6 %collective-permute-start.8 = (bf16[16,1664]{1,0:T(8,128)(2,1)S(1)}, bf16[16,1664]{1,0:T(8,128)(2,1)S(1)}, u32[]{:S(2)}, u32[]{:S(2)}) collective-permute-start(bf16[16,1664]{1,0:T(8,128)(2,1)S(1)} %fusion.4.after_ref), channel_id=1, source_target_pairs={{0,4},{1,5},{2,6},{3,7},{4,0},{5,1},{6,2},{7,3},{8,12},{9,13},{10,... | collective-permute-start | bytes 159752 | tf_op jit(solution)/shard_map/ppermute | solution.py:271
  38.6 2.5 %shard_map.91 = (bf16[1664,1536]{1,0:T(8,128)(2,1)S(1)}, f32[16,1664]{1,0:T(8,128)S(1)}) custom-call(bf16[1664,8192]{1,0:T(8,128)(2,1)} %refs_1_.3, bf16[16,1664]{1,0:T(8,128)(2,1)S(1)} %fusion.4.after_ref), custom_call_target="tpu_custom_call" | custom-call | bytes 5111808 | tf_op jit(solution)/shard_map/pallas_call | solution.py:369
  41.2 0.0 collective-permute-done.8
  41.2 2.7 %collective-permute-start.9 = (bf16[16,1664]{1,0:T(8,128)(2,1)S(1)}, bf16[16,1664]{1,0:T(8,128)(2,1)S(1)}, u32[]{:S(2)}, u32[]{:S(2)}) collective-permute-start(bf16[16,1664]{1,0:T(8,128)(2,1)S(1)} %get-tuple-element.53.after_ref), channel_id=1, source_target_pairs={{0,8},{1,9},{2,10},{3,11},{4,12},{5,13},{6,14},{7,15},{8,0},{9,1},... | collective-permute-start | bytes 159752 | tf_op jit(solution)/shard_map/ppermute | solution.py:271
  43.9 3.6 %shard_map.92 = (bf16[1664,2560]{1,0:T(8,128)(2,1)S(1)}, f32[16,1664]{1,0:T(8,128)S(1)}) custom-call(bf16[1664,8192]{1,0:T(8,128)(2,1)} %refs_1_.3, bf16[16,1664]{1,0:T(8,128)(2,1)S(1)} %get-tuple-element.53.after_ref), custom_call_target="tpu_custom_call" | custom-call | bytes 8519680 | tf_op jit(solution)/shard_map/pallas_call | solution.py:369
  47.5 0.0 collective-permute-done.9
  47.5 0.0 copy-start
  47.5 2.6 %shard_map.93 = (f32[8,1,64,128]{3,2,1,0:T(8,128)S(1)}, bf16[8,1,64,128]{3,2,1,0:T(8,128)(2,1)S(1)}) custom-call(f32[16,1664]{1,0:T(8,128)S(1)} %convert_add_fusion.1.refs_0_, bf16[1664,8192]{1,0:T(8,128)(2,1)} %refs_1_.3, bf16[1664,2560]{1,0:T(8,128)(2,1)S(1)} %get-tuple-element.47.refs_2_, bf16[1664,1536]{1,0:T(8,128)(2,1)S(1)} %get-tuple-element.48.refs_3_, ...), custom_call_target="tpu_custom_call" | custom-call | flops 436207616 | bytes 13631488 | tf_op jit(solution)/shard_map/pallas_call | solution.py:390
  50.1 0.1 collective-permute-start.10
  50.2 1.3 %collective-permute-done.10 = bf16[8,1,64,128]{3,2,1,0:T(8,128)(2,1)S(1)} collective-permute-done((bf16[8,1,64,128]{3,2,1,0:T(8,128)(2,1)S(1)}, bf16[8,1,64,128]{3,2,1,0:T(8,128)(2,1)S(1)}, u32[]{:S(2)}, u32[]{:S(2)}) %collective-permute-start.10) | collective-permute-done | bytes 131104 | tf_op jit(solution)/shard_map/ppermute | solution.py:271
  51.6 1.6 %collective-permute-start.11 = (bf16[4,1,64,128]{3,2,1,0:T(8,128)(2,1)S(1)}, bf16[4,1,64,128]{3,2,1,0:T(8,128)(2,1)S(1)}, u32[]{:S(2)}, u32[]{:S(2)}) collective-permute-start(bf16[4,1,64,128]{3,2,1,0:T(8,128)(2,1)S(1)} %slice.45), channel_id=1, source_target_pairs={{0,2},{1,3},{2,0},{3,1},{4,6},{5,7},{6,4},{7,5},{8,10},{9,11},{10,... | collective-permute-start | bytes 196616 | tf_op jit(solution)/shard_map/ppermute | solution.py:271
  53.1 2.8 %collective-permute-done.11 = bf16[4,1,64,128]{3,2,1,0:T(8,128)(2,1)S(1)} collective-permute-done((bf16[4,1,64,128]{3,2,1,0:T(8,128)(2,1)S(1)}, bf16[4,1,64,128]{3,2,1,0:T(8,128)(2,1)S(1)}, u32[]{:S(2)}, u32[]{:S(2)}) %collective-permute-start.11) | collective-permute-done | bytes 65568 | tf_op jit(solution)/shard_map/ppermute | solution.py:271
  55.9 1.6 %collective-permute-start.12 = (bf16[2,1,64,128]{3,2,1,0:T(8,128)(2,1)S(1)}, bf16[2,1,64,128]{3,2,1,0:T(8,128)(2,1)S(1)}, u32[]{:S(2)}, u32[]{:S(2)}) collective-permute-start(bf16[2,1,64,128]{3,2,1,0:T(8,128)(2,1)S(1)} %slice.46), channel_id=1, source_target_pairs={{0,4},{1,5},{2,6},{3,7},{4,0},{5,1},{6,2},{7,3},{8,12},{9,13},{10,... | collective-permute-start | bytes 98312 | tf_op jit(solution)/shard_map/ppermute | solution.py:271
  57.6 2.3 %collective-permute-done.12 = bf16[2,1,64,128]{3,2,1,0:T(8,128)(2,1)S(1)} collective-permute-done((bf16[2,1,64,128]{3,2,1,0:T(8,128)(2,1)S(1)}, bf16[2,1,64,128]{3,2,1,0:T(8,128)(2,1)S(1)}, u32[]{:S(2)}, u32[]{:S(2)}) %collective-permute-start.12) | collective-permute-done | bytes 32800 | tf_op jit(solution)/shard_map/ppermute | solution.py:271
  59.9 1.5 %collective-permute-start.13 = (bf16[1,1,64,128]{3,2,1,0:T(8,128)(2,1)S(1)}, bf16[1,1,64,128]{3,2,1,0:T(8,128)(2,1)S(1)}, u32[]{:S(2)}, u32[]{:S(2)}) collective-permute-start(bf16[1,1,64,128]{3,2,1,0:T(8,128)(2,1)S(1)} %slice.47), channel_id=1, source_target_pairs={{0,8},{1,9},{2,10},{3,11},{4,12},{5,13},{6,14},{7,15},{8,0},{9,1},... | collective-permute-start | bytes 49160 | tf_op jit(solution)/shard_map/ppermute | solution.py:271
  61.5 3.2 %collective-permute-done.13 = bf16[1,1,64,128]{3,2,1,0:T(8,128)(2,1)S(1)} collective-permute-done((bf16[1,1,64,128]{3,2,1,0:T(8,128)(2,1)S(1)}, bf16[1,1,64,128]{3,2,1,0:T(8,128)(2,1)S(1)}, u32[]{:S(2)}, u32[]{:S(2)}) %collective-permute-start.13) | collective-permute-done | bytes 16416 | tf_op jit(solution)/shard_map/ppermute | solution.py:271
  64.6 0.0 copy-done
  64.6 0.6 convert_element_type.54
  (18 shorter events, 0.3 us)
Async XLA Ops:
  0.0 5.1 %collective-permute-start = (bf16[1,8192]{1,0:T(2,128)(2,1)}, bf16[1,8192]{1,0:T(2,128)(2,1)S(1)}, u32[]{:S(2)}, u32[]{:S(2)}) collective-permute-start(bf16[1,8192]{1,0:T(2,128)(2,1)} %after_ref.1), channel_id=1, source_target_pairs={{0,16},{16,0},{1,17},{17,1},{2,18},{18,2},{3,19},{19,3},{4,20},{20... | collective-permute-start | bytes 49160 | tf_op jit(solution)/shard_map/ppermute | solution.py:280
  5.1 5.2 %collective-permute-start.1 = (bf16[2,1,32,128]{3,2,1,0:T(8,128)(2,1)S(1)}, bf16[2,1,32,128]{3,2,1,0:T(8,128)(2,1)S(1)}, u32[]{:S(2)}, u32[]{:S(2)}) collective-permute-start(bf16[2,1,32,128]{3,2,1,0:T(8,128)(2,1)S(1)} %shard_map.83.after_ref), channel_id=1, source_target_pairs={{0,8},{1,9},{2,10},{3,11},{4,12},{5,13},{6,14},{7,15},{8,0},{9,1},... | collective-permute-start | bytes 49160 | tf_op jit(solution)/shard_map/ppermute | solution.py:271
  10.3 4.0 %collective-permute-start.2 = (bf16[4,1,32,128]{3,2,1,0:T(8,128)(2,1)S(1)}, bf16[4,1,32,128]{3,2,1,0:T(8,128)(2,1)S(1)}, u32[]{:S(2)}, u32[]{:S(2)}) collective-permute-start(bf16[4,1,32,128]{3,2,1,0:T(8,128)(2,1)S(1)} %constant_dynamic-update-slice_fusion.after_ref), channel_id=1, source_target_pairs={{0,4},{1,5},{2,6},{3,7},{4,0},{5,1},{6,2},{7,3},{8,12},{9,13},{10,... | collective-permute-start | bytes 98312 | tf_op jit(solution)/shard_map/ppermute | solution.py:271
  14.3 4.3 %collective-permute-start.3 = (bf16[8,1,32,128]{3,2,1,0:T(8,128)(2,1)S(1)}, bf16[8,1,32,128]{3,2,1,0:T(8,128)(2,1)S(1)}, u32[]{:S(2)}, u32[]{:S(2)}) collective-permute-start(bf16[8,1,32,128]{3,2,1,0:T(8,128)(2,1)S(1)} %constant_dynamic-update-slice_fusion.2.after_ref), channel_id=1, source_target_pairs={{0,2},{1,3},{2,0},{3,1},{4,6},{5,7},{6,4},{7,5},{8,10},{9,11},{10,... | collective-permute-start | bytes 196616 | tf_op jit(solution)/shard_map/ppermute | solution.py:271
  18.6 1.4 %collective-permute-start.4 = (bf16[16,1,32,128]{3,2,1,0:T(8,128)(2,1)S(1)}, bf16[16,1,32,128]{3,2,1,0:T(8,128)(2,1)S(1)}, u32[]{:S(2)}, u32[]{:S(2)}) collective-permute-start(bf16[16,1,32,128]{3,2,1,0:T(8,128)(2,1)S(1)} %pad_maximum_fusion.1), channel_id=1, source_target_pairs={{0,1},{1,0},{2,3},{3,2},{4,5},{5,4},{6,7},{7,6},{8,9},{9,8},{10,11... | collective-permute-start | bytes 393224 | tf_op jit(solution)/shard_map/ppermute | solution.py:271
  25.8 5.2 %collective-permute-start.5 = (bf16[2,16,1664]{2,1,0:T(8,128)(2,1)S(1)}, bf16[2,16,1664]{2,1,0:T(8,128)(2,1)S(1)}, u32[]{:S(2)}, u32[]{:S(2)}) collective-permute-start(bf16[2,16,1664]{2,1,0:T(8,128)(2,1)S(1)} %bitcast.12), channel_id=1, source_target_pairs={{0,16},{16,0},{1,17},{17,1},{2,18},{18,2},{3,19},{19,3},{4,20},{20... | collective-permute-start | bytes 319496 | tf_op jit(solution)/shard_map/ppermute | solution.py:280
  31.4 1.3 %collective-permute-start.6 = (bf16[16,1664]{1,0:T(8,128)(2,1)S(1)}, bf16[16,1664]{1,0:T(8,128)(2,1)S(1)}, u32[]{:S(2)}, u32[]{:S(2)}) collective-permute-start(bf16[16,1664]{1,0:T(8,128)(2,1)S(1)} %get-tuple-element.43), channel_id=1, source_target_pairs={{0,1},{1,0},{2,3},{3,2},{4,5},{5,4},{6,7},{7,6},{8,9},{9,8},{10,11... | collective-permute-start | bytes 159752 | tf_op jit(solution)/shard_map/ppermute | solution.py:271
  32.8 4.2 %collective-permute-start.7 = (bf16[16,1664]{1,0:T(8,128)(2,1)S(1)}, bf16[16,1664]{1,0:T(8,128)(2,1)S(1)}, u32[]{:S(2)}, u32[]{:S(2)}) collective-permute-start(bf16[16,1664]{1,0:T(8,128)(2,1)S(1)} %get-tuple-element.55.after_ref), channel_id=1, source_target_pairs={{0,2},{1,3},{2,0},{3,1},{4,6},{5,7},{6,4},{7,5},{8,10},{9,11},{10,... | collective-permute-start | bytes 159752 | tf_op jit(solution)/shard_map/ppermute | solution.py:271
  37.0 4.2 %collective-permute-start.8 = (bf16[16,1664]{1,0:T(8,128)(2,1)S(1)}, bf16[16,1664]{1,0:T(8,128)(2,1)S(1)}, u32[]{:S(2)}, u32[]{:S(2)}) collective-permute-start(bf16[16,1664]{1,0:T(8,128)(2,1)S(1)} %fusion.4.after_ref), channel_id=1, source_target_pairs={{0,4},{1,5},{2,6},{3,7},{4,0},{5,1},{6,2},{7,3},{8,12},{9,13},{10,... | collective-permute-start | bytes 159752 | tf_op jit(solution)/shard_map/ppermute | solution.py:271
  41.2 6.2 %collective-permute-start.9 = (bf16[16,1664]{1,0:T(8,128)(2,1)S(1)}, bf16[16,1664]{1,0:T(8,128)(2,1)S(1)}, u32[]{:S(2)}, u32[]{:S(2)}) collective-permute-start(bf16[16,1664]{1,0:T(8,128)(2,1)S(1)} %get-tuple-element.53.after_ref), channel_id=1, source_target_pairs={{0,8},{1,9},{2,10},{3,11},{4,12},{5,13},{6,14},{7,15},{8,0},{9,1},... | collective-permute-start | bytes 159752 | tf_op jit(solution)/shard_map/ppermute | solution.py:271
  47.5 17.1 %copy-start = (f32[8192]{0:T(1024)S(1)}, f32[8192]{0:T(1024)}, u32[]{:S(2)}) copy-start(f32[8192]{0:T(1024)} %param.14) | copy-start | bytes 98308
  50.1 1.4 %collective-permute-start.10 = (bf16[8,1,64,128]{3,2,1,0:T(8,128)(2,1)S(1)}, bf16[8,1,64,128]{3,2,1,0:T(8,128)(2,1)S(1)}, u32[]{:S(2)}, u32[]{:S(2)}) collective-permute-start(bf16[8,1,64,128]{3,2,1,0:T(8,128)(2,1)S(1)} %get-tuple-element.52), channel_id=1, source_target_pairs={{0,1},{1,0},{2,3},{3,2},{4,5},{5,4},{6,7},{7,6},{8,9},{9,8},{10,11... | collective-permute-start | bytes 393224 | tf_op jit(solution)/shard_map/ppermute | solution.py:271
  51.6 4.3 %collective-permute-start.11 = (bf16[4,1,64,128]{3,2,1,0:T(8,128)(2,1)S(1)}, bf16[4,1,64,128]{3,2,1,0:T(8,128)(2,1)S(1)}, u32[]{:S(2)}, u32[]{:S(2)}) collective-permute-start(bf16[4,1,64,128]{3,2,1,0:T(8,128)(2,1)S(1)} %slice.45), channel_id=1, source_target_pairs={{0,2},{1,3},{2,0},{3,1},{4,6},{5,7},{6,4},{7,5},{8,10},{9,11},{10,... | collective-permute-start | bytes 196616 | tf_op jit(solution)/shard_map/ppermute | solution.py:271
  55.9 4.0 %collective-permute-start.12 = (bf16[2,1,64,128]{3,2,1,0:T(8,128)(2,1)S(1)}, bf16[2,1,64,128]{3,2,1,0:T(8,128)(2,1)S(1)}, u32[]{:S(2)}, u32[]{:S(2)}) collective-permute-start(bf16[2,1,64,128]{3,2,1,0:T(8,128)(2,1)S(1)} %slice.46), channel_id=1, source_target_pairs={{0,4},{1,5},{2,6},{3,7},{4,0},{5,1},{6,2},{7,3},{8,12},{9,13},{10,... | collective-permute-start | bytes 98312 | tf_op jit(solution)/shard_map/ppermute | solution.py:271
  59.9 4.7 %collective-permute-start.13 = (bf16[1,1,64,128]{3,2,1,0:T(8,128)(2,1)S(1)}, bf16[1,1,64,128]{3,2,1,0:T(8,128)(2,1)S(1)}, u32[]{:S(2)}, u32[]{:S(2)}) collective-permute-start(bf16[1,1,64,128]{3,2,1,0:T(8,128)(2,1)S(1)} %slice.47), channel_id=1, source_target_pairs={{0,8},{1,9},{2,10},{3,11},{4,12},{5,13},{6,14},{7,15},{8,0},{9,1},... | collective-permute-start | bytes 49160 | tf_op jit(solution)/shard_map/ppermute | solution.py:271

commit v5 on v4

--- a/solution.py
+++ b/solution.py
@@ -17,7 +17,7 @@
 ROWS = (2, 2, 2, 2)
 SPAN = 512
 AHEAD = 8
-SPANS = (5, 3, 3, 5)
+SPANS = (5, 3, 3, 4)
 
 VMEM = pl.BlockSpec(memory_space=pltpu.VMEM)
 HBM = pl.BlockSpec(memory_space=pltpu.HBM)
@@ -44,6 +44,13 @@
         here = codes_ref.at[:, pl.ds(first + index * step, step)]
         copies.append(fetch(here, out_ref.at[:, pl.ds(index * step, step)], sems.at[index]))
     return copies
+
+
+def rows_columns_kernel(before, step, span, codes_ref, after_ref, down_ref, out_ref, same_ref, columns_ref, sems, column_sems):
+    copies = fetch_columns(0, span, down_ref, columns_ref, column_sems)
+    rows_kernel(before, step, codes_ref, after_ref, out_ref, same_ref, sems)
+    for copy in copies:
+        copy.wait()
 
 
 def columns_kernel(first, step, bit, codes_ref, after_ref, out_ref, sign_ref, sems):
@@ -308,7 +315,22 @@
     for index, bit in enumerate(reversed(bits)):
         other = swap(pieces, bit)
         if index + 1 < len(ROWS):
-            part, pieces = some_rows(index + 1, first, pieces, ANY)
+            if index + 2 < len(ROWS):
+                part, pieces = some_rows(index + 1, first, pieces, ANY)
+            else:
+                part, pieces, down_part = pl.pallas_call(
+                    functools.partial(rows_columns_kernel, first, CHUNK, SPAN),
+                    out_shape=(
+                        pltpu.VMEM((ROWS[-1] * CHUNK, units), jnp.bfloat16),
+                        pltpu.VMEM(pieces.shape, pieces.dtype),
+                        pltpu.VMEM((units, SPAN), jnp.bfloat16),
+                    ),
+                    in_specs=[HBM, ANY, HBM],
+                    out_specs=(VMEM, VMEM, VMEM),
+                    scratch_shapes=[pltpu.SemaphoreType.DMA((ROWS[-1] + 1,)), pltpu.SemaphoreType.DMA((1,))],
+                    compiler_params=pltpu.CompilerParams(vmem_limit_bytes=2 * MIB),
+                    cost_estimate=cost(2 * ROWS[-1] * CHUNK * units + 2 * SPAN * units),
+                )(in_hbm(gate_codes), pieces, in_hbm(down_codes))
             held.append(part)
             first += part.shape[0]
         pieces = jnp.concatenate([pieces, other], axis=0)
@@ -342,7 +364,7 @@
     others = [by_part(send[step - 1], -step) for step in range(1, parts)]
     columns = SPANS[0] * SPAN
     part, small = pl.pallas_call(
-        functools.partial(columns_small_kernel, 0, SPAN),
+        functools.partial(columns_small_kernel, SPAN, SPAN),
         out_shape=(pltpu.VMEM((units, columns), jnp.bfloat16), pltpu.VMEM(hadamard.shape, hadamard.dtype)),
         in_specs=[HBM, ANY, HBM],
         out_specs=(VMEM, VMEM),
@@ -350,8 +372,8 @@
         compiler_params=pltpu.CompilerParams(vmem_limit_bytes=2 * MIB),
         cost_estimate=cost(2 * units * columns),
     )(in_hbm(down_codes), send, in_hbm(hadamard))
-    held = [part]
-    first = columns
+    held = [down_part, part]
+    first = SPAN + columns
 
     turned, send = pl.pallas_call(
         rotate_kernel,

time: 65.4 us -> 64.8 us (level)
  waiting for transfers between devices: 13.4 us -> 12.4 us
    pallas_call x1 -> x2, Pallas kernels: 3.59 us -> 6.14 us  [the longest x1 3.59 us: per_device(): pl.pallas_call(functools.partial(columns_small_kernel, SPAN, SPAN), out_s...]
    pallas_call x4 -> x3, Pallas kernels: 8.07 us -> 6.02 us  [some_rows(): pl.pallas_call(functools.partial(rows_kernel, first, CHUNK), out_shape=(p...]
    ppermute x12, waiting for transfers between devices: 13.3 us -> 12.3 us  [swap(): return lax.ppermute(value, 'hx', [(at, at ^ bit) for at in range(devices)])]
where the time goes in v5:
time: 64.8 us; the launch traced here: 64.7 us
  Pallas kernels  29 us (45%)
  starting transfers between devices  22.2 us (34%)
  waiting for transfers between devices  12.4 us (19%)
  local copies, waits for them, and re-layouts  0.69 us (1%)
    ppermute x12, starting transfers between devices, swap(): return lax.ppermute(value, 'hx', [(at, at ^ bit) for at in range(devices)])  17.6 us
    ppermute x12, waiting for transfers between devices, swap(): return lax.ppermute(value, 'hx', [(at, at ^ bit) for at in range(devices)])  12.3 us
    pallas_call x3, Pallas kernels, per_device(): pl.pallas_call(functools.partial(columns_kernel, first, SPAN, bit), out_s...  8.12 us
    pallas_call x3, Pallas kernels, some_rows(): pl.pallas_call(functools.partial(rows_kernel, first, CHUNK), out_shape=(p...  6.02 us
    pallas_call x1, Pallas kernels, per_device(): pl.pallas_call(functools.partial(hidden_kernel, group, parts, gathered, e...  5.76 us
    ppermute x2, starting transfers between devices, by_part(): lax.ppermute(value, 'groups', [(at, (at + step) % parts) for at in range(...  4.55 us
    pallas_call x1, Pallas kernels, per_device(): pl.pallas_call(functools.partial(columns_small_kernel, SPAN, SPAN), out_s...  3.59 us
    pallas_call x1, Pallas kernels, per_device(): pl.pallas_call(functools.partial(rows_columns_kernel, first, CHUNK, SPAN)...  2.55 us
  transfers between devices with their start and end apart: 14, of which 10 were waited for; matrix products, arithmetic and copies ran while one was open for 0% of the time, Pallas kernels for 31%

profile of v5, /device:TPU:0, one launch (start us, length us, event | category | flops | bytes accessed | tf_op | source)
XLA Modules:
  0.0 64.7 jit_solution(910962993424775929)
XLA Ops:
  0.0 3.0 %collective-permute-start = (bf16[1,8192]{1,0:T(2,128)(2,1)}, bf16[1,8192]{1,0:T(2,128)(2,1)S(1)}, u32[]{:S(2)}, u32[]{:S(2)}) collective-permute-start(bf16[1,8192]{1,0:T(2,128)(2,1)} %after_ref.1), channel_id=1, source_target_pairs={{0,16},{16,0},{1,17},{17,1},{2,18},{18,2},{3,19},{19,3},{4,20},{20... | collective-permute-start | bytes 49160 | tf_op jit(solution)/shard_map/ppermute | solution.py:287
  3.0 2.0 %shard_map.82 = (bf16[1024,1664]{1,0:T(8,128)(2,1)S(1)}, bf16[1,8192]{1,0:T(2,128)(2,1)S(1)}) custom-call(bf16[8192,1664]{1,0:T(8,128)(2,1)} %codes_ref.11, bf16[1,8192]{1,0:T(2,128)(2,1)} %after_ref.1), custom_call_target="tpu_custom_call" | custom-call | bytes 3407872 | tf_op jit(solution)/shard_map/pallas_call | solution.py:291
  5.0 0.1 collective-permute-done.refs_0_
  5.1 3.2 %collective-permute-start.1 = (bf16[2,1,32,128]{3,2,1,0:T(8,128)(2,1)S(1)}, bf16[2,1,32,128]{3,2,1,0:T(8,128)(2,1)S(1)}, u32[]{:S(2)}, u32[]{:S(2)}) collective-permute-start(bf16[2,1,32,128]{3,2,1,0:T(8,128)(2,1)S(1)} %shard_map.83.after_ref), channel_id=1, source_target_pairs={{0,8},{1,9},{2,10},{3,11},{4,12},{5,13},{6,14},{7,15},{8,0},{9,1},... | collective-permute-start | bytes 49160 | tf_op jit(solution)/shard_map/ppermute | solution.py:278
  8.3 2.0 %shard_map.84 = (bf16[1024,1664]{1,0:T(8,128)(2,1)S(1)}, bf16[2,1,32,128]{3,2,1,0:T(8,128)(2,1)S(1)}) custom-call(bf16[8192,1664]{1,0:T(8,128)(2,1)} %codes_ref.11, bf16[2,1,32,128]{3,2,1,0:T(8,128)(2,1)S(1)} %shard_map.83.after_ref), custom_call_target="tpu_custom_call" | custom-call | bytes 3407872 | tf_op jit(solution)/shard_map/pallas_call | solution.py:291
  10.3 0.0 collective-permute-done.1
  10.3 1.6 %collective-permute-start.2 = (bf16[4,1,32,128]{3,2,1,0:T(8,128)(2,1)S(1)}, bf16[4,1,32,128]{3,2,1,0:T(8,128)(2,1)S(1)}, u32[]{:S(2)}, u32[]{:S(2)}) collective-permute-start(bf16[4,1,32,128]{3,2,1,0:T(8,128)(2,1)S(1)} %constant_dynamic-update-slice_fusion.after_ref), channel_id=1, source_target_pairs={{0,4},{1,5},{2,6},{3,7},{4,0},{5,1},{6,2},{7,3},{8,12},{9,13},{10,... | collective-permute-start | bytes 98312 | tf_op jit(solution)/shard_map/ppermute | solution.py:278
  11.9 2.0 %shard_map.85 = (bf16[1024,1664]{1,0:T(8,128)(2,1)S(1)}, bf16[4,1,32,128]{3,2,1,0:T(8,128)(2,1)S(1)}) custom-call(bf16[8192,1664]{1,0:T(8,128)(2,1)} %codes_ref.11, bf16[4,1,32,128]{3,2,1,0:T(8,128)(2,1)S(1)} %constant_dynamic-update-slice_fusion.after_ref), custom_call_target="tpu_custom_call" | custom-call | bytes 3407872 | tf_op jit(solution)/shard_map/pallas_call | solution.py:291
  14.0 0.3 collective-permute-done.2
  14.3 1.5 %collective-permute-start.3 = (bf16[8,1,32,128]{3,2,1,0:T(8,128)(2,1)S(1)}, bf16[8,1,32,128]{3,2,1,0:T(8,128)(2,1)S(1)}, u32[]{:S(2)}, u32[]{:S(2)}) collective-permute-start(bf16[8,1,32,128]{3,2,1,0:T(8,128)(2,1)S(1)} %constant_dynamic-update-slice_fusion.2.after_ref), channel_id=1, source_target_pairs={{0,2},{1,3},{2,0},{3,1},{4,6},{5,7},{6,4},{7,5},{8,10},{9,11},{10,... | collective-permute-start | bytes 196616 | tf_op jit(solution)/shard_map/ppermute | solution.py:278
  15.8 2.5 %shard_map.86 = (bf16[1024,1664]{1,0:T(8,128)(2,1)S(1)}, bf16[8,1,32,128]{3,2,1,0:T(8,128)(2,1)S(1)}, bf16[1664,512]{1,0:T(8,128)(2,1)S(1)}) custom-call(bf16[8192,1664]{1,0:T(8,128)(2,1)} %codes_ref.11, bf16[8,1,32,128]{3,2,1,0:T(8,128)(2,1)S(1)} %constant_dynamic-update-slice_fusion.2.after_ref, bf16[1664,8192]{1,0:T(8,128)(2,1)} %refs_1_.3), custom_call_target="tpu_custom_call" | custom-call | bytes 5111808 | tf_op jit(solution)/shard_map/pallas_call | solution.py:321
  18.3 0.2 collective-permute-done.3
  18.6 0.1 collective-permute-start.4
  18.6 1.3 %collective-permute-done.4 = bf16[16,1,32,128]{3,2,1,0:T(8,128)(2,1)S(1)} collective-permute-done((bf16[16,1,32,128]{3,2,1,0:T(8,128)(2,1)S(1)}, bf16[16,1,32,128]{3,2,1,0:T(8,128)(2,1)S(1)}, u32[]{:S(2)}, u32[]{:S(2)}) %collective-permute-start.4) | collective-permute-done | bytes 131104 | tf_op jit(solution)/shard_map/ppermute | solution.py:278
  20.0 5.8 %shard_map.87 = (f32[16,1664]{1,0:T(8,128)S(1)}, f32[16,1664]{1,0:T(8,128)S(1)}, bf16[1,2,16,1664]{3,2,1,0:T(8,128)(2,1)S(1)}, f32[1,16,1664]{2,1,0:T(8,128)S(1)}) custom-call(bf16[32,1,32,128]{3,2,1,0:T(8,128)(2,1)S(1)} %pad_maximum_fusion.refs_0_, f32[64,1664]{1,0:T(8,128)} %refs_1_.2, bf16[8192,1664]{1,0:T(8,128)(2,1)} %refs_2_.1, f32[64,1664]{1,0:T(8,128)} %refs_3_.1, ...), custom_call_target="tpu_custom_call" | custom-call | flops 872415232 | bytes 13631488 | tf_op jit(solution)/shard_map/pallas_call | solution.py:340
  25.8 1.6 %collective-permute-start.5 = (bf16[2,16,1664]{2,1,0:T(8,128)(2,1)S(1)}, bf16[2,16,1664]{2,1,0:T(8,128)(2,1)S(1)}, u32[]{:S(2)}, u32[]{:S(2)}) collective-permute-start(bf16[2,16,1664]{2,1,0:T(8,128)(2,1)S(1)} %bitcast.12), channel_id=1, source_target_pairs={{0,16},{16,0},{1,17},{17,1},{2,18},{18,2},{3,19},{19,3},{4,20},{20... | collective-permute-start | bytes 319496 | tf_op jit(solution)/shard_map/ppermute | solution.py:287
  27.4 3.6 %shard_map.88 = (bf16[1664,2560]{1,0:T(8,128)(2,1)S(1)}, s32[52,52]{1,0:T(8,128)S(1)}) custom-call(bf16[1664,8192]{1,0:T(8,128)(2,1)} %refs_1_.3, bf16[1,2,16,1664]{3,2,1,0:T(8,128)(2,1)S(1)} %get-tuple-element.40.after_ref, s32[52,52]{1,0:T(8,128)} %hadamard_ref.1), custom_call_target="tpu_custom_call" | custom-call | bytes 8519680 | tf_op jit(solution)/shard_map/pallas_call | solution.py:366
  31.0 0.0 collective-permute-done.5.refs_0_
  31.0 0.5 shard_map.89
  31.4 0.1 collective-permute-start.6
  31.5 1.2 %collective-permute-done.6 = bf16[16,1664]{1,0:T(8,128)(2,1)S(1)} collective-permute-done((bf16[16,1664]{1,0:T(8,128)(2,1)S(1)}, bf16[16,1664]{1,0:T(8,128)(2,1)S(1)}, u32[]{:S(2)}, u32[]{:S(2)}) %collective-permute-start.6) | collective-permute-done | bytes 53280 | tf_op jit(solution)/shard_map/ppermute | solution.py:278
  32.8 1.5 %collective-permute-start.7 = (bf16[16,1664]{1,0:T(8,128)(2,1)S(1)}, bf16[16,1664]{1,0:T(8,128)(2,1)S(1)}, u32[]{:S(2)}, u32[]{:S(2)}) collective-permute-start(bf16[16,1664]{1,0:T(8,128)(2,1)S(1)} %get-tuple-element.57.after_ref), channel_id=1, source_target_pairs={{0,2},{1,3},{2,0},{3,1},{4,6},{5,7},{6,4},{7,5},{8,10},{9,11},{10,... | collective-permute-start | bytes 159752 | tf_op jit(solution)/shard_map/ppermute | solution.py:278
  34.3 2.5 %shard_map.90 = (bf16[1664,1536]{1,0:T(8,128)(2,1)S(1)}, f32[16,1664]{1,0:T(8,128)S(1)}) custom-call(bf16[1664,8192]{1,0:T(8,128)(2,1)} %refs_1_.3, bf16[16,1664]{1,0:T(8,128)(2,1)S(1)} %get-tuple-element.57.after_ref), custom_call_target="tpu_custom_call" | custom-call | bytes 5111808 | tf_op jit(solution)/shard_map/pallas_call | solution.py:391
  36.9 0.1 collective-permute-done.7
  37.0 1.6 %collective-permute-start.8 = (bf16[16,1664]{1,0:T(8,128)(2,1)S(1)}, bf16[16,1664]{1,0:T(8,128)(2,1)S(1)}, u32[]{:S(2)}, u32[]{:S(2)}) collective-permute-start(bf16[16,1664]{1,0:T(8,128)(2,1)S(1)} %fusion.4.after_ref), channel_id=1, source_target_pairs={{0,4},{1,5},{2,6},{3,7},{4,0},{5,1},{6,2},{7,3},{8,12},{9,13},{10,... | collective-permute-start | bytes 159752 | tf_op jit(solution)/shard_map/ppermute | solution.py:278
  38.6 2.5 %shard_map.91 = (bf16[1664,1536]{1,0:T(8,128)(2,1)S(1)}, f32[16,1664]{1,0:T(8,128)S(1)}) custom-call(bf16[1664,8192]{1,0:T(8,128)(2,1)} %refs_1_.3, bf16[16,1664]{1,0:T(8,128)(2,1)S(1)} %fusion.4.after_ref), custom_call_target="tpu_custom_call" | custom-call | bytes 5111808 | tf_op jit(solution)/shard_map/pallas_call | solution.py:391
  41.2 0.0 collective-permute-done.8
  41.2 2.7 %collective-permute-start.9 = (bf16[16,1664]{1,0:T(8,128)(2,1)S(1)}, bf16[16,1664]{1,0:T(8,128)(2,1)S(1)}, u32[]{:S(2)}, u32[]{:S(2)}) collective-permute-start(bf16[16,1664]{1,0:T(8,128)(2,1)S(1)} %get-tuple-element.55.after_ref), channel_id=1, source_target_pairs={{0,8},{1,9},{2,10},{3,11},{4,12},{5,13},{6,14},{7,15},{8,0},{9,1},... | collective-permute-start | bytes 159752 | tf_op jit(solution)/shard_map/ppermute | solution.py:278
  43.9 3.1 %shard_map.92 = (bf16[1664,2048]{1,0:T(8,128)(2,1)S(1)}, f32[16,1664]{1,0:T(8,128)S(1)}) custom-call(bf16[1664,8192]{1,0:T(8,128)(2,1)} %refs_1_.3, bf16[16,1664]{1,0:T(8,128)(2,1)S(1)} %get-tuple-element.55.after_ref), custom_call_target="tpu_custom_call" | custom-call | bytes 6815744 | tf_op jit(solution)/shard_map/pallas_call | solution.py:391
  47.0 0.0 collective-permute-done.9
  47.0 0.0 copy-start
  47.0 2.5 %shard_map.93 = (f32[8,1,64,128]{3,2,1,0:T(8,128)S(1)}, bf16[8,1,64,128]{3,2,1,0:T(8,128)(2,1)S(1)}) custom-call(f32[16,1664]{1,0:T(8,128)S(1)} %convert_add_fusion.1.refs_0_, bf16[1664,8192]{1,0:T(8,128)(2,1)} %refs_1_.3, bf16[1664,512]{1,0:T(8,128)(2,1)S(1)} %get-tuple-element.48.refs_2_, bf16[1664,2560]{1,0:T(8,128)(2,1)S(1)} %get-tuple-element.49.refs_3_, ...), custom_call_target="tpu_custom_call" | custom-call | flops 436207616 | bytes 13631488 | tf_op jit(solution)/shard_map/pallas_call | solution.py:412
  49.5 0.1 collective-permute-start.10
  49.6 1.3 %collective-permute-done.10 = bf16[8,1,64,128]{3,2,1,0:T(8,128)(2,1)S(1)} collective-permute-done((bf16[8,1,64,128]{3,2,1,0:T(8,128)(2,1)S(1)}, bf16[8,1,64,128]{3,2,1,0:T(8,128)(2,1)S(1)}, u32[]{:S(2)}, u32[]{:S(2)}) %collective-permute-start.10) | collective-permute-done | bytes 131104 | tf_op jit(solution)/shard_map/ppermute | solution.py:278
  51.0 1.6 %collective-permute-start.11 = (bf16[4,1,64,128]{3,2,1,0:T(8,128)(2,1)S(1)}, bf16[4,1,64,128]{3,2,1,0:T(8,128)(2,1)S(1)}, u32[]{:S(2)}, u32[]{:S(2)}) collective-permute-start(bf16[4,1,64,128]{3,2,1,0:T(8,128)(2,1)S(1)} %slice.45), channel_id=1, source_target_pairs={{0,2},{1,3},{2,0},{3,1},{4,6},{5,7},{6,4},{7,5},{8,10},{9,11},{10,... | collective-permute-start | bytes 196616 | tf_op jit(solution)/shard_map/ppermute | solution.py:278
  52.5 2.8 %collective-permute-done.11 = bf16[4,1,64,128]{3,2,1,0:T(8,128)(2,1)S(1)} collective-permute-done((bf16[4,1,64,128]{3,2,1,0:T(8,128)(2,1)S(1)}, bf16[4,1,64,128]{3,2,1,0:T(8,128)(2,1)S(1)}, u32[]{:S(2)}, u32[]{:S(2)}) %collective-permute-start.11) | collective-permute-done | bytes 65568 | tf_op jit(solution)/shard_map/ppermute | solution.py:278
  55.3 1.6 %collective-permute-start.12 = (bf16[2,1,64,128]{3,2,1,0:T(8,128)(2,1)S(1)}, bf16[2,1,64,128]{3,2,1,0:T(8,128)(2,1)S(1)}, u32[]{:S(2)}, u32[]{:S(2)}) collective-permute-start(bf16[2,1,64,128]{3,2,1,0:T(8,128)(2,1)S(1)} %slice.46), channel_id=1, source_target_pairs={{0,4},{1,5},{2,6},{3,7},{4,0},{5,1},{6,2},{7,3},{8,12},{9,13},{10,... | collective-permute-start | bytes 98312 | tf_op jit(solution)/shard_map/ppermute | solution.py:278
  57.0 2.3 %collective-permute-done.12 = bf16[2,1,64,128]{3,2,1,0:T(8,128)(2,1)S(1)} collective-permute-done((bf16[2,1,64,128]{3,2,1,0:T(8,128)(2,1)S(1)}, bf16[2,1,64,128]{3,2,1,0:T(8,128)(2,1)S(1)}, u32[]{:S(2)}, u32[]{:S(2)}) %collective-permute-start.12) | collective-permute-done | bytes 32800 | tf_op jit(solution)/shard_map/ppermute | solution.py:278
  59.3 2.1 %collective-permute-start.13 = (bf16[1,1,64,128]{3,2,1,0:T(8,128)(2,1)S(1)}, bf16[1,1,64,128]{3,2,1,0:T(8,128)(2,1)S(1)}, u32[]{:S(2)}, u32[]{:S(2)}) collective-permute-start(bf16[1,1,64,128]{3,2,1,0:T(8,128)(2,1)S(1)} %slice.47), channel_id=1, source_target_pairs={{0,8},{1,9},{2,10},{3,11},{4,12},{5,13},{6,14},{7,15},{8,0},{9,1},... | collective-permute-start | bytes 49160 | tf_op jit(solution)/shard_map/ppermute | solution.py:278
  61.4 2.6 %collective-permute-done.13 = bf16[1,1,64,128]{3,2,1,0:T(8,128)(2,1)S(1)} collective-permute-done((bf16[1,1,64,128]{3,2,1,0:T(8,128)(2,1)S(1)}, bf16[1,1,64,128]{3,2,1,0:T(8,128)(2,1)S(1)}, u32[]{:S(2)}, u32[]{:S(2)}) %collective-permute-start.13) | collective-permute-done | bytes 16416 | tf_op jit(solution)/shard_map/ppermute | solution.py:278
  64.0 0.0 copy-done
  64.0 0.6 convert_element_type.54
  (18 shorter events, 0.3 us)
Async XLA Ops:
  0.0 5.1 %collective-permute-start = (bf16[1,8192]{1,0:T(2,128)(2,1)}, bf16[1,8192]{1,0:T(2,128)(2,1)S(1)}, u32[]{:S(2)}, u32[]{:S(2)}) collective-permute-start(bf16[1,8192]{1,0:T(2,128)(2,1)} %after_ref.1), channel_id=1, source_target_pairs={{0,16},{16,0},{1,17},{17,1},{2,18},{18,2},{3,19},{19,3},{4,20},{20... | collective-permute-start | bytes 49160 | tf_op jit(solution)/shard_map/ppermute | solution.py:287
  5.1 5.2 %collective-permute-start.1 = (bf16[2,1,32,128]{3,2,1,0:T(8,128)(2,1)S(1)}, bf16[2,1,32,128]{3,2,1,0:T(8,128)(2,1)S(1)}, u32[]{:S(2)}, u32[]{:S(2)}) collective-permute-start(bf16[2,1,32,128]{3,2,1,0:T(8,128)(2,1)S(1)} %shard_map.83.after_ref), channel_id=1, source_target_pairs={{0,8},{1,9},{2,10},{3,11},{4,12},{5,13},{6,14},{7,15},{8,0},{9,1},... | collective-permute-start | bytes 49160 | tf_op jit(solution)/shard_map/ppermute | solution.py:278
  10.3 4.0 %collective-permute-start.2 = (bf16[4,1,32,128]{3,2,1,0:T(8,128)(2,1)S(1)}, bf16[4,1,32,128]{3,2,1,0:T(8,128)(2,1)S(1)}, u32[]{:S(2)}, u32[]{:S(2)}) collective-permute-start(bf16[4,1,32,128]{3,2,1,0:T(8,128)(2,1)S(1)} %constant_dynamic-update-slice_fusion.after_ref), channel_id=1, source_target_pairs={{0,4},{1,5},{2,6},{3,7},{4,0},{5,1},{6,2},{7,3},{8,12},{9,13},{10,... | collective-permute-start | bytes 98312 | tf_op jit(solution)/shard_map/ppermute | solution.py:278
  14.3 4.3 %collective-permute-start.3 = (bf16[8,1,32,128]{3,2,1,0:T(8,128)(2,1)S(1)}, bf16[8,1,32,128]{3,2,1,0:T(8,128)(2,1)S(1)}, u32[]{:S(2)}, u32[]{:S(2)}) collective-permute-start(bf16[8,1,32,128]{3,2,1,0:T(8,128)(2,1)S(1)} %constant_dynamic-update-slice_fusion.2.after_ref), channel_id=1, source_target_pairs={{0,2},{1,3},{2,0},{3,1},{4,6},{5,7},{6,4},{7,5},{8,10},{9,11},{10,... | collective-permute-start | bytes 196616 | tf_op jit(solution)/shard_map/ppermute | solution.py:278
  18.6 1.4 %collective-permute-start.4 = (bf16[16,1,32,128]{3,2,1,0:T(8,128)(2,1)S(1)}, bf16[16,1,32,128]{3,2,1,0:T(8,128)(2,1)S(1)}, u32[]{:S(2)}, u32[]{:S(2)}) collective-permute-start(bf16[16,1,32,128]{3,2,1,0:T(8,128)(2,1)S(1)} %pad_maximum_fusion.1), channel_id=1, source_target_pairs={{0,1},{1,0},{2,3},{3,2},{4,5},{5,4},{6,7},{7,6},{8,9},{9,8},{10,11... | collective-permute-start | bytes 393224 | tf_op jit(solution)/shard_map/ppermute | solution.py:278
  25.8 5.2 %collective-permute-start.5 = (bf16[2,16,1664]{2,1,0:T(8,128)(2,1)S(1)}, bf16[2,16,1664]{2,1,0:T(8,128)(2,1)S(1)}, u32[]{:S(2)}, u32[]{:S(2)}) collective-permute-start(bf16[2,16,1664]{2,1,0:T(8,128)(2,1)S(1)} %bitcast.12), channel_id=1, source_target_pairs={{0,16},{16,0},{1,17},{17,1},{2,18},{18,2},{3,19},{19,3},{4,20},{20... | collective-permute-start | bytes 319496 | tf_op jit(solution)/shard_map/ppermute | solution.py:287
  31.4 1.3 %collective-permute-start.6 = (bf16[16,1664]{1,0:T(8,128)(2,1)S(1)}, bf16[16,1664]{1,0:T(8,128)(2,1)S(1)}, u32[]{:S(2)}, u32[]{:S(2)}) collective-permute-start(bf16[16,1664]{1,0:T(8,128)(2,1)S(1)} %get-tuple-element.44), channel_id=1, source_target_pairs={{0,1},{1,0},{2,3},{3,2},{4,5},{5,4},{6,7},{7,6},{8,9},{9,8},{10,11... | collective-permute-start | bytes 159752 | tf_op jit(solution)/shard_map/ppermute | solution.py:278
  32.8 4.2 %collective-permute-start.7 = (bf16[16,1664]{1,0:T(8,128)(2,1)S(1)}, bf16[16,1664]{1,0:T(8,128)(2,1)S(1)}, u32[]{:S(2)}, u32[]{:S(2)}) collective-permute-start(bf16[16,1664]{1,0:T(8,128)(2,1)S(1)} %get-tuple-element.57.after_ref), channel_id=1, source_target_pairs={{0,2},{1,3},{2,0},{3,1},{4,6},{5,7},{6,4},{7,5},{8,10},{9,11},{10,... | collective-permute-start | bytes 159752 | tf_op jit(solution)/shard_map/ppermute | solution.py:278
  37.0 4.2 %collective-permute-start.8 = (bf16[16,1664]{1,0:T(8,128)(2,1)S(1)}, bf16[16,1664]{1,0:T(8,128)(2,1)S(1)}, u32[]{:S(2)}, u32[]{:S(2)}) collective-permute-start(bf16[16,1664]{1,0:T(8,128)(2,1)S(1)} %fusion.4.after_ref), channel_id=1, source_target_pairs={{0,4},{1,5},{2,6},{3,7},{4,0},{5,1},{6,2},{7,3},{8,12},{9,13},{10,... | collective-permute-start | bytes 159752 | tf_op jit(solution)/shard_map/ppermute | solution.py:278
  41.2 5.7 %collective-permute-start.9 = (bf16[16,1664]{1,0:T(8,128)(2,1)S(1)}, bf16[16,1664]{1,0:T(8,128)(2,1)S(1)}, u32[]{:S(2)}, u32[]{:S(2)}) collective-permute-start(bf16[16,1664]{1,0:T(8,128)(2,1)S(1)} %get-tuple-element.55.after_ref), channel_id=1, source_target_pairs={{0,8},{1,9},{2,10},{3,11},{4,12},{5,13},{6,14},{7,15},{8,0},{9,1},... | collective-permute-start | bytes 159752 | tf_op jit(solution)/shard_map/ppermute | solution.py:278
  47.0 17.0 %copy-start = (f32[8192]{0:T(1024)S(1)}, f32[8192]{0:T(1024)}, u32[]{:S(2)}) copy-start(f32[8192]{0:T(1024)} %param.14) | copy-start | bytes 98308
  49.5 1.4 %collective-permute-start.10 = (bf16[8,1,64,128]{3,2,1,0:T(8,128)(2,1)S(1)}, bf16[8,1,64,128]{3,2,1,0:T(8,128)(2,1)S(1)}, u32[]{:S(2)}, u32[]{:S(2)}) collective-permute-start(bf16[8,1,64,128]{3,2,1,0:T(8,128)(2,1)S(1)} %get-tuple-element.54), channel_id=1, source_target_pairs={{0,1},{1,0},{2,3},{3,2},{4,5},{5,4},{6,7},{7,6},{8,9},{9,8},{10,11... | collective-permute-start | bytes 393224 | tf_op jit(solution)/shard_map/ppermute | solution.py:278
  51.0 4.3 %collective-permute-start.11 = (bf16[4,1,64,128]{3,2,1,0:T(8,128)(2,1)S(1)}, bf16[4,1,64,128]{3,2,1,0:T(8,128)(2,1)S(1)}, u32[]{:S(2)}, u32[]{:S(2)}) collective-permute-start(bf16[4,1,64,128]{3,2,1,0:T(8,128)(2,1)S(1)} %slice.45), channel_id=1, source_target_pairs={{0,2},{1,3},{2,0},{3,1},{4,6},{5,7},{6,4},{7,5},{8,10},{9,11},{10,... | collective-permute-start | bytes 196616 | tf_op jit(solution)/shard_map/ppermute | solution.py:278
  55.3 4.0 %collective-permute-start.12 = (bf16[2,1,64,128]{3,2,1,0:T(8,128)(2,1)S(1)}, bf16[2,1,64,128]{3,2,1,0:T(8,128)(2,1)S(1)}, u32[]{:S(2)}, u32[]{:S(2)}) collective-permute-start(bf16[2,1,64,128]{3,2,1,0:T(8,128)(2,1)S(1)} %slice.46), channel_id=1, source_target_pairs={{0,4},{1,5},{2,6},{3,7},{4,0},{5,1},{6,2},{7,3},{8,12},{9,13},{10,... | collective-permute-start | bytes 98312 | tf_op jit(solution)/shard_map/ppermute | solution.py:278
  59.3 4.7 %collective-permute-start.13 = (bf16[1,1,64,128]{3,2,1,0:T(8,128)(2,1)S(1)}, bf16[1,1,64,128]{3,2,1,0:T(8,128)(2,1)S(1)}, u32[]{:S(2)}, u32[]{:S(2)}) collective-permute-start(bf16[1,1,64,128]{3,2,1,0:T(8,128)(2,1)S(1)} %slice.47), channel_id=1, source_target_pairs={{0,8},{1,9},{2,10},{3,11},{4,12},{5,13},{6,14},{7,15},{8,0},{9,1},... | collective-permute-start | bytes 49160 | tf_op jit(solution)/shard_map/ppermute | solution.py:278

commit v6 on v5

--- a/solution.py
+++ b/solution.py
@@ -17,7 +17,7 @@
 ROWS = (2, 2, 2, 2)
 SPAN = 512
 AHEAD = 8
-SPANS = (5, 3, 3, 4)
+SPANS = (5, 3, 3, 3)
 
 VMEM = pl.BlockSpec(memory_space=pltpu.VMEM)
 HBM = pl.BlockSpec(memory_space=pltpu.HBM)
@@ -323,11 +323,11 @@
                     out_shape=(
                         pltpu.VMEM((ROWS[-1] * CHUNK, units), jnp.bfloat16),
                         pltpu.VMEM(pieces.shape, pieces.dtype),
-                        pltpu.VMEM((units, SPAN), jnp.bfloat16),
+                        pltpu.VMEM((units, 2 * SPAN), jnp.bfloat16),
                     ),
                     in_specs=[HBM, ANY, HBM],
                     out_specs=(VMEM, VMEM, VMEM),
-                    scratch_shapes=[pltpu.SemaphoreType.DMA((ROWS[-1] + 1,)), pltpu.SemaphoreType.DMA((1,))],
+                    scratch_shapes=[pltpu.SemaphoreType.DMA((ROWS[-1] + 1,)), pltpu.SemaphoreType.DMA((2,))],
                     compiler_params=pltpu.CompilerParams(vmem_limit_bytes=2 * MIB),
                     cost_estimate=cost(2 * ROWS[-1] * CHUNK * units + 2 * SPAN * units),
                 )(in_hbm(gate_codes), pieces, in_hbm(down_codes))
@@ -364,7 +364,7 @@
     others = [by_part(send[step - 1], -step) for step in range(1, parts)]
     columns = SPANS[0] * SPAN
     part, small = pl.pallas_call(
-        functools.partial(columns_small_kernel, SPAN, SPAN),
+        functools.partial(columns_small_kernel, 2 * SPAN, SPAN),
         out_shape=(pltpu.VMEM((units, columns), jnp.bfloat16), pltpu.VMEM(hadamard.shape, hadamard.dtype)),
         in_specs=[HBM, ANY, HBM],
         out_specs=(VMEM, VMEM),
@@ -373,7 +373,7 @@
         cost_estimate=cost(2 * units * columns),
     )(in_hbm(down_codes), send, in_hbm(hadamard))
     held = [down_part, part]
-    first = SPAN + columns
+    first = 2 * SPAN + columns
 
     turned, send = pl.pallas_call(
         rotate_kernel,

time: 64.8 us -> 64.7 us (level)
  transfers between devices with their start and end apart: 14 -> 14, of which waited for: 10 -> 9; matrix products, arithmetic and copies ran while one was open for 0% -> 0% of each run, Pallas kernels for 31% -> 31%
where the time goes in v6:
time: 64.7 us; the launch traced here: 64.5 us
  Pallas kernels  29 us (45%)
  starting transfers between devices  22 us (34%)
  waiting for transfers between devices  12.3 us (19%)
  local copies, waits for them, and re-layouts  0.69 us (1%)
    ppermute x12, starting transfers between devices, swap(): return lax.ppermute(value, 'hx', [(at, at ^ bit) for at in range(devices)])  17.5 us
    ppermute x12, waiting for transfers between devices, swap(): return lax.ppermute(value, 'hx', [(at, at ^ bit) for at in range(devices)])  12.2 us
    pallas_call x3, Pallas kernels, per_device(): pl.pallas_call(functools.partial(columns_kernel, first, SPAN, bit), out_s...  7.59 us
    pallas_call x3, Pallas kernels, some_rows(): pl.pallas_call(functools.partial(rows_kernel, first, CHUNK), out_shape=(p...  6.02 us
    pallas_call x1, Pallas kernels, per_device(): pl.pallas_call(functools.partial(hidden_kernel, group, parts, gathered, e...  5.75 us
    ppermute x2, starting transfers between devices, by_part(): lax.ppermute(value, 'groups', [(at, (at + step) % parts) for at in range(...  4.57 us
    pallas_call x1, Pallas kernels, per_device(): pl.pallas_call(functools.partial(columns_small_kernel, 2 * SPAN, SPAN), o...  3.59 us
    pallas_call x1, Pallas kernels, per_device(): pl.pallas_call(functools.partial(rows_columns_kernel, first, CHUNK, SPAN)...  3.08 us
  transfers between devices with their start and end apart: 14, of which 9 were waited for; matrix products, arithmetic and copies ran while one was open for 0% of the time, Pallas kernels for 31%

profile of v6, /device:TPU:0, one launch (start us, length us, event | category | flops | bytes accessed | tf_op | source)
XLA Modules:
  0.0 64.5 jit_solution(1316323063002049874)
XLA Ops:
  0.0 3.0 %collective-permute-start = (bf16[1,8192]{1,0:T(2,128)(2,1)}, bf16[1,8192]{1,0:T(2,128)(2,1)S(1)}, u32[]{:S(2)}, u32[]{:S(2)}) collective-permute-start(bf16[1,8192]{1,0:T(2,128)(2,1)} %after_ref.1), channel_id=1, source_target_pairs={{0,16},{16,0},{1,17},{17,1},{2,18},{18,2},{3,19},{19,3},{4,20},{20... | collective-permute-start | bytes 49160 | tf_op jit(solution)/shard_map/ppermute | solution.py:287
  3.0 2.0 %shard_map.82 = (bf16[1024,1664]{1,0:T(8,128)(2,1)S(1)}, bf16[1,8192]{1,0:T(2,128)(2,1)S(1)}) custom-call(bf16[8192,1664]{1,0:T(8,128)(2,1)} %codes_ref.11, bf16[1,8192]{1,0:T(2,128)(2,1)} %after_ref.1), custom_call_target="tpu_custom_call" | custom-call | bytes 3407872 | tf_op jit(solution)/shard_map/pallas_call | solution.py:291
  5.0 0.1 collective-permute-done.refs_0_
  5.1 3.2 %collective-permute-start.1 = (bf16[2,1,32,128]{3,2,1,0:T(8,128)(2,1)S(1)}, bf16[2,1,32,128]{3,2,1,0:T(8,128)(2,1)S(1)}, u32[]{:S(2)}, u32[]{:S(2)}) collective-permute-start(bf16[2,1,32,128]{3,2,1,0:T(8,128)(2,1)S(1)} %shard_map.83.after_ref), channel_id=1, source_target_pairs={{0,8},{1,9},{2,10},{3,11},{4,12},{5,13},{6,14},{7,15},{8,0},{9,1},... | collective-permute-start | bytes 49160 | tf_op jit(solution)/shard_map/ppermute | solution.py:278
  8.3 2.0 %shard_map.84 = (bf16[1024,1664]{1,0:T(8,128)(2,1)S(1)}, bf16[2,1,32,128]{3,2,1,0:T(8,128)(2,1)S(1)}) custom-call(bf16[8192,1664]{1,0:T(8,128)(2,1)} %codes_ref.11, bf16[2,1,32,128]{3,2,1,0:T(8,128)(2,1)S(1)} %shard_map.83.after_ref), custom_call_target="tpu_custom_call" | custom-call | bytes 3407872 | tf_op jit(solution)/shard_map/pallas_call | solution.py:291
  10.3 0.0 collective-permute-done.1
  10.3 1.6 %collective-permute-start.2 = (bf16[4,1,32,128]{3,2,1,0:T(8,128)(2,1)S(1)}, bf16[4,1,32,128]{3,2,1,0:T(8,128)(2,1)S(1)}, u32[]{:S(2)}, u32[]{:S(2)}) collective-permute-start(bf16[4,1,32,128]{3,2,1,0:T(8,128)(2,1)S(1)} %constant_dynamic-update-slice_fusion.after_ref), channel_id=1, source_target_pairs={{0,4},{1,5},{2,6},{3,7},{4,0},{5,1},{6,2},{7,3},{8,12},{9,13},{10,... | collective-permute-start | bytes 98312 | tf_op jit(solution)/shard_map/ppermute | solution.py:278
  11.9 2.0 %shard_map.85 = (bf16[1024,1664]{1,0:T(8,128)(2,1)S(1)}, bf16[4,1,32,128]{3,2,1,0:T(8,128)(2,1)S(1)}) custom-call(bf16[8192,1664]{1,0:T(8,128)(2,1)} %codes_ref.11, bf16[4,1,32,128]{3,2,1,0:T(8,128)(2,1)S(1)} %constant_dynamic-update-slice_fusion.after_ref), custom_call_target="tpu_custom_call" | custom-call | bytes 3407872 | tf_op jit(solution)/shard_map/pallas_call | solution.py:291
  14.0 0.3 collective-permute-done.2
  14.3 1.5 %collective-permute-start.3 = (bf16[8,1,32,128]{3,2,1,0:T(8,128)(2,1)S(1)}, bf16[8,1,32,128]{3,2,1,0:T(8,128)(2,1)S(1)}, u32[]{:S(2)}, u32[]{:S(2)}) collective-permute-start(bf16[8,1,32,128]{3,2,1,0:T(8,128)(2,1)S(1)} %constant_dynamic-update-slice_fusion.2.after_ref), channel_id=1, source_target_pairs={{0,2},{1,3},{2,0},{3,1},{4,6},{5,7},{6,4},{7,5},{8,10},{9,11},{10,... | collective-permute-start | bytes 196616 | tf_op jit(solution)/shard_map/ppermute | solution.py:278
  15.8 3.1 %shard_map.86 = (bf16[1024,1664]{1,0:T(8,128)(2,1)S(1)}, bf16[8,1,32,128]{3,2,1,0:T(8,128)(2,1)S(1)}, bf16[1664,1024]{1,0:T(8,128)(2,1)S(1)}) custom-call(bf16[8192,1664]{1,0:T(8,128)(2,1)} %codes_ref.11, bf16[8,1,32,128]{3,2,1,0:T(8,128)(2,1)S(1)} %constant_dynamic-update-slice_fusion.2.after_ref, bf16[1664,8192]{1,0:T(8,128)(2,1)} %refs_1_.3), custom_call_target="tpu_custom_call" | custom-call | bytes 5111808 | tf_op jit(solution)/shard_map/pallas_call | solution.py:321
  18.9 0.0 collective-permute-done.3
  18.9 0.1 collective-permute-start.4
  19.0 1.3 %collective-permute-done.4 = bf16[16,1,32,128]{3,2,1,0:T(8,128)(2,1)S(1)} collective-permute-done((bf16[16,1,32,128]{3,2,1,0:T(8,128)(2,1)S(1)}, bf16[16,1,32,128]{3,2,1,0:T(8,128)(2,1)S(1)}, u32[]{:S(2)}, u32[]{:S(2)}) %collective-permute-start.4) | collective-permute-done | bytes 131104 | tf_op jit(solution)/shard_map/ppermute | solution.py:278
  20.3 5.7 %shard_map.87 = (f32[16,1664]{1,0:T(8,128)S(1)}, f32[16,1664]{1,0:T(8,128)S(1)}, bf16[1,2,16,1664]{3,2,1,0:T(8,128)(2,1)S(1)}, f32[1,16,1664]{2,1,0:T(8,128)S(1)}) custom-call(bf16[32,1,32,128]{3,2,1,0:T(8,128)(2,1)S(1)} %pad_maximum_fusion.refs_0_, f32[64,1664]{1,0:T(8,128)} %refs_1_.2, bf16[8192,1664]{1,0:T(8,128)(2,1)} %refs_2_.1, f32[64,1664]{1,0:T(8,128)} %refs_3_.1, ...), custom_call_target="tpu_custom_call" | custom-call | flops 872415232 | bytes 13631488 | tf_op jit(solution)/shard_map/pallas_call | solution.py:340
  26.1 1.6 %collective-permute-start.5 = (bf16[2,16,1664]{2,1,0:T(8,128)(2,1)S(1)}, bf16[2,16,1664]{2,1,0:T(8,128)(2,1)S(1)}, u32[]{:S(2)}, u32[]{:S(2)}) collective-permute-start(bf16[2,16,1664]{2,1,0:T(8,128)(2,1)S(1)} %bitcast.12), channel_id=1, source_target_pairs={{0,16},{16,0},{1,17},{17,1},{2,18},{18,2},{3,19},{19,3},{4,20},{20... | collective-permute-start | bytes 319496 | tf_op jit(solution)/shard_map/ppermute | solution.py:287
  27.7 3.6 %shard_map.88 = (bf16[1664,2560]{1,0:T(8,128)(2,1)S(1)}, s32[52,52]{1,0:T(8,128)S(1)}) custom-call(bf16[1664,8192]{1,0:T(8,128)(2,1)} %refs_1_.3, bf16[1,2,16,1664]{3,2,1,0:T(8,128)(2,1)S(1)} %get-tuple-element.40.after_ref, s32[52,52]{1,0:T(8,128)} %hadamard_ref.1), custom_call_target="tpu_custom_call" | custom-call | bytes 8519680 | tf_op jit(solution)/shard_map/pallas_call | solution.py:366
  31.3 0.0 collective-permute-done.5.refs_0_
  31.3 0.5 shard_map.89
  31.8 0.1 collective-permute-start.6
  31.9 1.2 %collective-permute-done.6 = bf16[16,1664]{1,0:T(8,128)(2,1)S(1)} collective-permute-done((bf16[16,1664]{1,0:T(8,128)(2,1)S(1)}, bf16[16,1664]{1,0:T(8,128)(2,1)S(1)}, u32[]{:S(2)}, u32[]{:S(2)}) %collective-permute-start.6) | collective-permute-done | bytes 53280 | tf_op jit(solution)/shard_map/ppermute | solution.py:278
  33.1 1.2 %collective-permute-start.7 = (bf16[16,1664]{1,0:T(8,128)(2,1)S(1)}, bf16[16,1664]{1,0:T(8,128)(2,1)S(1)}, u32[]{:S(2)}, u32[]{:S(2)}) collective-permute-start(bf16[16,1664]{1,0:T(8,128)(2,1)S(1)} %get-tuple-element.57.after_ref), channel_id=1, source_target_pairs={{0,2},{1,3},{2,0},{3,1},{4,6},{5,7},{6,4},{7,5},{8,10},{9,11},{10,... | collective-permute-start | bytes 159752 | tf_op jit(solution)/shard_map/ppermute | solution.py:278
  34.3 2.5 %shard_map.90 = (bf16[1664,1536]{1,0:T(8,128)(2,1)S(1)}, f32[16,1664]{1,0:T(8,128)S(1)}) custom-call(bf16[1664,8192]{1,0:T(8,128)(2,1)} %refs_1_.3, bf16[16,1664]{1,0:T(8,128)(2,1)S(1)} %get-tuple-element.57.after_ref), custom_call_target="tpu_custom_call" | custom-call | bytes 5111808 | tf_op jit(solution)/shard_map/pallas_call | solution.py:391
  36.9 0.5 collective-permute-done.7
  37.3 1.6 %collective-permute-start.8 = (bf16[16,1664]{1,0:T(8,128)(2,1)S(1)}, bf16[16,1664]{1,0:T(8,128)(2,1)S(1)}, u32[]{:S(2)}, u32[]{:S(2)}) collective-permute-start(bf16[16,1664]{1,0:T(8,128)(2,1)S(1)} %fusion.4.after_ref), channel_id=1, source_target_pairs={{0,4},{1,5},{2,6},{3,7},{4,0},{5,1},{6,2},{7,3},{8,12},{9,13},{10,... | collective-permute-start | bytes 159752 | tf_op jit(solution)/shard_map/ppermute | solution.py:278
  39.0 2.5 %shard_map.91 = (bf16[1664,1536]{1,0:T(8,128)(2,1)S(1)}, f32[16,1664]{1,0:T(8,128)S(1)}) custom-call(bf16[1664,8192]{1,0:T(8,128)(2,1)} %refs_1_.3, bf16[16,1664]{1,0:T(8,128)(2,1)S(1)} %fusion.4.after_ref), custom_call_target="tpu_custom_call" | custom-call | bytes 5111808 | tf_op jit(solution)/shard_map/pallas_call | solution.py:391
  41.5 0.0 collective-permute-done.8
  41.6 2.7 %collective-permute-start.9 = (bf16[16,1664]{1,0:T(8,128)(2,1)S(1)}, bf16[16,1664]{1,0:T(8,128)(2,1)S(1)}, u32[]{:S(2)}, u32[]{:S(2)}) collective-permute-start(bf16[16,1664]{1,0:T(8,128)(2,1)S(1)} %get-tuple-element.55.after_ref), channel_id=1, source_target_pairs={{0,8},{1,9},{2,10},{3,11},{4,12},{5,13},{6,14},{7,15},{8,0},{9,1},... | collective-permute-start | bytes 159752 | tf_op jit(solution)/shard_map/ppermute | solution.py:278
  44.2 2.5 %shard_map.92 = (bf16[1664,1536]{1,0:T(8,128)(2,1)S(1)}, f32[16,1664]{1,0:T(8,128)S(1)}) custom-call(bf16[1664,8192]{1,0:T(8,128)(2,1)} %refs_1_.3, bf16[16,1664]{1,0:T(8,128)(2,1)S(1)} %get-tuple-element.55.after_ref), custom_call_target="tpu_custom_call" | custom-call | bytes 5111808 | tf_op jit(solution)/shard_map/pallas_call | solution.py:391
  46.8 0.0 collective-permute-done.9
  46.8 0.0 copy-start
  46.8 2.5 %shard_map.93 = (f32[8,1,64,128]{3,2,1,0:T(8,128)S(1)}, bf16[8,1,64,128]{3,2,1,0:T(8,128)(2,1)S(1)}) custom-call(f32[16,1664]{1,0:T(8,128)S(1)} %convert_add_fusion.1.refs_0_, bf16[1664,8192]{1,0:T(8,128)(2,1)} %refs_1_.3, bf16[1664,1024]{1,0:T(8,128)(2,1)S(1)} %get-tuple-element.48.refs_2_, bf16[1664,2560]{1,0:T(8,128)(2,1)S(1)} %get-tuple-element.49.refs_3_, ...), custom_call_target="tpu_custom_call" | custom-call | flops 436207616 | bytes 13631488 | tf_op jit(solution)/shard_map/pallas_call | solution.py:412
  49.3 0.1 collective-permute-start.10
  49.4 1.3 %collective-permute-done.10 = bf16[8,1,64,128]{3,2,1,0:T(8,128)(2,1)S(1)} collective-permute-done((bf16[8,1,64,128]{3,2,1,0:T(8,128)(2,1)S(1)}, bf16[8,1,64,128]{3,2,1,0:T(8,128)(2,1)S(1)}, u32[]{:S(2)}, u32[]{:S(2)}) %collective-permute-start.10) | collective-permute-done | bytes 131104 | tf_op jit(solution)/shard_map/ppermute | solution.py:278
  50.8 1.2 %collective-permute-start.11 = (bf16[4,1,64,128]{3,2,1,0:T(8,128)(2,1)S(1)}, bf16[4,1,64,128]{3,2,1,0:T(8,128)(2,1)S(1)}, u32[]{:S(2)}, u32[]{:S(2)}) collective-permute-start(bf16[4,1,64,128]{3,2,1,0:T(8,128)(2,1)S(1)} %slice.45), channel_id=1, source_target_pairs={{0,2},{1,3},{2,0},{3,1},{4,6},{5,7},{6,4},{7,5},{8,10},{9,11},{10,... | collective-permute-start | bytes 196616 | tf_op jit(solution)/shard_map/ppermute | solution.py:278
  52.0 3.1 %collective-permute-done.11 = bf16[4,1,64,128]{3,2,1,0:T(8,128)(2,1)S(1)} collective-permute-done((bf16[4,1,64,128]{3,2,1,0:T(8,128)(2,1)S(1)}, bf16[4,1,64,128]{3,2,1,0:T(8,128)(2,1)S(1)}, u32[]{:S(2)}, u32[]{:S(2)}) %collective-permute-start.11) | collective-permute-done | bytes 65568 | tf_op jit(solution)/shard_map/ppermute | solution.py:278
  55.2 1.6 %collective-permute-start.12 = (bf16[2,1,64,128]{3,2,1,0:T(8,128)(2,1)S(1)}, bf16[2,1,64,128]{3,2,1,0:T(8,128)(2,1)S(1)}, u32[]{:S(2)}, u32[]{:S(2)}) collective-permute-start(bf16[2,1,64,128]{3,2,1,0:T(8,128)(2,1)S(1)} %slice.46), channel_id=1, source_target_pairs={{0,4},{1,5},{2,6},{3,7},{4,0},{5,1},{6,2},{7,3},{8,12},{9,13},{10,... | collective-permute-start | bytes 98312 | tf_op jit(solution)/shard_map/ppermute | solution.py:278
  56.8 2.3 %collective-permute-done.12 = bf16[2,1,64,128]{3,2,1,0:T(8,128)(2,1)S(1)} collective-permute-done((bf16[2,1,64,128]{3,2,1,0:T(8,128)(2,1)S(1)}, bf16[2,1,64,128]{3,2,1,0:T(8,128)(2,1)S(1)}, u32[]{:S(2)}, u32[]{:S(2)}) %collective-permute-start.12) | collective-permute-done | bytes 32800 | tf_op jit(solution)/shard_map/ppermute | solution.py:278
  59.2 2.6 %collective-permute-start.13 = (bf16[1,1,64,128]{3,2,1,0:T(8,128)(2,1)S(1)}, bf16[1,1,64,128]{3,2,1,0:T(8,128)(2,1)S(1)}, u32[]{:S(2)}, u32[]{:S(2)}) collective-permute-start(bf16[1,1,64,128]{3,2,1,0:T(8,128)(2,1)S(1)} %slice.47), channel_id=1, source_target_pairs={{0,8},{1,9},{2,10},{3,11},{4,12},{5,13},{6,14},{7,15},{8,0},{9,1},... | collective-permute-start | bytes 49160 | tf_op jit(solution)/shard_map/ppermute | solution.py:278
  61.8 2.1 %collective-permute-done.13 = bf16[1,1,64,128]{3,2,1,0:T(8,128)(2,1)S(1)} collective-permute-done((bf16[1,1,64,128]{3,2,1,0:T(8,128)(2,1)S(1)}, bf16[1,1,64,128]{3,2,1,0:T(8,128)(2,1)S(1)}, u32[]{:S(2)}, u32[]{:S(2)}) %collective-permute-start.13) | collective-permute-done | bytes 16416 | tf_op jit(solution)/shard_map/ppermute | solution.py:278
  63.9 0.0 copy-done
  63.9 0.6 convert_element_type.54
  (18 shorter events, 0.3 us)
Async XLA Ops:
  0.0 5.1 %collective-permute-start = (bf16[1,8192]{1,0:T(2,128)(2,1)}, bf16[1,8192]{1,0:T(2,128)(2,1)S(1)}, u32[]{:S(2)}, u32[]{:S(2)}) collective-permute-start(bf16[1,8192]{1,0:T(2,128)(2,1)} %after_ref.1), channel_id=1, source_target_pairs={{0,16},{16,0},{1,17},{17,1},{2,18},{18,2},{3,19},{19,3},{4,20},{20... | collective-permute-start | bytes 49160 | tf_op jit(solution)/shard_map/ppermute | solution.py:287
  5.1 5.2 %collective-permute-start.1 = (bf16[2,1,32,128]{3,2,1,0:T(8,128)(2,1)S(1)}, bf16[2,1,32,128]{3,2,1,0:T(8,128)(2,1)S(1)}, u32[]{:S(2)}, u32[]{:S(2)}) collective-permute-start(bf16[2,1,32,128]{3,2,1,0:T(8,128)(2,1)S(1)} %shard_map.83.after_ref), channel_id=1, source_target_pairs={{0,8},{1,9},{2,10},{3,11},{4,12},{5,13},{6,14},{7,15},{8,0},{9,1},... | collective-permute-start | bytes 49160 | tf_op jit(solution)/shard_map/ppermute | solution.py:278
  10.3 4.0 %collective-permute-start.2 = (bf16[4,1,32,128]{3,2,1,0:T(8,128)(2,1)S(1)}, bf16[4,1,32,128]{3,2,1,0:T(8,128)(2,1)S(1)}, u32[]{:S(2)}, u32[]{:S(2)}) collective-permute-start(bf16[4,1,32,128]{3,2,1,0:T(8,128)(2,1)S(1)} %constant_dynamic-update-slice_fusion.after_ref), channel_id=1, source_target_pairs={{0,4},{1,5},{2,6},{3,7},{4,0},{5,1},{6,2},{7,3},{8,12},{9,13},{10,... | collective-permute-start | bytes 98312 | tf_op jit(solution)/shard_map/ppermute | solution.py:278
  14.3 4.6 %collective-permute-start.3 = (bf16[8,1,32,128]{3,2,1,0:T(8,128)(2,1)S(1)}, bf16[8,1,32,128]{3,2,1,0:T(8,128)(2,1)S(1)}, u32[]{:S(2)}, u32[]{:S(2)}) collective-permute-start(bf16[8,1,32,128]{3,2,1,0:T(8,128)(2,1)S(1)} %constant_dynamic-update-slice_fusion.2.after_ref), channel_id=1, source_target_pairs={{0,2},{1,3},{2,0},{3,1},{4,6},{5,7},{6,4},{7,5},{8,10},{9,11},{10,... | collective-permute-start | bytes 196616 | tf_op jit(solution)/shard_map/ppermute | solution.py:278
  18.9 1.4 %collective-permute-start.4 = (bf16[16,1,32,128]{3,2,1,0:T(8,128)(2,1)S(1)}, bf16[16,1,32,128]{3,2,1,0:T(8,128)(2,1)S(1)}, u32[]{:S(2)}, u32[]{:S(2)}) collective-permute-start(bf16[16,1,32,128]{3,2,1,0:T(8,128)(2,1)S(1)} %pad_maximum_fusion.1), channel_id=1, source_target_pairs={{0,1},{1,0},{2,3},{3,2},{4,5},{5,4},{6,7},{7,6},{8,9},{9,8},{10,11... | collective-permute-start | bytes 393224 | tf_op jit(solution)/shard_map/ppermute | solution.py:278
  26.1 5.2 %collective-permute-start.5 = (bf16[2,16,1664]{2,1,0:T(8,128)(2,1)S(1)}, bf16[2,16,1664]{2,1,0:T(8,128)(2,1)S(1)}, u32[]{:S(2)}, u32[]{:S(2)}) collective-permute-start(bf16[2,16,1664]{2,1,0:T(8,128)(2,1)S(1)} %bitcast.12), channel_id=1, source_target_pairs={{0,16},{16,0},{1,17},{17,1},{2,18},{18,2},{3,19},{19,3},{4,20},{20... | collective-permute-start | bytes 319496 | tf_op jit(solution)/shard_map/ppermute | solution.py:287
  31.8 1.3 %collective-permute-start.6 = (bf16[16,1664]{1,0:T(8,128)(2,1)S(1)}, bf16[16,1664]{1,0:T(8,128)(2,1)S(1)}, u32[]{:S(2)}, u32[]{:S(2)}) collective-permute-start(bf16[16,1664]{1,0:T(8,128)(2,1)S(1)} %get-tuple-element.44), channel_id=1, source_target_pairs={{0,1},{1,0},{2,3},{3,2},{4,5},{5,4},{6,7},{7,6},{8,9},{9,8},{10,11... | collective-permute-start | bytes 159752 | tf_op jit(solution)/shard_map/ppermute | solution.py:278
  33.1 4.2 %collective-permute-start.7 = (bf16[16,1664]{1,0:T(8,128)(2,1)S(1)}, bf16[16,1664]{1,0:T(8,128)(2,1)S(1)}, u32[]{:S(2)}, u32[]{:S(2)}) collective-permute-start(bf16[16,1664]{1,0:T(8,128)(2,1)S(1)} %get-tuple-element.57.after_ref), channel_id=1, source_target_pairs={{0,2},{1,3},{2,0},{3,1},{4,6},{5,7},{6,4},{7,5},{8,10},{9,11},{10,... | collective-permute-start | bytes 159752 | tf_op jit(solution)/shard_map/ppermute | solution.py:278
  37.3 4.2 %collective-permute-start.8 = (bf16[16,1664]{1,0:T(8,128)(2,1)S(1)}, bf16[16,1664]{1,0:T(8,128)(2,1)S(1)}, u32[]{:S(2)}, u32[]{:S(2)}) collective-permute-start(bf16[16,1664]{1,0:T(8,128)(2,1)S(1)} %fusion.4.after_ref), channel_id=1, source_target_pairs={{0,4},{1,5},{2,6},{3,7},{4,0},{5,1},{6,2},{7,3},{8,12},{9,13},{10,... | collective-permute-start | bytes 159752 | tf_op jit(solution)/shard_map/ppermute | solution.py:278
  41.6 5.2 %collective-permute-start.9 = (bf16[16,1664]{1,0:T(8,128)(2,1)S(1)}, bf16[16,1664]{1,0:T(8,128)(2,1)S(1)}, u32[]{:S(2)}, u32[]{:S(2)}) collective-permute-start(bf16[16,1664]{1,0:T(8,128)(2,1)S(1)} %get-tuple-element.55.after_ref), channel_id=1, source_target_pairs={{0,8},{1,9},{2,10},{3,11},{4,12},{5,13},{6,14},{7,15},{8,0},{9,1},... | collective-permute-start | bytes 159752 | tf_op jit(solution)/shard_map/ppermute | solution.py:278
  46.8 17.1 %copy-start = (f32[8192]{0:T(1024)S(1)}, f32[8192]{0:T(1024)}, u32[]{:S(2)}) copy-start(f32[8192]{0:T(1024)} %param.14) | copy-start | bytes 98308
  49.3 1.4 %collective-permute-start.10 = (bf16[8,1,64,128]{3,2,1,0:T(8,128)(2,1)S(1)}, bf16[8,1,64,128]{3,2,1,0:T(8,128)(2,1)S(1)}, u32[]{:S(2)}, u32[]{:S(2)}) collective-permute-start(bf16[8,1,64,128]{3,2,1,0:T(8,128)(2,1)S(1)} %get-tuple-element.54), channel_id=1, source_target_pairs={{0,1},{1,0},{2,3},{3,2},{4,5},{5,4},{6,7},{7,6},{8,9},{9,8},{10,11... | collective-permute-start | bytes 393224 | tf_op jit(solution)/shard_map/ppermute | solution.py:278
  50.8 4.3 %collective-permute-start.11 = (bf16[4,1,64,128]{3,2,1,0:T(8,128)(2,1)S(1)}, bf16[4,1,64,128]{3,2,1,0:T(8,128)(2,1)S(1)}, u32[]{:S(2)}, u32[]{:S(2)}) collective-permute-start(bf16[4,1,64,128]{3,2,1,0:T(8,128)(2,1)S(1)} %slice.45), channel_id=1, source_target_pairs={{0,2},{1,3},{2,0},{3,1},{4,6},{5,7},{6,4},{7,5},{8,10},{9,11},{10,... | collective-permute-start | bytes 196616 | tf_op jit(solution)/shard_map/ppermute | solution.py:278
  55.2 4.0 %collective-permute-start.12 = (bf16[2,1,64,128]{3,2,1,0:T(8,128)(2,1)S(1)}, bf16[2,1,64,128]{3,2,1,0:T(8,128)(2,1)S(1)}, u32[]{:S(2)}, u32[]{:S(2)}) collective-permute-start(bf16[2,1,64,128]{3,2,1,0:T(8,128)(2,1)S(1)} %slice.46), channel_id=1, source_target_pairs={{0,4},{1,5},{2,6},{3,7},{4,0},{5,1},{6,2},{7,3},{8,12},{9,13},{10,... | collective-permute-start | bytes 98312 | tf_op jit(solution)/shard_map/ppermute | solution.py:278
  59.2 4.7 %collective-permute-start.13 = (bf16[1,1,64,128]{3,2,1,0:T(8,128)(2,1)S(1)}, bf16[1,1,64,128]{3,2,1,0:T(8,128)(2,1)S(1)}, u32[]{:S(2)}, u32[]{:S(2)}) collective-permute-start(bf16[1,1,64,128]{3,2,1,0:T(8,128)(2,1)S(1)} %slice.47), channel_id=1, source_target_pairs={{0,8},{1,9},{2,10},{3,11},{4,12},{5,13},{6,14},{7,15},{8,0},{9,1},... | collective-permute-start | bytes 49160 | tf_op jit(solution)/shard_map/ppermute | solution.py:278
